TPU v7x, 128 devices: a whole 4x4x4 slice. The times are simulated.
128 devices in a mesh: shard: 16 (over z, y), ctx: 2 (over x_lo), tp: 4 (over x_hi, core).
Axes of the slice: x: 4 (x_hi: 2, x_lo: 2; x = x_hi * 2 + x_lo), y: 4, z: 4, core: 2. Of those that a mesh axis runs over, the one named last changes fastest.
Arguments:
- tokens: bfloat16 [16, 1024, 1088], P('shard', ('ctx', 'tp')), may hold values from -6 to 6
- cotangent: bfloat16 [16, 1024, 1088], P('shard', ('ctx', 'tp')), may hold values from -6 to 6
- block_order: int32 [4], replicated, may hold values from 0 to 3, each once
- head_count: int32 [4], replicated, may hold values from 3 to 5, as said below
- ln_gain: float32 [2, 2, 1088], replicated, may hold values from 0.1 to 1.9
- ln_bias: float32 [2, 2, 1088], replicated, may hold values from -1.5 to 1.5
- w_qkv: bfloat16 [2, 4, 5, 1088, 192], P(None, 'tp', None, ('shard', 'ctx')), may hold values from -0.1875 to 0.1875
- b_qv: float32 [2, 4, 5, 128], P(None, 'tp'), may hold values from -3 to 3
- w_out: bfloat16 [2, 4, 5, 64, 1088], P(None, 'tp', None, None, ('shard', 'ctx')), may hold values from -0.75 to 0.75
- b_out: float32 [2, 1088], replicated, may hold values from -3 to 3
- w_fc: bfloat16 [2, 1088, 4352], P(None, ('shard', 'ctx'), 'tp'), may hold values from -0.1875 to 0.1875
- b_fc: float32 [2, 4352], P(None, 'tp'), may hold values from -3 to 3
- w_down: bfloat16 [2, 4352, 1088], P(None, 'tp', ('shard', 'ctx')), may hold values from -0.09375 to 0.09375
- b_down: float32 [2, 1088], replicated, may hold values from -3 to 3
Outputs:
- mixed: bfloat16 [16, 1024, 1088], P('shard', ('ctx', 'tp'))
- grad_tokens: float32 [16, 1024, 1088], P('shard', ('ctx', 'tp'))
- grad_ln_gain: float32 [2, 2, 1088], replicated
- grad_ln_bias: float32 [2, 2, 1088], replicated
- grad_w_qkv: float32 [2, 4, 5, 1088, 192], P(None, 'tp', None, ('shard', 'ctx'))
- grad_b_qv: float32 [2, 4, 5, 128], P(None, 'tp')
- grad_w_out: float32 [2, 4, 5, 64, 1088], P(None, 'tp', None, None, ('shard', 'ctx'))
- grad_b_out: float32 [2, 1088], replicated
- grad_w_fc: float32 [2, 1088, 4352], P(None, ('shard', 'ctx'), 'tp')
- grad_b_fc: float32 [2, 4352], P(None, 'tp')
- grad_w_down: float32 [2, 4352, 1088], P(None, 'tp', ('shard', 'ctx'))
- grad_b_down: float32 [2, 1088], replicated
Inputs may be any that keep to these rules, and one draw needn't show every extreme that they name: Each stored block of 256 rows of a sequence holds the positions of block block_order[b]; each block number appears once. `head_count`: the counts sum to 17; at least one rank, drawn from the seed, uses all 5 slots; no rank uses fewer than 3; a rank uses its slots from the first.
All inputs are finite; a program needn't handle non-finite values.
Results may differ from a plain program's by a relative error of at most 0.025.
Values may be sent and summed in bfloat16 or wider, within the bound.
No kernel may reach another device: no remote copies, remote signals or barrier semaphores. Data moves between devices by JAX's collectives and lax.ppermute only.
A program may use at most 192 MiB of HBM per device.

v0:
```python
from functools import partial

import jax
import jax.numpy as jnp
from jax import lax
from jax.sharding import PartitionSpec as P

HD = 64
LEN = 1024
LAYERS = 2


EPS = 1e-05


def copy_for_each(x, axis):
    copies = jnp.broadcast_to(x, (lax.axis_size(axis), *x.shape))
    return lax.all_to_all(copies, axis, split_axis=0, concat_axis=0, tiled=True)


def joined_along(tiles, dim):
    lengths = list(tiles.shape[1:])
    lengths[dim] *= tiles.shape[0]
    return jnp.moveaxis(tiles, 0, dim).reshape(lengths)


def collect(x, axis, dim):
    tiles = copy_for_each(x, axis)
    return joined_along(tiles, dim)


def in_blocks(x, dim, devices):
    lengths = x.shape
    tiles = x.reshape(*lengths[:dim], devices, lengths[dim] // devices, *lengths[dim + 1 :])
    return jnp.moveaxis(tiles, dim, 0)


def sum_at_owner(x, axis, dim):
    tiles = in_blocks(x, dim, lax.axis_size(axis))
    arrived = lax.all_to_all(tiles, axis, split_axis=0, concat_axis=0, tiled=True)
    return arrived.astype(jnp.float32).sum(axis=0)


def sum_packed(arrays, axis, dims):
    devices = lax.axis_size(axis)
    tiles = [in_blocks(a, dim, devices) for a, dim in zip(arrays, dims)]
    lines = jnp.concatenate([b.reshape(devices, -1) for b in tiles], axis=1)
    extent = max(16, -(-lines.shape[1] // 1024) * 8)
    lines = jnp.pad(lines, ((0, 0), (0, extent * 128 - lines.shape[1]))).reshape(-1, 128)
    flat, at, gathered = (lax.psum_scatter(lines, axis, tiled=True).reshape(-1), 0, [])
    for b in tiles:
        part = b[0]
        gathered.append(flat[at : at + part.size].reshape(part.shape))
        at += part.size
    return tuple(gathered)


def layer_norm(values_in, gain, shift):
    average = jnp.mean(values_in, axis=-1, keepdims=True)
    centred = values_in - average
    variance = jnp.mean(centred * centred, axis=-1, keepdims=True)
    return centred * lax.rsqrt(variance + EPS) * gain + shift


def gelu_exact(values_in):
    return jax.nn.gelu(values_in, approximate=False)


def place_rows(block_order):
    parts_count = block_order.shape[0]
    block_rows = LEN // parts_count
    row_index = jnp.arange(LEN, dtype=jnp.int32)
    onehot = row_index[:, None] // block_rows == jnp.arange(parts_count, dtype=jnp.int32)[None, :]
    chosen = jnp.sum(jnp.where(onehot, block_order[None, :], 0), axis=1)
    return chosen * block_rows + row_index % block_rows


def attend_forward(pieces, allowed, score_scale, slot_live):
    queries, keys_all, values_all = pieces
    raw_scores = (
        jnp.einsum("hqe,hke->hqk", queries, keys_all, preferred_element_type=jnp.float32)
        * score_scale
    )
    masked = jnp.where(allowed, raw_scores, -1e30)
    highest = jnp.max(masked, axis=-1, keepdims=True)
    exponent = jnp.exp(masked - highest)
    totals = jnp.sum(exponent, axis=-1, keepdims=True)
    attn_probs = (exponent / totals).astype(jnp.bfloat16)
    mixed_heads = jnp.einsum(
        "hqk,hke->hqe", attn_probs, values_all, preferred_element_type=jnp.float32
    )
    mixed_heads = mixed_heads * slot_live[:, None, None]
    return (mixed_heads.astype(jnp.bfloat16), (highest + jnp.log(totals))[..., 0])


def attend_backward(pieces, allowed, score_scale):
    queries, keys_all, values_all, log_total, grad_heads = pieces
    raw_scores = (
        jnp.einsum("hqe,hke->hqk", queries, keys_all, preferred_element_type=jnp.float32)
        * score_scale
    )
    attn_probs = jnp.exp(jnp.where(allowed, raw_scores, -1e30) - log_total[..., None])
    grad_probs = jnp.einsum(
        "hqe,hke->hqk", grad_heads, values_all, preferred_element_type=jnp.float32
    )
    centred = grad_probs - jnp.sum(grad_probs * attn_probs, axis=-1, keepdims=True)
    grad_scores = (attn_probs * centred).astype(jnp.bfloat16)
    grad_queries = jnp.einsum(
        "hqk,hke->hqe", grad_scores, keys_all, preferred_element_type=jnp.float32
    )
    grad_queries = (grad_queries * score_scale).astype(jnp.bfloat16)
    grad_keys = (
        jnp.einsum("hqk,hqe->hke", grad_scores, queries, preferred_element_type=jnp.float32)
        * score_scale
    )
    grad_values = jnp.einsum(
        "hqk,hqe->hke",
        attn_probs.astype(jnp.bfloat16),
        grad_heads,
        preferred_element_type=jnp.float32,
    )
    return (grad_queries, grad_keys, grad_values)


def gather_rows(values_in):
    return collect(values_in, "tp", 1)


def sum_rows(values_in):
    return sum_at_owner(values_in.astype(jnp.bfloat16), "tp", 1)


def gather_grads(values_in):
    return collect(values_in, "tp", 1)


def sum_inputs(values_in):
    return sum_at_owner(values_in.astype(jnp.bfloat16), "tp", 1)


def shards(
    tokens,
    cotangent,
    block_order,
    head_count,
    ln_gain,
    ln_bias,
    w_qkv,
    b_qv,
    w_out,
    b_out,
    w_fc,
    b_fc,
    w_down,
    b_down,
):
    tp_index = lax.axis_index("tp")
    ctx_index = lax.axis_index("ctx")
    slots = w_qkv.shape[2]
    my_count = jnp.sum(
        jnp.where(jnp.arange(head_count.shape[0], dtype=jnp.int32) == tp_index, head_count, 0)
    )
    slot_live = (jnp.arange(slots, dtype=jnp.int32) < my_count).astype(jnp.float32)
    places = place_rows(block_order)
    local_rows = LEN // lax.axis_size("ctx")
    query_places = lax.dynamic_slice_in_dim(places, ctx_index * local_rows, local_rows)
    allowed = places[None, :] <= query_places[:, None]
    score_scale = HD ** (-0.5)
    forward_step = partial(
        attend_forward, allowed=allowed, score_scale=score_scale, slot_live=slot_live
    )
    backward_step = partial(attend_backward, allowed=allowed, score_scale=score_scale)
    hidden = tokens.astype(jnp.float32)
    stored = []
    for layer_idx in range(LAYERS):
        fetched = (
            lax.all_gather(w_qkv[layer_idx, 0], ("shard", "ctx"), axis=1, tiled=True),
            lax.all_gather(w_out[layer_idx, 0], ("shard", "ctx"), axis=2, tiled=True),
            lax.all_gather(w_fc[layer_idx], ("shard", "ctx"), axis=0, tiled=True),
            lax.all_gather(w_down[layer_idx], ("shard", "ctx"), axis=1, tiled=True),
        )
        weight_qkv, weight_out, weight_fc, weight_down = fetched
        normed = layer_norm(hidden, ln_gain[layer_idx, 0], ln_bias[layer_idx, 0]).astype(
            jnp.bfloat16
        )
        normed_all = gather_rows(normed)
        projected = jnp.einsum(
            "srd,hde->shre", normed_all, weight_qkv, preferred_element_type=jnp.float32
        )
        head_bias = b_qv[layer_idx, 0]
        queries = (projected[..., :HD] + head_bias[None, :, None, :HD]).astype(jnp.bfloat16)
        keys_local = projected[..., HD : 2 * HD].astype(jnp.bfloat16)
        values_local = (projected[..., 2 * HD :] + head_bias[None, :, None, HD:]).astype(
            jnp.bfloat16
        )
        keys_all, values_all = (
            lax.all_gather(keys_local, "ctx", axis=2, tiled=True),
            lax.all_gather(values_local, "ctx", axis=2, tiled=True),
        )
        attended, log_total = lax.map(forward_step, (queries, keys_all, values_all))
        mixed_out = jnp.einsum(
            "shre,hed->srd", attended, weight_out, preferred_element_type=jnp.float32
        )
        middle = hidden + (sum_rows(mixed_out) + b_out[layer_idx])
        normed_two = layer_norm(middle, ln_gain[layer_idx, 1], ln_bias[layer_idx, 1]).astype(
            jnp.bfloat16
        )
        normed_two_all = gather_rows(normed_two)
        inner_pre = (
            jnp.einsum("srd,df->srf", normed_two_all, weight_fc, preferred_element_type=jnp.float32)
            + b_fc[layer_idx]
        )
        activated = gelu_exact(inner_pre).astype(jnp.bfloat16)
        down_out = jnp.einsum(
            "srf,fd->srd", activated, weight_down, preferred_element_type=jnp.float32
        )
        stored.append(
            (
                hidden,
                normed_all,
                queries,
                keys_all,
                values_all,
                log_total,
                attended,
                middle,
                normed_two_all,
                inner_pre,
                activated,
                fetched,
            )
        )
        hidden = middle + (sum_rows(down_out) + b_down[layer_idx])
    mixed = hidden.astype(jnp.bfloat16)
    gradient = cotangent.astype(jnp.float32)
    results = [None] * LAYERS
    for layer_idx in reversed(range(LAYERS)):
        (
            hidden,
            normed_all,
            queries,
            keys_all,
            values_all,
            log_total,
            attended,
            middle,
            normed_two_all,
            inner_pre,
            activated,
            fetched,
        ) = stored[layer_idx]
        weight_qkv, weight_out, weight_fc, weight_down = fetched
        grad_branch = gradient.astype(jnp.bfloat16)
        grad_branch_all = gather_grads(grad_branch)
        grad_down_w = jnp.einsum(
            "srf,srd->fd", activated, grad_branch_all, preferred_element_type=jnp.float32
        )
        grad_down_b = jnp.sum(grad_branch.astype(jnp.float32), axis=(0, 1))
        grad_activated = jnp.einsum(
            "srd,fd->srf", grad_branch_all, weight_down, preferred_element_type=jnp.float32
        )
        gelu_pull = jax.vjp(gelu_exact, inner_pre)[1]
        grad_inner = gelu_pull(grad_activated)[0].astype(jnp.bfloat16)
        grad_fc_w = jnp.einsum(
            "srd,srf->df", normed_two_all, grad_inner, preferred_element_type=jnp.float32
        )
        grad_fc_b = jnp.sum(grad_inner.astype(jnp.float32), axis=(0, 1))
        grad_normed_two = sum_inputs(
            jnp.einsum("srf,df->srd", grad_inner, weight_fc, preferred_element_type=jnp.float32)
        )
        norm_pull_two = jax.vjp(layer_norm, middle, ln_gain[layer_idx, 1], ln_bias[layer_idx, 1])[1]
        grad_middle, gain_two, shift_two = norm_pull_two(grad_normed_two)
        grad_middle = gradient + grad_middle
        grad_mix = grad_middle.astype(jnp.bfloat16)
        grad_mix_all = gather_grads(grad_mix)
        grad_out_b = jnp.sum(grad_mix.astype(jnp.float32), axis=(0, 1))
        grad_out_w = jnp.einsum(
            "shre,srd->hed", attended, grad_mix_all, preferred_element_type=jnp.float32
        )
        grad_heads = jnp.einsum(
            "srd,hed->shre", grad_mix_all, weight_out, preferred_element_type=jnp.float32
        )
        grad_heads = grad_heads.astype(jnp.bfloat16) * slot_live[None, :, None, None].astype(
            jnp.bfloat16
        )
        grad_queries, keys_part, values_part = lax.map(
            backward_step, (queries, keys_all, values_all, log_total, grad_heads)
        )
        grad_keys, grad_values = (
            lax.psum_scatter(
                keys_part.astype(jnp.bfloat16), "ctx", scatter_dimension=2, tiled=True
            ).astype(jnp.float32),
            lax.psum_scatter(
                values_part.astype(jnp.bfloat16), "ctx", scatter_dimension=2, tiled=True
            ).astype(jnp.float32),
        )
        grad_keys_low = grad_keys.astype(jnp.bfloat16)
        grad_values_low = grad_values.astype(jnp.bfloat16)
        grad_projected = jnp.concatenate([grad_queries, grad_keys_low, grad_values_low], axis=-1)
        grad_qkv_w = jnp.einsum(
            "srd,shre->hde", normed_all, grad_projected, preferred_element_type=jnp.float32
        )
        grad_head_b = jnp.concatenate(
            [
                jnp.sum(grad_queries.astype(jnp.float32), axis=(0, 2)),
                jnp.sum(grad_values_low.astype(jnp.float32), axis=(0, 2)),
            ],
            axis=-1,
        )
        grad_normed = sum_inputs(
            jnp.einsum(
                "shre,hde->srd", grad_projected, weight_qkv, preferred_element_type=jnp.float32
            )
        )
        norm_pull_one = jax.vjp(layer_norm, hidden, ln_gain[layer_idx, 0], ln_bias[layer_idx, 0])[1]
        grad_hidden, gain_one, shift_one = norm_pull_one(grad_normed)
        gradient = grad_middle + grad_hidden
        halfway = tuple(
            (
                part.astype(jnp.float32)
                for part in sum_packed(
                    (
                        grad_qkv_w.astype(jnp.bfloat16),
                        grad_out_w.astype(jnp.bfloat16),
                        grad_fc_w.astype(jnp.bfloat16),
                        grad_down_w.astype(jnp.bfloat16),
                    ),
                    "shard",
                    (1, 2, 0, 1),
                )
            )
        )
        shares = (
            lax.psum_scatter(
                halfway[0].astype(jnp.bfloat16), "ctx", scatter_dimension=1, tiled=True
            ).astype(jnp.float32),
            lax.psum_scatter(
                halfway[1].astype(jnp.bfloat16), "ctx", scatter_dimension=2, tiled=True
            ).astype(jnp.float32),
            lax.psum_scatter(
                halfway[2].astype(jnp.bfloat16), "ctx", scatter_dimension=0, tiled=True
            ).astype(jnp.float32),
            lax.psum_scatter(
                halfway[3].astype(jnp.bfloat16), "ctx", scatter_dimension=1, tiled=True
            ).astype(jnp.float32),
        )
        head_sum, fc_sum = lax.psum((grad_head_b, grad_fc_b), ("shard", "ctx"))
        gain_sum, shift_sum, out_sum, down_sum = lax.psum(
            (
                jnp.stack([gain_one, gain_two]),
                jnp.stack([shift_one, shift_two]),
                grad_out_b,
                grad_down_b,
            ),
            ("shard", "ctx", "tp"),
        )
        results[layer_idx] = (
            gain_sum,
            shift_sum,
            shares[0],
            head_sum,
            shares[1],
            out_sum,
            shares[2],
            fc_sum,
            shares[3],
            down_sum,
        )

    def stacked(position):
        return jnp.stack([entry[position] for entry in results])

    return (
        mixed,
        gradient,
        stacked(0),
        stacked(1),
        stacked(2)[:, None],
        stacked(3)[:, None],
        stacked(4)[:, None],
        stacked(5),
        stacked(6),
        stacked(7),
        stacked(8),
        stacked(9),
    )


def solution(mesh):
    in_specs = (
        P("shard", ("ctx", "tp"), None),
        P("shard", ("ctx", "tp"), None),
        P(),
        P(),
        P(),
        P(),
        P(None, "tp", None, ("shard", "ctx"), None),
        P(None, "tp", None, None),
        P(None, "tp", None, None, ("shard", "ctx")),
        P(),
        P(None, ("shard", "ctx"), "tp"),
        P(None, "tp"),
        P(None, "tp", ("shard", "ctx")),
        P(),
    )
    out_specs = (
        P("shard", ("ctx", "tp"), None),
        P("shard", ("ctx", "tp"), None),
        P(),
        P(),
        P(None, "tp", None, ("shard", "ctx"), None),
        P(None, "tp", None, None),
        P(None, "tp", None, None, ("shard", "ctx")),
        P(),
        P(None, ("shard", "ctx"), "tp"),
        P(None, "tp"),
        P(None, "tp", ("shard", "ctx")),
        P(),
    )
    return jax.shard_map(shards, mesh=mesh, in_specs=in_specs, out_specs=out_specs, check_vma=False)
```

profile of v0, /device:TPU:0, one launch (start us, length us, event | category | flops | bytes accessed | tf_op | source)
XLA Modules:
  0.0 1892.7 jit_solution(14040538360349883036)
XLA Ops:
  22.0 151.7 %all-gather.1 = bf16[1,1,5,64,1088]{3,2,1,0,4:T(8,128)(2,1)S(1)} all-gather(bf16[1,1,5,64,34]{3,2,1,0,4:T(8,128)(2,1)S(1)} %copy.241), channel_id=3, replica_groups=mesh['shard'=16,'ctx'=2,'tp'=4] {'shard','ctx'}, dimensions={4}, use_global_device_ids=true | all-gather | bytes 718080 | tf_op jit(solution)/shard_map/all_gather | solution.py:178
  182.4 14.7 all-gather.15.cloned.1.call-done
  206.6 13.3 all_gather.38
  219.9 13.4 all_gather.37
  250.9 27.9 %all-to-all-done.1 = bf16[4,1,128,1088]{2,3,1,0:T(8,128)(2,1)S(1)} async-done(((bf16[4,1,128,1088]{2,3,1,0:T(8,128)(2,1)}), bf16[4,1,128,1088]{2,3,1,0:T(8,128)(2,1)S(1)}, u32[]{:S(2)}, u32[]{:S(2)}) %all-to-all-start.1) | async-done | bytes 1114144 | tf_op jit(solution)/shard_map/all_to_all | solution.py:40
  286.2 97.5 %all-gather.19.cloned.1.call-done = bf16[1,1088,1088]{1,0,2:T(2,128)(2,1)} async-done(((bf16[1,1088,34]{1,0,2:T(2,128)(2,1)}), bf16[1,1088,1088]{1,0,2:T(2,128)(2,1)}) %all-gather.19.cloned.1.call-update) | async-done | bytes 2367504 | tf_op jit(solution)/shard_map/all_gather | solution.py:180
  396.6 155.8 %all-gather.17.cloned.1.call-done = bf16[1,1088,1088]{2,0,1:T(2,128)(2,1)} async-done(((bf16[1,34,1088]{2,0,1:T(2,128)(2,1)}), bf16[1,1088,1088]{2,0,1:T(2,128)(2,1)}) %all-gather.17.cloned.1.call-update) | async-done | bytes 2367504 | tf_op jit(solution)/shard_map/all_gather | solution.py:179
  571.5 27.8 %all-to-all-done.3 = bf16[4,1,128,1088]{2,3,1,0:T(8,128)(2,1)S(1)} async-done(((bf16[4,1,128,1088]{2,3,1,0:T(8,128)(2,1)}), bf16[4,1,128,1088]{2,3,1,0:T(8,128)(2,1)S(1)}, u32[]{:S(2)}, u32[]{:S(2)}) %all-to-all-start.3) | async-done | bytes 1114144 | tf_op jit(solution)/shard_map/all_to_all | solution.py:40
  606.3 143.1 %all-gather.5 = bf16[1,1,5,64,1088]{3,2,1,0,4:T(8,128)(2,1)S(1)} all-gather(bf16[1,1,5,64,34]{3,2,1,0,4:T(8,128)(2,1)S(1)} %copy.243), channel_id=7, replica_groups=mesh['shard'=16,'ctx'=2,'tp'=4] {'shard','ctx'}, dimensions={4}, use_global_device_ids=true | all-gather | bytes 718080 | tf_op jit(solution)/shard_map/all_gather | solution.py:178
  764.3 17.1 all_gather.44
  781.4 16.2 all_gather.43
  808.4 31.6 %all_to_all.80 = bf16[4,1,128,1088]{2,3,1,0:T(8,128)(2,1)} all-to-all(bf16[4,1,128,1088]{2,3,1,0:T(8,128)(2,1)S(1)} %copy.193), channel_id=1, replica_groups=mesh['shard'=16,'ctx'=2,'tp'=4] {'tp'}, dimensions={0} | all-to-all | bytes 2228224 | tf_op jit(solution)/shard_map/all_to_all | solution.py:40
  847.2 26.3 %all-to-all-done.8 = bf16[4,1,128,1088]{2,3,1,0:T(8,128)(2,1)S(1)} async-done(((bf16[4,1,128,1088]{2,3,1,0:T(8,128)(2,1)}), bf16[4,1,128,1088]{2,3,1,0:T(8,128)(2,1)S(1)}, u32[]{:S(2)}, u32[]{:S(2)}) %all-to-all-start.8) | async-done | bytes 1114144 | tf_op jit(solution)/shard_map/all_to_all | solution.py:18
  880.3 51.9 %all-gather.25.cloned.1.call-done = bf16[1,1088,1088]{1,0,2:T(2,128)(2,1)} async-done(((bf16[1,1088,34]{1,0,2:T(2,128)(2,1)}), bf16[1,1088,1088]{1,0,2:T(2,128)(2,1)}) %all-gather.25.cloned.1.call-update) | async-done | bytes 2367504 | tf_op jit(solution)/shard_map/all_gather | solution.py:180
  946.8 156.2 %all-gather.23.cloned.1.call-done = bf16[1,1088,1088]{2,0,1:T(2,128)(2,1)} async-done(((bf16[1,34,1088]{2,0,1:T(2,128)(2,1)}), bf16[1,1088,1088]{2,0,1:T(2,128)(2,1)}) %all-gather.23.cloned.1.call-update) | async-done | bytes 2367504 | tf_op jit(solution)/shard_map/all_gather | solution.py:179
  1152.2 14.2 all-to-all-done.7
  1174.6 15.9 all-to-all-done.10
  1233.2 21.4 %reduce-scatter.15.cloned.1.call-done = bf16[1,5,512,64]{2,3,1,0:T(8,128)(2,1)} async-done(((bf16[1,5,1024,64]{2,3,1,0:T(8,128)(2,1)}), bf16[1,5,512,64]{2,3,1,0:T(8,128)(2,1)}) %reduce-scatter.15.cloned.1.call-update) | async-done | bytes 327696 | tf_op jit(solution)/shard_map/reduce_scatter | solution.py:290
  1261.3 20.4 %all_to_all.81 = bf16[4,1,128,1088]{2,3,1,0:T(8,128)(2,1)S(1)} all-to-all(bf16[4,1,128,1088]{2,3,1,0:T(8,128)(2,1)S(1)} %copy.200), channel_id=1, replica_groups=mesh['shard'=16,'ctx'=2,'tp'=4] {'tp'}, dimensions={0} | all-to-all | bytes 2228224 | tf_op jit(solution)/shard_map/all_to_all | solution.py:40
  1401.3 24.0 %fusion.19 = bf16[16,235520]{1,0:T(8,128)(2,1)} fusion(bf16[16,73984]{1,0:T(8,128)(2,1)} %reshape.1277, bf16[16,73984]{1,0:T(8,128)(2,1)S(1)} %reshape_reshape.7, bf16[16,21760]{1,0:T(8,128)(2,1)} %reshape.1275, bf16[16,65280]{1,0:T(8,128)(2,1)} %reshape.1273), kind=kLoop, calls=%fused_computation.34 | loop fusion | flops 48988160 | bytes 15056896 | tf_op jit(solution)/shard_map/concatenate | solution.py:47
  1528.7 13.6 fusion.16
  1563.3 164.9 %all-reduce.13 = (f32[1,5,128]{2,0,1:T(1,128)S(1)}, f32[1,5,128]{2,0,1:T(1,128)S(1)}, f32[1,1088]{1,0:T(1,128)S(1)}, f32[1,1088]{1,0:T(1,128)S(1)}) all-reduce(f32[1,5,128]{2,0,1:T(1,128)S(1)} %stack.164, f32[1,5,128]{2,0,1:T(1,128)S(1)} %stack.163, ...), channel_id=1, replica_groups=mesh['shard'=16,'ctx'=2,'tp'=4] {'shard','ctx'}, use_global_device_ids=true, to_apply=%region_57.58 | all-reduce | flops 3456 | bytes 27648 | tf_op jit(solution)/shard_map/psum | solution.py:347
  1730.4 65.5 %all-reduce.12 = (f32[1,2,1088]{2,1,0:T(2,128)S(1)}, f32[1,2,1088]{2,1,0:T(2,128)S(1)}, f32[1,2,1088]{2,1,0:T(2,128)S(1)}, f32[1,2,1088]{2,1,0:T(2,128)S(1)}, f3...) all-reduce(f32[1,2,1088]{2,1,0:T(2,128)S(1)} %maximum_bitcast_fusio, ...), channel_id=1, replica_groups=mesh['shard'=16,'ctx'=2,'tp'=4] {'shard','ctx','tp'}, use_global_device_ids=true, to_apply=%region_41.42 | all-reduce | flops 13056 | bytes 104448 | tf_op jit(solution)/shard_map/psum | solution.py:348
  1833.0 47.3 %all-reduce.22.cloned.1.call-done = (bf16[5,68,192]{2,1,0:T(8,128)(2,1)}, bf16[5,68,192]{2,1,0:T(8,128)(2,1)}, bf16[1088,68]{1,0:T(8,128)(2,1)}, bf16[1088,68]{1,0:T(8,128)(2,1)}) async-done(((bf16[5,68,192]{2,1,0:T(8,128)(2,1)}, bf16[5,68,192]{2,1,0:T(8,128)(2,1)}, bf16[1088,68]{1,0:T(8,128)(2,1)}, bf16[1088,68]{1,0:T(8,128)(2,1)}), (bf16[5,68,192]{2,1,0:T(8,128)(2,1)}, bf16[5,68,192]{2,1,0:T(8,128)(2,1)}, ...) | async-done | bytes 557072
  (543 shorter events, 543.2 us)
Async XLA Ops:
  7.2 189.9 %all-gather.15.cloned.1.call-start = ((), (), s32[]{:S(2)}) async-start(), calls=%async_computation.28 | async-start | bytes 4595712 | tf_op jit(solution)/shard_map/all_gather | solution.py:177
  9.3 374.4 %all-gather.19.cloned.1.call-start = ((), (), s32[]{:S(2)}) async-start(), calls=%async_computation.30 | async-start | bytes 5170176 | tf_op jit(solution)/shard_map/all_gather | solution.py:180
  11.4 541.0 %all-gather.17.cloned.1.call-start = ((), (), s32[]{:S(2)}) async-start(), calls=%async_computation.29 | async-start | bytes 5170176 | tf_op jit(solution)/shard_map/all_gather | solution.py:179
  16.5 160.6 %all-to-all-start = ((bf16[4,1,128,1088]{2,3,1,0:T(8,128)(2,1)}), bf16[4,1,128,1088]{2,3,1,0:T(8,128)(2,1)}, u32[]{:S(2)}, u32[]{:S(2)}) async-start(bf16[4,1,128,1088]{2,3,1,0:T(8,128)(2,1)} %broadcast_in_dim.186), calls=%async_computation | async-start | bytes 2228224 | tf_op jit(solution)/shard_map/all_to_all | solution.py:18
  21.0 730.9 %all-gather.21.cloned.1.call-start = ((), (), s32[]{:S(2)}) async-start(), calls=%async_computation.31 | async-start | bytes 4595712 | tf_op jit(solution)/shard_map/all_gather | solution.py:177
  245.2 33.6 %all-to-all-start.1 = ((bf16[4,1,128,1088]{2,3,1,0:T(8,128)(2,1)}), bf16[4,1,128,1088]{2,3,1,0:T(8,128)(2,1)S(1)}, u32[]{:S(2)}, u32[]{:S(2)}) async-start(bf16[4,1,128,1088]{2,3,1,0:T(8,128)(2,1)} %copy.184), calls=%async_computation.1 | async-start | bytes 2228224 | tf_op jit(solution)/shard_map/all_to_all | solution.py:40
  281.5 114.4 %all-to-all-start.2 = ((bf16[4,1,128,1088]{2,3,1,0:T(8,128)(2,1)}), bf16[4,1,128,1088]{2,3,1,0:T(8,128)(2,1)S(1)}, u32[]{:S(2)}, u32[]{:S(2)}) async-start(bf16[4,1,128,1088]{2,3,1,0:T(8,128)(2,1)} %broadcast_in_dim.189), calls=%async_computation.2 | async-start | bytes 2228224 | tf_op jit(solution)/shard_map/all_to_all | solution.py:18
  285.0 647.2 %all-gather.25.cloned.1.call-start = ((), (), s32[]{:S(2)}) async-start(), calls=%async_computation.33 | async-start | bytes 5170176 | tf_op jit(solution)/shard_map/all_gather | solution.py:180
  567.4 31.9 %all-to-all-start.3 = ((bf16[4,1,128,1088]{2,3,1,0:T(8,128)(2,1)}), bf16[4,1,128,1088]{2,3,1,0:T(8,128)(2,1)S(1)}, u32[]{:S(2)}, u32[]{:S(2)}) async-start(bf16[4,1,128,1088]{2,3,1,0:T(8,128)(2,1)} %copy.187), calls=%async_computation.3 | async-start | bytes 2228224 | tf_op jit(solution)/shard_map/all_to_all | solution.py:40
  601.4 155.7 %all-to-all-start.4 = ((bf16[4,1,128,1088]{2,3,1,0:T(8,128)(2,1)}), bf16[4,1,128,1088]{2,3,1,0:T(8,128)(2,1)}, u32[]{:S(2)}, u32[]{:S(2)}) async-start(bf16[4,1,128,1088]{2,3,1,0:T(8,128)(2,1)} %broadcast_in_dim.190), calls=%async_computation.4 | async-start | bytes 2228224 | tf_op jit(solution)/shard_map/all_to_all | solution.py:18
  605.7 497.2 %all-gather.23.cloned.1.call-start = ((), (), s32[]{:S(2)}) async-start(), calls=%async_computation.32 | async-start | bytes 5170176 | tf_op jit(solution)/shard_map/all_gather | solution.py:179
  841.1 32.4 %all-to-all-start.8 = ((bf16[4,1,128,1088]{2,3,1,0:T(8,128)(2,1)}), bf16[4,1,128,1088]{2,3,1,0:T(8,128)(2,1)S(1)}, u32[]{:S(2)}, u32[]{:S(2)}) async-start(bf16[4,1,128,1088]{2,3,1,0:T(8,128)(2,1)} %broadcast_in_dim.192), calls=%async_computation.8 | async-start | bytes 2228224 | tf_op jit(solution)/shard_map/all_to_all | solution.py:18
  874.6 69.8 %all-to-all-start.6 = ((bf16[4,1,128,1088]{2,3,1,0:T(8,128)(2,1)}), bf16[4,1,128,1088]{2,3,1,0:T(8,128)(2,1)}, u32[]{:S(2)}, u32[]{:S(2)}) async-start(bf16[4,1,128,1088]{2,3,1,0:T(8,128)(2,1)} %broadcast_in_dim.191), calls=%async_computation.6 | async-start | bytes 2228224 | tf_op jit(solution)/shard_map/all_to_all | solution.py:18
  1173.9 59.3 %reduce-scatter.17.cloned.1.call-start = ((), (), s32[]{:S(2)}) async-start(), calls=%async_computation.23 | async-start | bytes 983040 | tf_op jit(solution)/shard_map/reduce_scatter | solution.py:293
  1215.5 39.0 %reduce-scatter.15.cloned.1.call-start = ((), (), s32[]{:S(2)}) async-start(), calls=%async_computation.22 | async-start | bytes 983040 | tf_op jit(solution)/shard_map/reduce_scatter | solution.py:290
  1322.9 69.4 %all-to-all-start.13 = ((bf16[4,1,128,1088]{2,3,1,0:T(8,128)(2,1)}), bf16[4,1,128,1088]{2,3,1,0:T(8,128)(2,1)}, u32[]{:S(2)}, u32[]{:S(2)}) async-start(bf16[4,1,128,1088]{2,3,1,0:T(8,128)(2,1)} %copy.202), calls=%async_computation.15 | async-start | bytes 2228224 | tf_op jit(solution)/shard_map/all_to_all | solution.py:40
  1396.5 36.2 %all-to-all-start.14 = ((bf16[4,1,128,1088]{2,3,1,0:T(8,128)(2,1)}), bf16[4,1,128,1088]{2,3,1,0:T(8,128)(2,1)S(1)}, u32[]{:S(2)}, u32[]{:S(2)}) async-start(bf16[4,1,128,1088]{2,3,1,0:T(8,128)(2,1)} %broadcast_in_dim.202), calls=%async_computation.16 | async-start | bytes 2228224 | tf_op jit(solution)/shard_map/all_to_all | solution.py:18
  1401.3 110.6 %reduce-scatter.21.cloned.1.call-start = ((), (), s32[]{:S(2)}) async-start(), calls=%async_computation.25 | async-start | bytes 983040 | tf_op jit(solution)/shard_map/reduce_scatter | solution.py:293
  1453.7 58.1 %reduce-scatter.19.cloned.1.call-start = ((), (), s32[]{:S(2)}) async-start(), calls=%async_computation.24 | async-start | bytes 983040 | tf_op jit(solution)/shard_map/reduce_scatter | solution.py:290
  1466.7 332.7 %all-reduce.20.cloned.1.call-start = ((), (), s32[]{:S(2)}) async-start(), calls=%async_computation.34 | async-start | bytes 30146560
  1557.9 171.5 %all-to-all-start.15 = ((bf16[4,1,128,1088]{2,3,1,0:T(8,128)(2,1)}), bf16[4,1,128,1088]{2,3,1,0:T(8,128)(2,1)S(1)}, u32[]{:S(2)}, u32[]{:S(2)}) async-start(bf16[4,1,128,1088]{2,3,1,0:T(8,128)(2,1)} %copy.204), calls=%async_computation.19 | async-start | bytes 2228224 | tf_op jit(solution)/shard_map/all_to_all | solution.py:40
  1562.8 265.1 %reduce-scatter.23.cloned.1.call-start = ((), (), s32[]{:S(2)}) async-start(), calls=%async_computation.26 | async-start | bytes 208896 | tf_op jit(solution)/shard_map/reduce_scatter | solution.py:337
  1804.6 26.5 %reduce-scatter.25.cloned.1.call-start = ((), (), s32[]{:S(2)}) async-start(), calls=%async_computation.27 | async-start | bytes 208896 | tf_op jit(solution)/shard_map/reduce_scatter | solution.py:337
  1819.1 61.2 %all-reduce.22.cloned.1.call-start = ((), (), s32[]{:S(2)}) async-start(), calls=%async_computation.35 | async-start | bytes 1851392
  (119 other events, 3303.8 us)
Sparse Core Ops, SparseCore 0:
  10.3 186.8 all-gather.14
  199.4 184.2 all-gather.18
  385.9 166.4 all-gather.16
  553.9 186.2 all-gather.20
  742.2 189.9 all-gather.24
  934.3 168.6 all-gather.22
  1215.6 16.9 reduce-scatter.16
  1235.0 19.4 reduce-scatter.14
  1453.9 20.3 reduce-scatter.20
  1476.5 19.4 reduce-scatter.18
  1550.0 207.4 all-reduce.19
  1804.7 10.6 reduce-scatter.22
  1819.2 11.9 reduce-scatter.24
  1834.8 45.4 all-reduce.21
where the time goes:
time: 1900 us; the launch traced here: 1890 us
  waiting for transfers between devices  673 us (35%)
  blocking collectives  647 us (34%)
  local copies, waits for them, and re-layouts  268 us (14%)
  matrix products  138 us (7%)
  other arithmetic  84.1 us (4%)
  starting transfers between devices  65 us (3%)
    all_gather x2, waiting for transfers between devices, shards(): lax.all_gather(w_fc[layer_idx], ('shard', 'ctx'), axis=0, tiled=True)  312 us
    all_gather x2, blocking collectives, shards(): lax.all_gather(w_out[layer_idx, 0], ('shard', 'ctx'), axis=2, tiled=True)  295 us
    psum x1, blocking collectives, shards(): head_sum, fc_sum = lax.psum((grad_head_b, grad_fc_b), ('shard', 'ctx'))  165 us
    all_gather x2, waiting for transfers between devices, shards(): lax.all_gather(w_down[layer_idx], ('shard', 'ctx'), axis=1, tiled=True)  149 us
    all_to_all x6, waiting for transfers between devices, sum_at_owner(): lax.all_to_all(tiles, axis, split_axis=0, concat_axis=0, tiled=True)  76.3 us
    psum x1, blocking collectives, shards(): lax.psum((jnp.stack([gain_one, gain_two]), jnp.stack([shift_one, shift_tw...  65.5 us
    all_to_all x2, blocking collectives, sum_at_owner(): lax.all_to_all(tiles, axis, split_axis=0, concat_axis=0, tiled=True)  52 us
    unnamed x18, waiting for transfers between devices  48.2 us
  transfers between devices with their start and end apart: 30, of which 15 were waited for; matrix products, arithmetic and copies ran while one was open for 18% of the time, Pallas kernels for 0%

commit v1 on v0

v1 whole, which is shorter than its diff:
```python
import jax
import jax.numpy as jnp
from jax import lax
from jax.sharding import PartitionSpec as P

D = 1088
HD = 64
LAYERS = 2
EPS = 1e-05
SHARDS = 16
CHUNK = 34
WIDE = 36
DP = 2 * SHARDS * WIDE
HEADS_HERE = 3
QW = HEADS_HERE * HD
FH = 544
FP = 640
ROWS = 128
BF = jnp.bfloat16
F32 = jnp.float32
LINE = ("ctx", "tp")


def line_perm(target):
    pairs = []
    for c in range(2):
        for h in range(2):
            for k in range(2):
                x2, k2 = target(2 * h + c, k)
                pairs.append((c * 4 + h * 2 + k, (x2 % 2) * 4 + (x2 // 2) * 2 + k2))
    return pairs


def swap_core(v):
    return lax.ppermute(v, LINE, line_perm(lambda x, k: (x, 1 - k)))


def swap_x(v, m):
    return lax.ppermute(v, LINE, line_perm(lambda x, k: (x ^ m, k)))


def swap_ctx(v):
    return lax.ppermute(v, "ctx", [(0, 1), (1, 0)])


def swap_shard(v, m):
    return lax.ppermute(v, "shard", [(i, i ^ m) for i in range(SHARDS)])


def gather_rows(piece):
    mine = jnp.concatenate([piece] + [swap_x(piece, m) for m in (1, 2, 3)], axis=0)
    return jnp.concatenate([mine, swap_core(mine)], axis=0)


def sum_rows(partial):
    half = 4 * ROWS
    arrived = swap_core(partial[half:].astype(BF))
    chip = partial[:half] + arrived.astype(F32)
    low = chip.astype(BF)
    parts = [swap_x(low[m * ROWS : (m + 1) * ROWS], m).astype(F32) for m in (1, 2, 3)]
    return (chip[:ROWS] + parts[0]) + (parts[1] + parts[2])


def sum_shards(v):
    v = (v + swap_shard(v, 1)) + (swap_shard(v, 2) + swap_shard(v, 3))
    return (v + swap_shard(v, 4)) + (swap_shard(v, 8) + swap_shard(v, 12))


def sum_line(v):
    v = v + swap_core(v)
    return (v + swap_x(v, 1)) + (swap_x(v, 2) + swap_x(v, 3))


def dot(a, b, dims):
    return lax.dot_general(a, b, (dims, ((), ())), preferred_element_type=F32)


def norm_forward(x, gain, shift, mask):
    mean = jnp.sum(x, axis=-1, keepdims=True) * (1.0 / D)
    centred = (x - mean) * mask
    var = jnp.sum(centred * centred, axis=-1, keepdims=True) * (1.0 / D)
    rstd = lax.rsqrt(var + EPS)
    xhat = centred * rstd
    return (xhat * gain + shift).astype(BF), xhat, rstd


def norm_backward(dy, xhat, rstd, gain, mask):
    e = dy * gain
    mean_e = jnp.sum(e, axis=-1, keepdims=True) * (1.0 / D)
    mean_ex = jnp.sum(e * xhat, axis=-1, keepdims=True) * (1.0 / D)
    dx = rstd * (e - mean_e - xhat * mean_ex) * mask
    return dx, jnp.sum(dy * xhat, axis=0), jnp.sum(dy, axis=0)


def gelu_exact(v):
    return jax.nn.gelu(v, approximate=False)


def split_heads(v):
    return jnp.moveaxis(v.reshape(v.shape[0], HEADS_HERE, HD), 1, 0)


def join_heads(v):
    return jnp.moveaxis(v, 0, 1).reshape(v.shape[1], HEADS_HERE * HD)


def attend_forward(queries, keys, values, allowed, live):
    scores = jnp.einsum("hqe,hke->hqk", queries, keys, preferred_element_type=F32) * HD**-0.5
    masked = jnp.where(allowed, scores, -1e30)
    highest = jnp.max(masked, axis=-1, keepdims=True)
    exponent = jnp.exp(masked - highest)
    totals = jnp.sum(exponent, axis=-1, keepdims=True)
    probs = (exponent / totals).astype(BF)
    heads = jnp.einsum("hqk,hke->hqe", probs, values, preferred_element_type=F32)
    return (heads * live[:, None, None]).astype(BF), highest + jnp.log(totals)


def attend_backward(queries, keys, values, log_total, grad_heads, allowed):
    scores = jnp.einsum("hqe,hke->hqk", queries, keys, preferred_element_type=F32) * HD**-0.5
    probs = jnp.exp(jnp.where(allowed, scores, -1e30) - log_total)
    grad_probs = jnp.einsum("hqe,hke->hqk", grad_heads, values, preferred_element_type=F32)
    centred = grad_probs - jnp.sum(grad_probs * probs, axis=-1, keepdims=True)
    grad_scores = (probs * centred).astype(BF)
    grad_q = jnp.einsum("hqk,hke->hqe", grad_scores, keys, preferred_element_type=F32)
    grad_k = jnp.einsum("hqk,hqe->hke", grad_scores, queries, preferred_element_type=F32)
    grad_v = jnp.einsum("hqk,hqe->hke", probs.astype(BF), grad_heads, preferred_element_type=F32)
    return (
        (grad_q * HD**-0.5).astype(BF),
        (grad_k * HD**-0.5).astype(BF),
        grad_v.astype(BF),
    )


def heads_first(w_qkv, w_out, h):
    first, count = (0, 3) if h == 0 else (3, 2)
    picked = jnp.moveaxis(w_qkv[first : first + count], 0, 1)
    outs = jnp.moveaxis(w_out[first : first + count], 2, 0)
    cols = [picked[:, :, i * HD : (i + 1) * HD] for i in range(3)] + [outs]
    cols = [jnp.pad(a, ((0, 0), (0, HEADS_HERE - count), (0, 0))) for a in cols]
    return jnp.concatenate([a.reshape(CHUNK, QW) for a in cols], axis=1)


def hidden_first(w_fc, w_down, h):
    gap = ((0, 0), (0, FP - FH))
    return jnp.concatenate(
        [
            jnp.pad(w_fc[:, h * FH : (h + 1) * FH], gap),
            jnp.pad(w_down[h * FH : (h + 1) * FH].T, gap),
        ],
        axis=1,
    )


def shards(
    tokens,
    cotangent,
    block_order,
    head_count,
    ln_gain,
    ln_bias,
    w_qkv,
    b_qv,
    w_out,
    b_out,
    w_fc,
    b_fc,
    w_down,
    b_down,
):
    ctx = lax.axis_index("ctx")
    tp = lax.axis_index("tp")
    first = ctx == 0

    wide = jnp.arange(DP, dtype=jnp.int32)
    inside = wide % WIDE
    source = jnp.where(inside < CHUNK, wide // WIDE * CHUNK + inside, -1)
    spread = (source[None, :] == jnp.arange(D, dtype=jnp.int32)[:, None]).astype(BF)
    mask = (inside < CHUNK).astype(F32)[None, :]

    def widen(v):
        full = v.reshape(-1, D)
        out = lax.dot_general(
            full,
            spread.astype(full.dtype),
            (((1,), (0,)), ((), ())),
            precision=lax.Precision.HIGHEST if full.dtype == F32 else None,
            preferred_element_type=F32,
        )
        return out.reshape(*v.shape[:-1], DP)

    def narrow(v):
        return lax.dot_general(
            v,
            spread.astype(v.dtype),
            (((1,), (1,)), ((), ())),
            precision=lax.Precision.HIGHEST if v.dtype == F32 else None,
            preferred_element_type=F32,
        )

    def exchanged(halves):
        keep = jnp.where(first, halves[0], halves[1])
        send = jnp.where(first, halves[1], halves[0])
        recv = swap_ctx(send)
        top = jnp.where(first, keep, recv)
        low = jnp.where(first, recv, keep)
        gap = ((0, WIDE - CHUNK), (0, 0))
        return jnp.concatenate([jnp.pad(top, gap), jnp.pad(low, gap)], axis=0)

    packs = []
    for l in range(LAYERS):
        packs.append(
            (
                exchanged([heads_first(w_qkv[l, 0], w_out[l, 0], h) for h in range(2)]),
                exchanged([hidden_first(w_fc[l], w_down[l], h) for h in range(2)]),
            )
        )

    def fetch(pack):
        return lax.all_gather(pack, "shard", axis=0, tiled=True)

    weights = [(fetch(a), fetch(b)) for a, b in packs]

    core = tp % 2
    x = (tp // 2) * 2 + ctx
    units = []
    for j in range(2):
        for m in range(4):
            chip = x ^ m
            block = (chip % 2) * 2 + chip // 2
            start = jnp.sum(jnp.where(jnp.arange(4) == block, block_order, 0)) * 256
            units.append(start + (core ^ j) * ROWS + jnp.arange(ROWS, dtype=jnp.int32))
    places = jnp.concatenate(units)
    allowed = places[None, :] <= places[:, None]
    my_count = jnp.sum(jnp.where(jnp.arange(4) == tp, head_count, 0))
    slot = jnp.arange(HEADS_HERE, dtype=jnp.int32) + ctx * HEADS_HERE
    live = ((slot < my_count) & (slot < 5)).astype(F32)

    head_bias = jnp.pad(b_qv[:, 0], ((0, 0), (0, 1), (0, 0)))
    head_bias = jnp.where(first, head_bias[:, :3], head_bias[:, 3:])
    q_bias = head_bias[:, :, :HD].reshape(LAYERS, QW)
    v_bias = head_bias[:, :, HD:].reshape(LAYERS, QW)
    fc_bias = jnp.where(first, b_fc[:, :FH], b_fc[:, FH:])

    vectors = widen(
        jnp.concatenate([ln_gain.reshape(4, D), ln_bias.reshape(4, D), b_out, b_down], axis=0)
    )
    gains = vectors[0:4].reshape(LAYERS, 2, DP)
    shifts = vectors[4:8].reshape(LAYERS, 2, DP)
    out_bias, down_bias = vectors[8:10], vectors[10:12]

    hidden = widen(tokens[0])
    gradient = widen(cotangent[0])
    stored = []
    for l in range(LAYERS):
        w_heads, w_hidden = weights[l]
        normed, xhat, rstd = norm_forward(hidden, gains[l, 0], shifts[l, 0], mask)
        normed_all = gather_rows(normed)
        projected = dot(normed_all, w_heads[:, : 3 * QW], ((1,), (0,)))
        queries = split_heads((projected[:, :QW] + q_bias[l]).astype(BF))
        keys = split_heads(projected[:, QW : 2 * QW].astype(BF))
        values = split_heads((projected[:, 2 * QW :] + v_bias[l]).astype(BF))
        attended, log_total = attend_forward(queries, keys, values, allowed, live)
        attended = join_heads(attended)
        mixed_out = dot(attended, w_heads[:, 3 * QW :], ((1,), (1,)))
        middle = hidden + (sum_rows(mixed_out) + out_bias[l])
        normed_two, xhat_two, rstd_two = norm_forward(middle, gains[l, 1], shifts[l, 1], mask)
        normed_two_all = gather_rows(normed_two)
        inner = dot(normed_two_all, w_hidden[:, :FH], ((1,), (0,))) + fc_bias[l]
        activated = gelu_exact(inner).astype(BF)
        down_out = dot(activated, w_hidden[:, FP : FP + FH], ((1,), (1,)))
        hidden = middle + (sum_rows(down_out) + down_bias[l])
        stored.append(
            (
                normed_all,
                xhat,
                rstd,
                queries,
                keys,
                values,
                log_total,
                attended,
                normed_two_all,
                xhat_two,
                rstd_two,
                inner,
                activated,
            )
        )
    mixed = narrow(hidden.astype(BF)).astype(BF)

    small = [None] * LAYERS
    biases = [None] * LAYERS
    head_sums = [None] * LAYERS
    hidden_sums = [None] * LAYERS

    def to_owner(v):
        return lax.psum_scatter(v, "shard", scatter_dimension=0, tiled=True)

    for l in reversed(range(LAYERS)):
        w_heads, w_hidden = weights[l]
        (
            normed_all,
            xhat,
            rstd,
            queries,
            keys,
            values,
            log_total,
            attended,
            normed_two_all,
            xhat_two,
            rstd_two,
            inner,
            activated,
        ) = stored[l]
        g_low = gradient.astype(BF)
        g_all = gather_rows(g_low)
        grad_down_b = jnp.sum(g_low.astype(F32), axis=0)
        grad_down_w = dot(g_all, activated, ((0,), (0,))).astype(BF)
        grad_activated = dot(g_all, w_hidden[:, FP : FP + FH], ((1,), (0,)))
        grad_inner = jax.vjp(gelu_exact, inner)[1](grad_activated)[0].astype(BF)
        grad_fc_w = dot(normed_two_all, grad_inner, ((0,), (0,))).astype(BF)
        grad_fc_b = jnp.sum(grad_inner.astype(F32), axis=0)
        grad_two = sum_rows(dot(grad_inner, w_hidden[:, :FH], ((1,), (1,))))
        dx, gain_two, shift_two = norm_backward(grad_two, xhat_two, rstd_two, gains[l, 1], mask)
        grad_middle = gradient + dx
        m_low = grad_middle.astype(BF)
        m_all = gather_rows(m_low)
        grad_out_b = jnp.sum(m_low.astype(F32), axis=0)
        grad_out_w = dot(m_all, attended, ((0,), (0,))).astype(BF)
        gap = ((0, 0), (0, FP - FH))
        hidden_sums[l] = to_owner(
            jnp.concatenate(
                [jnp.pad(grad_fc_w, gap), jnp.pad(grad_down_w, gap), grad_out_w], axis=1
            )
        )
        grad_heads = split_heads(dot(m_all, w_heads[:, 3 * QW :], ((1,), (0,))).astype(BF))
        grad_heads = grad_heads * live[:, None, None].astype(BF)
        grad_q, grad_k, grad_v = attend_backward(
            queries, keys, values, log_total, grad_heads, allowed
        )
        grad_qkv = jnp.concatenate([join_heads(a) for a in (grad_q, grad_k, grad_v)], axis=1)
        head_sums[l] = to_owner(dot(normed_all, grad_qkv, ((0,), (0,))).astype(BF))
        qkv_b = jnp.sum(grad_qkv.astype(F32), axis=0)
        grad_one = sum_rows(dot(grad_qkv, w_heads[:, : 3 * QW], ((1,), (1,))))
        dx, gain_one, shift_one = norm_backward(grad_one, xhat, rstd, gains[l, 0], mask)
        gradient = grad_middle + dx
        small[l] = [gain_one, gain_two, shift_one, shift_two, grad_out_b, grad_down_b]
        biases[l] = jnp.pad(
            jnp.concatenate([grad_fc_b, qkv_b[:QW], qkv_b[2 * QW :]]), (0, DP - FH - 2 * QW)
        )

    line = sum_line(jnp.stack(small[0] + small[1]))
    own = jnp.stack(biases)
    other = swap_ctx(own)
    both = jnp.concatenate([jnp.where(first, own, other), jnp.where(first, other, own)], axis=0)
    sums = sum_shards(jnp.concatenate([line, both], axis=0))
    vectors = narrow(sums[:12]).reshape(LAYERS, 6, D)
    halves = sums[12:].reshape(2, LAYERS, DP)
    fc_sum = jnp.concatenate([halves[0, :, :FH], halves[1, :, :FH]], axis=1)

    def slots_of(v):
        v = v.reshape(2, LAYERS, HEADS_HERE, HD)
        return jnp.concatenate([v[0], v[1, :, :2]], axis=1)

    head_sum = jnp.concatenate(
        [slots_of(halves[:, :, FH : FH + QW]), slots_of(halves[:, :, FH + QW : FH + 2 * QW])],
        axis=-1,
    )

    def own_features(v):
        keep = jnp.where(first, v[:WIDE], v[WIDE:])
        recv = swap_ctx(jnp.where(first, v[WIDE:], v[:WIDE]))
        return (
            jnp.where(first, keep, recv)[:CHUNK].astype(F32),
            jnp.where(first, recv, keep)[:CHUNK].astype(F32),
        )

    grads = [[], [], [], []]
    for l in range(LAYERS):
        a, b = own_features(head_sums[l])

        def slot_major(v, count):
            return jnp.transpose(v.reshape(CHUNK, 3, HEADS_HERE, HD)[:, :, :count], (2, 0, 1, 3))

        qkv = jnp.concatenate([slot_major(a, 3), slot_major(b, 2)], axis=0)
        grads[0].append(qkv.reshape(5, CHUNK, 3 * HD))
        a, b = own_features(hidden_sums[l])
        outs = jnp.concatenate([a[:, 2 * FP :], b[:, 2 * FP : 2 * FP + 2 * HD]], axis=1)
        grads[1].append(outs.T.reshape(5, HD, CHUNK))
        grads[2].append(jnp.concatenate([a[:, :FH], b[:, :FH]], axis=1))
        grads[3].append(jnp.concatenate([a[:, FP : FP + FH], b[:, FP : FP + FH]], axis=1).T)

    return (
        mixed[None],
        narrow(gradient)[None],
        vectors[:, 0:2],
        vectors[:, 2:4],
        jnp.stack(grads[0])[:, None],
        head_sum[:, None],
        jnp.stack(grads[1])[:, None],
        vectors[:, 4],
        jnp.stack(grads[2]),
        fc_sum,
        jnp.stack(grads[3]),
        vectors[:, 5],
    )


def solution(mesh):
    in_specs = (
        P("shard", ("ctx", "tp"), None),
        P("shard", ("ctx", "tp"), None),
        P(),
        P(),
        P(),
        P(),
        P(None, "tp", None, ("shard", "ctx"), None),
        P(None, "tp", None, None),
        P(None, "tp", None, None, ("shard", "ctx")),
        P(),
        P(None, ("shard", "ctx"), "tp"),
        P(None, "tp"),
        P(None, "tp", ("shard", "ctx")),
        P(),
    )
    out_specs = (
        P("shard", ("ctx", "tp"), None),
        P("shard", ("ctx", "tp"), None),
        P(),
        P(),
        P(None, "tp", None, ("shard", "ctx"), None),
        P(None, "tp", None, None),
        P(None, "tp", None, None, ("shard", "ctx")),
        P(),
        P(None, ("shard", "ctx"), "tp"),
        P(None, "tp"),
        P(None, "tp", ("shard", "ctx")),
        P(),
    )
    return jax.shard_map(shards, mesh=mesh, in_specs=in_specs, out_specs=out_specs, check_vma=False)
```

time: 1900 us -> 716 us (0.38)
  blocking collectives: 647 us -> 0 us
  waiting for transfers between devices: 673 us -> 318 us
  local copies, waits for them, and re-layouts: 268 us -> 69.8 us
  starting transfers between devices: 65 us -> 95.8 us
    all_gather x6 -> x4, waiting for transfers between devices: 476 us -> 39.5 us  [fetch(): return lax.all_gather(pack, 'shard', axis=0, tiled=True)]
    all_gather x6 -> x0, blocking collectives: 355 us -> none  [the longest x2 295 us: shards(): lax.all_gather(w_out[layer_idx, 0], ('shard', 'ctx'), axis=2, tiled=True)]
    psum x2 -> x0, blocking collectives: 230 us -> none  [the longest x1 165 us: shards(): head_sum, fc_sum = lax.psum((grad_head_b, grad_fc_b), ('shard', 'ctx'))]
    ppermute x0 -> x83, waiting for transfers between devices: none -> 203 us  [the longest x51 162 us: swap_x(): return lax.ppermute(v, LINE, line_perm(lambda x, k: (x ^ m, k)))]
    all_to_all x14 -> x0, waiting for transfers between devices: 124 us -> none  [the longest x6 76.3 us: sum_at_owner(): lax.all_to_all(tiles, axis, split_axis=0, concat_axis=0, tiled=True)]
    ppermute x0 -> x83, starting transfers between devices: none -> 95.6 us  [the longest x51 72 us: swap_x(): return lax.ppermute(v, LINE, line_perm(lambda x, k: (x ^ m, k)))]
    reshape x26 -> x28, local copies, waits for them, and re-layouts: 90.3 us -> 3.8 us  [the longest x16 1.57 us: heads_first(): return jnp.concatenate([a.reshape(CHUNK, QW) for a in cols], axis=1)]
    all_to_all x14 -> x0, starting transfers between devices: 60.5 us -> none  [the longest x8 33.1 us: copy_for_each(): return lax.all_to_all(copies, axis, split_axis=0, concat_axis=0, tiled=True)]
  transfers between devices with their start and end apart: 30 -> 88, of which waited for: 15 -> 47; matrix products, arithmetic and copies ran while one was open for 18% -> 25% of each run, Pallas kernels for 0% -> 0%
where the time goes in v1:
time: 716 us; the launch traced here: 709 us
  waiting for transfers between devices  318 us (44%)
  matrix products  128 us (18%)
  starting transfers between devices  95.8 us (13%)
  other arithmetic  77.7 us (11%)
  local copies, waits for them, and re-layouts  69.8 us (10%)
  between operations  20 us (3%)
    ppermute x51, waiting for transfers between devices, swap_x(): return lax.ppermute(v, LINE, line_perm(lambda x, k: (x ^ m, k)))  162 us
    dot_general x24, matrix products, dot(): return lax.dot_general(a, b, (dims, ((), ())), preferred_element_type=F32)  76.2 us
    unnamed x6, waiting for transfers between devices  75.4 us
    ppermute x51, starting transfers between devices, swap_x(): return lax.ppermute(v, LINE, line_perm(lambda x, k: (x ^ m, k)))  72 us
    all_gather x4, waiting for transfers between devices, fetch(): return lax.all_gather(pack, 'shard', axis=0, tiled=True)  39.5 us
    unnamed x295, local copies, waits for them, and re-layouts  34.7 us
    ppermute x9, waiting for transfers between devices, swap_ctx(): return lax.ppermute(v, 'ctx', [(0, 1), (1, 0)])  23.7 us
    concatenate x2, other arithmetic, shards(): jnp.concatenate([jnp.pad(grad_fc_w, gap), jnp.pad(grad_down_w, gap), grad...  17.3 us
  transfers between devices with their start and end apart: 88, of which 47 were waited for; matrix products, arithmetic and copies ran while one was open for 25% of the time, Pallas kernels for 0%

profile of v1, /device:TPU:0, one launch (start us, length us, event | category | flops | bytes accessed | tf_op | source)
XLA Modules:
  0.0 708.7 jit_solution(13813586420129392006)
XLA Ops:
  27.0 6.7 collective-permute-done.4
  47.6 34.3 %all-gather.5.cloned.1.call-done = bf16[1152,768]{1,0:T(8,128)(2,1)} async-done(((bf16[72,768]{1,0:T(8,128)(2,1)}), bf16[1152,768]{1,0:T(8,128)(2,1)}) %all-gather.5.cloned.1.call-update) | async-done | bytes 1769488 | tf_op jit(solution)/shard_map/all_gather | solution.py:219
  117.5 7.9 %collective-permute-done.8 = bf16[128,1152]{1,0:T(8,128)(2,1)S(1)} collective-permute-done((bf16[128,1152]{1,0:T(8,128)(2,1)S(1)}, bf16[128,1152]{1,0:T(8,128)(2,1)S(1)}, u32[]{:S(2)}, u32[]{:S(2)}) %collective-permute-start.8) | collective-permute-done | bytes 294944 | tf_op jit(solution)/shard_map/ppermute | solution.py:39
  131.0 11.4 %collective-permute-done.11 = bf16[128,1152]{1,0:T(8,128)(2,1)S(1)} collective-permute-done((bf16[128,1152]{1,0:T(8,128)(2,1)S(1)}, bf16[128,1152]{1,0:T(8,128)(2,1)S(1)}, u32[]{:S(2)}, u32[]{:S(2)}) %collective-permute-start.11) | collective-permute-done | bytes 294944 | tf_op jit(solution)/shard_map/ppermute | solution.py:39
  150.7 9.6 %multiply_convert_fusion.3 = (bf16[1024,544]{0,1:T(8,128)(2,1)S(1)}, f32[1024,544]{0,1:T(8,128)}, f32[1024,544]{0,1:T(8,128)}) fusion(f32[544]{0:T(1024)S(1)} %get-tuple-element.89, bf16[1024,1152]{1,0:T(8,128)(2,1)} %constant_dynamic-update-slice_fusion.6, bf16[1152,1280]{1,0:T(8,128)(2,1)} %all-gather.7.cloned.1.call-done), kind=kOutput, calls=%fused_computation.98 | convolution fusion | flops 1320222720 | bytes 9406592 | tf_op jit(solution)/shard_map/dot_general | solution.py:75
  184.0 7.5 %collective-permute-done.17 = bf16[128,1152]{1,0:T(8,128)(2,1)S(1)} collective-permute-done((bf16[128,1152]{1,0:T(8,128)(2,1)}, bf16[128,1152]{1,0:T(8,128)(2,1)S(1)}, u32[]{:S(2)}, u32[]{:S(2)}) %collective-permute-start.17) | collective-permute-done | bytes 294944 | tf_op jit(solution)/shard_map/ppermute | solution.py:39
  198.8 11.4 %collective-permute-done.20 = bf16[128,1152]{1,0:T(8,128)(2,1)S(1)} collective-permute-done((bf16[128,1152]{1,0:T(8,128)(2,1)S(1)}, bf16[128,1152]{1,0:T(8,128)(2,1)S(1)}, u32[]{:S(2)}, u32[]{:S(2)}) %collective-permute-start.20) | collective-permute-done | bytes 294944 | tf_op jit(solution)/shard_map/ppermute | solution.py:39
  262.3 7.3 %collective-permute-done.38 = bf16[128,1152]{1,0:T(8,128)(2,1)S(1)} collective-permute-done((bf16[128,1152]{1,0:T(8,128)(2,1)S(1)}, bf16[128,1152]{1,0:T(8,128)(2,1)S(1)}, u32[]{:S(2)}, u32[]{:S(2)}) %collective-permute-start.38) | collective-permute-done | bytes 294944 | tf_op jit(solution)/shard_map/ppermute | solution.py:39
  276.9 6.9 collective-permute-done.25
  289.4 10.8 %collective-permute-done.29 = bf16[128,1152]{1,0:T(8,128)(2,1)S(1)} collective-permute-done((bf16[128,1152]{1,0:T(8,128)(2,1)S(1)}, bf16[128,1152]{1,0:T(8,128)(2,1)S(1)}, u32[]{:S(2)}, u32[]{:S(2)}) %collective-permute-start.29) | collective-permute-done | bytes 294944 | tf_op jit(solution)/shard_map/ppermute | solution.py:39
  305.0 9.5 %multiply_convert_fusion.2 = (bf16[1024,544]{0,1:T(8,128)(2,1)}, f32[1024,544]{0,1:T(8,128)S(1)}, f32[1024,544]{0,1:T(8,128)S(1)}) fusion(f32[544]{0:T(1024)S(1)} %copy-done.104, bf16[1024,1152]{1,0:T(8,128)(2,1)} %constant_dynamic-update-slice_fusion.16, bf16[1152,1280]{1,0:T(8,128)(2,1)} %all-gather.11.cloned.1.call-done), kind=kOutput, calls=%fused_computation.85 | convolution fusion | flops 1320222720 | bytes 9406592 | tf_op jit(solution)/shard_map/dot_general | solution.py:75
  327.2 5.8 collective-permute-done.41
  332.9 6.8 collective-permute-done.43
  344.8 11.5 %collective-permute-done.46 = bf16[128,1152]{1,0:T(8,128)(2,1)S(1)} collective-permute-done((bf16[128,1152]{1,0:T(8,128)(2,1)S(1)}, bf16[128,1152]{1,0:T(8,128)(2,1)S(1)}, u32[]{:S(2)}, u32[]{:S(2)}) %collective-permute-start.46) | collective-permute-done | bytes 294944 | tf_op jit(solution)/shard_map/ppermute | solution.py:39
  400.7 6.8 collective-permute-done.51
  415.8 8.0 %collective-permute-done.54 = bf16[128,1152]{1,0:T(8,128)(2,1)S(1)} collective-permute-done((bf16[128,1152]{1,0:T(8,128)(2,1)S(1)}, bf16[128,1152]{1,0:T(8,128)(2,1)S(1)}, u32[]{:S(2)}, u32[]{:S(2)}) %collective-permute-start.54) | collective-permute-done | bytes 294944 | tf_op jit(solution)/shard_map/ppermute | solution.py:39
  433.7 8.6 %fusion.26 = bf16[1152,1472]{0,1:T(8,128)(2,1)} fusion(bf16[1152,544]{0,1:T(8,128)(2,1)S(1)} %convolution_convert_fusion.2, bf16[1152,544]{0,1:T(8,128)(2,1)S(1)} %convolution_convert_fusion.3, bf16[1152,192]{0,1:T(8,128)(2,1)S(1)} %convolution_convert_fusion.6), kind=kLoop, calls=%fused_computation.40 | loop fusion | flops 20348928 | bytes 6340608 | tf_op jit(solution)/shard_map/concatenate | solution.py:333
  452.7 6.7 collective-permute-done.59
  467.8 8.8 %collective-permute-done.62 = bf16[128,1152]{1,0:T(8,128)(2,1)S(1)} collective-permute-done((bf16[128,1152]{1,0:T(8,128)(2,1)S(1)}, bf16[128,1152]{1,0:T(8,128)(2,1)S(1)}, u32[]{:S(2)}, u32[]{:S(2)}) %collective-permute-start.62) | collective-permute-done | bytes 294944 | tf_op jit(solution)/shard_map/ppermute | solution.py:39
  507.4 8.6 %fusion.24 = bf16[1152,1472]{0,1:T(8,128)(2,1)} fusion(bf16[1152,544]{0,1:T(8,128)(2,1)S(1)} %copy-done.37, bf16[1152,544]{0,1:T(8,128)(2,1)S(1)} %copy-done.38, bf16[1152,192]{0,1:T(8,128)(2,1)S(1)} %convolution_convert_fusion.7), kind=kLoop, calls=%fused_computation.38 | loop fusion | flops 20348928 | bytes 6340608 | tf_op jit(solution)/shard_map/concatenate | solution.py:333
  532.3 5.7 collective-permute-done.35
  553.9 6.1 collective-permute-done.67
  595.2 75.3 %all-reduce.36.cloned.1.call-done = (bf16[1152,576]{1,0:T(8,128)(2,1)}, bf16[1152,576]{1,0:T(8,128)(2,1)}, bf16[1152,1472]{0,1:T(8,128)(2,1)}, bf16[1152,1472]{0,1:T(8,128)(2,1)}) async-done(((bf16[1152,576]{1,0:T(8,128)(2,1)}, bf16[1152,576]{1,0:T(8,128)(2,1)}, bf16[1152,1472]{0,1:T(8,128)(2,1)}, bf16[1152,1472]{0,1:T(8,128)(2,1)}), (bf16[1152,576]{1,0:T(8,128)(2,1)}, bf16[1152,576]{1,0:T(8,128)(2,1)}, ...) | async-done | bytes 9437200
  682.8 12.8 %collective-permute-done.81 = bf16[36,1472]{0,1:T(8,128)(2,1)S(1)} collective-permute-done((bf16[36,1472]{0,1:T(8,128)(2,1)S(1)}, bf16[36,1472]{0,1:T(8,128)(2,1)S(1)}, u32[]{:S(2)}, u32[]{:S(2)}) %collective-permute-start.81) | collective-permute-done | bytes 106016 | tf_op jit(solution)/shard_map/ppermute | solution.py:43
  (776 shorter events, 393.7 us)
Async XLA Ops:
  7.2 74.7 %all-gather.5.cloned.1.call-start = ((), (), s32[]{:S(2)}) async-start(), calls=%async_computation | async-start | bytes 1880064 | tf_op jit(solution)/shard_map/all_gather | solution.py:219
  15.4 26.3 %collective-permute-start.2 = (bf16[128,1152]{1,0:T(8,128)(2,1)S(1)}, bf16[128,1152]{1,0:T(8,128)(2,1)S(1)}, u32[]{:S(2)}, u32[]{:S(2)}) collective-permute-start(bf16[128,1152]{1,0:T(8,128)(2,1)S(1)} %get-tuple-element.152), channel_id=1, source_target_pairs={{0,6},{1,7},{2,4},{3,5},{4,2},{5,3},{6,0},{7,1},{8,14},{9,15},{10,... | collective-permute-start | bytes 884744 | tf_op jit(solution)/shard_map/ppermute | solution.py:39
  18.4 23.4 %collective-permute-start.1 = (bf16[128,1152]{1,0:T(8,128)(2,1)S(1)}, bf16[128,1152]{1,0:T(8,128)(2,1)S(1)}, u32[]{:S(2)}, u32[]{:S(2)}) collective-permute-start(bf16[128,1152]{1,0:T(8,128)(2,1)S(1)} %get-tuple-element.152), channel_id=1, source_target_pairs={{0,2},{1,3},{2,0},{3,1},{4,6},{5,7},{6,4},{7,5},{8,10},{9,11},{10,... | collective-permute-start | bytes 884744 | tf_op jit(solution)/shard_map/ppermute | solution.py:39
  19.2 22.6 %collective-permute-start = (bf16[128,1152]{1,0:T(8,128)(2,1)S(1)}, bf16[128,1152]{1,0:T(8,128)(2,1)S(1)}, u32[]{:S(2)}, u32[]{:S(2)}) collective-permute-start(bf16[128,1152]{1,0:T(8,128)(2,1)S(1)} %get-tuple-element.152), channel_id=1, source_target_pairs={{0,4},{1,5},{2,6},{3,7},{4,0},{5,1},{6,2},{7,3},{8,12},{9,13},{10,... | collective-permute-start | bytes 884744 | tf_op jit(solution)/shard_map/ppermute | solution.py:39
  34.5 116.2 %all-gather.7.cloned.1.call-start = ((), (), s32[]{:S(2)}) async-start(), calls=%async_computation.1 | async-start | bytes 3133440 | tf_op jit(solution)/shard_map/all_gather | solution.py:219
  35.2 66.8 %collective-permute-start.13 = (bf16[34,1280]{1,0:T(8,128)(2,1)}, bf16[34,1280]{1,0:T(8,128)(2,1)}, u32[]{:S(2)}, u32[]{:S(2)}) collective-permute-start(bf16[34,1280]{1,0:T(8,128)(2,1)} %broadcast_select_fusion.10), channel_id=1, source_target_pairs={{0,4},{4,0},{1,5},{5,1},{2,6},{6,2},{3,7},{7,3},{8,12},{12,8},{9,1... | collective-permute-start | bytes 261128 | tf_op jit(solution)/shard_map/ppermute | solution.py:43
  103.7 119.4 %all-gather.9.cloned.1.call-start = ((), (), s32[]{:S(2)}) async-start(), calls=%async_computation.2 | async-start | bytes 1880064 | tf_op jit(solution)/shard_map/all_gather | solution.py:219
  109.1 16.3 %collective-permute-start.8 = (bf16[128,1152]{1,0:T(8,128)(2,1)S(1)}, bf16[128,1152]{1,0:T(8,128)(2,1)S(1)}, u32[]{:S(2)}, u32[]{:S(2)}) collective-permute-start(bf16[128,1152]{1,0:T(8,128)(2,1)S(1)} %get-tuple-element.187), channel_id=1, source_target_pairs={{0,6},{1,7},{2,4},{3,5},{4,2},{5,3},{6,0},{7,1},{8,14},{9,15},{10,... | collective-permute-start | bytes 884744 | tf_op jit(solution)/shard_map/ppermute | solution.py:39
  175.0 16.5 %collective-permute-start.17 = (bf16[128,1152]{1,0:T(8,128)(2,1)}, bf16[128,1152]{1,0:T(8,128)(2,1)S(1)}, u32[]{:S(2)}, u32[]{:S(2)}) collective-permute-start(bf16[128,1152]{1,0:T(8,128)(2,1)} %get-tuple-element.184), channel_id=1, source_target_pairs={{0,6},{1,7},{2,4},{3,5},{4,2},{5,3},{6,0},{7,1},{8,14},{9,15},{10,... | collective-permute-start | bytes 884744 | tf_op jit(solution)/shard_map/ppermute | solution.py:39
  179.6 125.4 %all-gather.11.cloned.1.call-start = ((), (), s32[]{:S(2)}) async-start(), calls=%async_computation.3 | async-start | bytes 3133440 | tf_op jit(solution)/shard_map/all_gather | solution.py:219
  249.5 420.9 %all-reduce.36.cloned.1.call-start = ((), (), s32[]{:S(2)}) async-start(), calls=%async_computation.4 | async-start | bytes 19464192
  252.2 17.4 %collective-permute-start.38 = (bf16[128,1152]{1,0:T(8,128)(2,1)S(1)}, bf16[128,1152]{1,0:T(8,128)(2,1)S(1)}, u32[]{:S(2)}, u32[]{:S(2)}) collective-permute-start(bf16[128,1152]{1,0:T(8,128)(2,1)S(1)} %get-tuple-element.103), channel_id=1, source_target_pairs={{0,6},{1,7},{2,4},{3,5},{4,2},{5,3},{6,0},{7,1},{8,14},{9,15},{10,... | collective-permute-start | bytes 884744 | tf_op jit(solution)/shard_map/ppermute | solution.py:39
  254.9 16.6 %collective-permute-start.37 = (bf16[128,1152]{1,0:T(8,128)(2,1)S(1)}, bf16[128,1152]{1,0:T(8,128)(2,1)S(1)}, u32[]{:S(2)}, u32[]{:S(2)}) collective-permute-start(bf16[128,1152]{1,0:T(8,128)(2,1)S(1)} %get-tuple-element.103), channel_id=1, source_target_pairs={{0,2},{1,3},{2,0},{3,1},{4,6},{5,7},{6,4},{7,5},{8,10},{9,11},{10,... | collective-permute-start | bytes 884744 | tf_op jit(solution)/shard_map/ppermute | solution.py:39
  255.4 16.0 %collective-permute-start.36 = (bf16[128,1152]{1,0:T(8,128)(2,1)S(1)}, bf16[128,1152]{1,0:T(8,128)(2,1)S(1)}, u32[]{:S(2)}, u32[]{:S(2)}) collective-permute-start(bf16[128,1152]{1,0:T(8,128)(2,1)S(1)} %get-tuple-element.103), channel_id=1, source_target_pairs={{0,4},{1,5},{2,6},{3,7},{4,0},{5,1},{6,2},{7,3},{8,12},{9,13},{10,... | collective-permute-start | bytes 884744 | tf_op jit(solution)/shard_map/ppermute | solution.py:39
  258.7 18.2 %collective-permute-start.24 = (bf16[128,1152]{1,0:T(8,128)(2,1)S(1)}, bf16[128,1152]{1,0:T(8,128)(2,1)S(1)}, u32[]{:S(2)}, u32[]{:S(2)}) collective-permute-start(bf16[128,1152]{1,0:T(8,128)(2,1)S(1)} %get-tuple-element.180), channel_id=1, source_target_pairs={{0,4},{1,5},{2,6},{3,7},{4,0},{5,1},{6,2},{7,3},{8,12},{9,13},{10,... | collective-permute-start | bytes 884744 | tf_op jit(solution)/shard_map/ppermute | solution.py:39
  259.9 16.9 %collective-permute-start.26 = (bf16[128,1152]{1,0:T(8,128)(2,1)S(1)}, bf16[128,1152]{1,0:T(8,128)(2,1)S(1)}, u32[]{:S(2)}, u32[]{:S(2)}) collective-permute-start(bf16[128,1152]{1,0:T(8,128)(2,1)S(1)} %get-tuple-element.181), channel_id=1, source_target_pairs={{0,6},{1,7},{2,4},{3,5},{4,2},{5,3},{6,0},{7,1},{8,14},{9,15},{10,... | collective-permute-start | bytes 884744 | tf_op jit(solution)/shard_map/ppermute | solution.py:39
  271.6 29.5 %collective-permute-start.39 = (bf16[512,1152]{1,0:T(8,128)(2,1)S(1)}, bf16[512,1152]{1,0:T(8,128)(2,1)S(1)}, u32[]{:S(2)}, u32[]{:S(2)}) collective-permute-start(bf16[512,1152]{1,0:T(8,128)(2,1)S(1)} %pad_maximum_fusion.4), channel_id=1, source_target_pairs={{0,1},{1,0},{2,3},{3,2},{4,5},{5,4},{6,7},{7,6},{8,9},{9,8},{10,11... | collective-permute-start | bytes 3538952 | tf_op jit(solution)/shard_map/ppermute | solution.py:35
  323.3 16.5 %collective-permute-start.43 = (bf16[128,1152]{1,0:T(8,128)(2,1)S(1)}, bf16[128,1152]{1,0:T(8,128)(2,1)S(1)}, u32[]{:S(2)}, u32[]{:S(2)}) collective-permute-start(bf16[128,1152]{1,0:T(8,128)(2,1)S(1)} %get-tuple-element.175), channel_id=1, source_target_pairs={{0,6},{1,7},{2,4},{3,5},{4,2},{5,3},{6,0},{7,1},{8,14},{9,15},{10,... | collective-permute-start | bytes 884744 | tf_op jit(solution)/shard_map/ppermute | solution.py:39
  389.1 127.0 %collective-permute-start.32 = (bf16[512,1152]{1,0:T(8,128)(2,1)}, bf16[512,1152]{1,0:T(8,128)(2,1)}, u32[]{:S(2)}, u32[]{:S(2)}) collective-permute-start(bf16[512,1152]{1,0:T(8,128)(2,1)} %slice.1091), channel_id=1, source_target_pairs={{0,1},{1,0},{2,3},{3,2},{4,5},{5,4},{6,7},{7,6},{8,9},{9,8},{10,11... | collective-permute-start | bytes 3538952 | tf_op jit(solution)/shard_map/ppermute | solution.py:35
  391.1 16.4 %collective-permute-start.51 = (bf16[128,1152]{1,0:T(8,128)(2,1)S(1)}, bf16[128,1152]{1,0:T(8,128)(2,1)S(1)}, u32[]{:S(2)}, u32[]{:S(2)}) collective-permute-start(bf16[128,1152]{1,0:T(8,128)(2,1)S(1)} %get-tuple-element.172), channel_id=1, source_target_pairs={{0,6},{1,7},{2,4},{3,5},{4,2},{5,3},{6,0},{7,1},{8,14},{9,15},{10,... | collective-permute-start | bytes 884744 | tf_op jit(solution)/shard_map/ppermute | solution.py:39
  442.8 16.6 %collective-permute-start.59 = (bf16[128,1152]{1,0:T(8,128)(2,1)S(1)}, bf16[128,1152]{1,0:T(8,128)(2,1)S(1)}, u32[]{:S(2)}, u32[]{:S(2)}) collective-permute-start(bf16[128,1152]{1,0:T(8,128)(2,1)S(1)} %get-tuple-element.169), channel_id=1, source_target_pairs={{0,6},{1,7},{2,4},{3,5},{4,2},{5,3},{6,0},{7,1},{8,14},{9,15},{10,... | collective-permute-start | bytes 884744 | tf_op jit(solution)/shard_map/ppermute | solution.py:39
  520.8 17.2 %collective-permute-start.35 = (bf16[128,1152]{1,0:T(8,128)(2,1)}, bf16[128,1152]{1,0:T(8,128)(2,1)}, u32[]{:S(2)}, u32[]{:S(2)}) collective-permute-start(bf16[128,1152]{1,0:T(8,128)(2,1)} %get-tuple-element.178), channel_id=1, source_target_pairs={{0,6},{1,7},{2,4},{3,5},{4,2},{5,3},{6,0},{7,1},{8,14},{9,15},{10,... | collective-permute-start | bytes 884744 | tf_op jit(solution)/shard_map/ppermute | solution.py:39
  678.1 17.7 %collective-permute-start.82 = (bf16[36,1472]{0,1:T(8,128)(2,1)S(1)}, bf16[36,1472]{0,1:T(8,128)(2,1)S(1)}, u32[]{:S(2)}, u32[]{:S(2)}) collective-permute-start(bf16[36,1472]{0,1:T(8,128)(2,1)S(1)} %get-tuple-element.156), channel_id=1, source_target_pairs={{0,4},{4,0},{1,5},{5,1},{2,6},{6,2},{3,7},{7,3},{8,12},{12,8},{9,1... | collective-permute-start | bytes 317960 | tf_op jit(solution)/shard_map/ppermute | solution.py:43
  679.7 15.9 %collective-permute-start.81 = (bf16[36,1472]{0,1:T(8,128)(2,1)S(1)}, bf16[36,1472]{0,1:T(8,128)(2,1)S(1)}, u32[]{:S(2)}, u32[]{:S(2)}) collective-permute-start(bf16[36,1472]{0,1:T(8,128)(2,1)S(1)} %get-tuple-element.154), channel_id=1, source_target_pairs={{0,4},{4,0},{1,5},{5,1},{2,6},{6,2},{3,7},{7,3},{8,12},{12,8},{9,1... | collective-permute-start | bytes 317960 | tf_op jit(solution)/shard_map/ppermute | solution.py:43
  (194 other events, 2360.6 us)
Sparse Core Ops, SparseCore 0:
  34.6 47.1 all-gather.4
  103.8 46.8 all-gather.6
  179.7 43.3 all-gather.8
  249.7 46.6 all-gather.10
  516.2 154.1 all-reduce.35

commit v2 on v1

--- a/solution.py
+++ b/solution.py
@@ -1,6 +1,8 @@
 import jax
 import jax.numpy as jnp
 from jax import lax
+from jax.experimental import pallas as pl
+from jax.experimental.pallas import tpu as pltpu
 from jax.sharding import PartitionSpec as P
 
 D = 1088
@@ -13,8 +15,9 @@
 DP = 2 * SHARDS * WIDE
 HEADS_HERE = 3
 QW = HEADS_HERE * HD
-FH = 544
-FP = 640
+FR = 1088
+FC = 2 * FR
+HW = 4 * QW
 ROWS = 128
 BF = jnp.bfloat16
 F32 = jnp.float32
@@ -47,6 +50,45 @@
     return lax.ppermute(v, "shard", [(i, i ^ m) for i in range(SHARDS)])
 
 
+def ordered(parts, place):
+    odd, high = place % 2 == 1, place // 2 == 1
+    parts = [jnp.where(odd, parts[i ^ 1], parts[i]) for i in range(4)]
+    return jnp.concatenate([jnp.where(high, parts[i ^ 2], parts[i]) for i in range(4)], axis=0)
+
+
+def gather_shards(v):
+    shard = lax.axis_index("shard")
+    v = ordered([v] + [swap_shard(v, m) for m in (1, 2, 3)], shard % 4)
+    return ordered([v] + [swap_shard(v, 4 * m) for m in (1, 2, 3)], shard // 4)
+
+
+def to_shards(v):
+    shard = lax.axis_index("shard")
+
+    def stage(v, axis, step):
+        place = shard // step % 4
+
+        def part(m):
+            return lax.dynamic_index_in_dim(v, place ^ m, axis, keepdims=False)
+
+        came = [swap_shard(part(m).astype(BF), m * step).astype(F32) for m in (1, 2, 3)]
+        return (part(0).astype(F32) + came[0]) + (came[1] + came[2])
+
+    v = v.reshape(4, 4, v.shape[0] // SHARDS, v.shape[1])
+    half = v.shape[3] // 2
+    a = stage(stage(v[..., :half], 1, 1), 0, 4)
+    b = stage(stage(v[..., half:], 0, 4), 0, 1)
+    return jnp.concatenate([a, b], axis=1)
+
+
+def gather_pair(piece):
+    return jnp.concatenate([piece, swap_core(piece)], axis=0)
+
+
+def sum_pair(partial):
+    return partial[:ROWS] + swap_core(partial[ROWS:].astype(BF)).astype(F32)
+
+
 def gather_rows(piece):
     mine = jnp.concatenate([piece] + [swap_x(piece, m) for m in (1, 2, 3)], axis=0)
     return jnp.concatenate([mine, swap_core(mine)], axis=0)
@@ -66,8 +108,8 @@
     return (v + swap_shard(v, 4)) + (swap_shard(v, 8) + swap_shard(v, 12))
 
 
-def sum_line(v):
-    v = v + swap_core(v)
+def sum_line_parts(both_cores, each_core):
+    v = jnp.concatenate([both_cores + swap_core(both_cores), each_core], axis=0)
     return (v + swap_x(v, 1)) + (swap_x(v, 2) + swap_x(v, 3))
 
 
@@ -97,11 +139,14 @@
 
 
 def split_heads(v):
-    return jnp.moveaxis(v.reshape(v.shape[0], HEADS_HERE, HD), 1, 0)
-
-
-def join_heads(v):
-    return jnp.moveaxis(v, 0, 1).reshape(v.shape[1], HEADS_HERE * HD)
+    parts = v.shape[1] // QW
+    v = v.reshape(v.shape[0], HEADS_HERE, parts, HD)
+    return [jnp.moveaxis(v[:, :, i], 1, 0) for i in range(parts)]
+
+
+def join_heads(*parts):
+    v = jnp.stack(parts, axis=2)
+    return jnp.moveaxis(v, 0, 1).reshape(v.shape[1], -1)
 
 
 def attend_forward(queries, keys, values, allowed, live):
@@ -131,24 +176,55 @@
     )
 
 
-def heads_first(w_qkv, w_out, h):
-    first, count = (0, 3) if h == 0 else (3, 2)
-    picked = jnp.moveaxis(w_qkv[first : first + count], 0, 1)
-    outs = jnp.moveaxis(w_out[first : first + count], 2, 0)
-    cols = [picked[:, :, i * HD : (i + 1) * HD] for i in range(3)] + [outs]
-    cols = [jnp.pad(a, ((0, 0), (0, HEADS_HERE - count), (0, 0))) for a in cols]
-    return jnp.concatenate([a.reshape(CHUNK, QW) for a in cols], axis=1)
-
-
-def hidden_first(w_fc, w_down, h):
-    gap = ((0, 0), (0, FP - FH))
-    return jnp.concatenate(
-        [
-            jnp.pad(w_fc[:, h * FH : (h + 1) * FH], gap),
-            jnp.pad(w_down[h * FH : (h + 1) * FH].T, gap),
-        ],
-        axis=1,
-    )
+def head_halves(w_qkv, w_out):
+    cols = jnp.moveaxis(w_qkv, 0, 1).reshape(CHUNK, 15 * HD)
+    outs = w_out.reshape(5 * HD, CHUNK).T
+    gap = ((0, 0), (0, HD))
+    return (
+        jnp.concatenate([cols[:, : 3 * QW], outs[:, :QW]], axis=1),
+        jnp.concatenate(
+            [jnp.pad(cols[:, 3 * QW :], ((0, 0), (0, QW))), jnp.pad(outs[:, QW:], gap)], axis=1
+        ),
+    )
+
+
+GRAD_ROWS = 384
+
+
+def hidden_grads_body(heads, x_ref, dinner_ref, g_ref, act_ref, *refs):
+    out_ref = refs[-1]
+    turned = (((0,), (0,)), ((), ()))
+    out_ref[:, :FC] = lax.dot_general(
+        x_ref[...], dinner_ref[...], turned, preferred_element_type=F32
+    ).astype(BF)
+    out_ref[:, FC : 2 * FC] = lax.dot_general(
+        g_ref[...], act_ref[...], turned, preferred_element_type=F32
+    ).astype(BF)
+    if heads:
+        out_ref[:, 2 * FC :] = refs[0][...]
+
+
+def hidden_grads(x, dinner, g, act, head_grads=None):
+    rows = x.shape[0]
+    wide = 2 * FC + (0 if head_grads is None else HW)
+    args = [x, dinner, g, act] + ([] if head_grads is None else [head_grads])
+    feature = pl.BlockSpec((rows, GRAD_ROWS), lambda i: (0, i))
+    whole = pl.BlockSpec((rows, FC), lambda i: (0, 0))
+    specs = [feature, whole, feature, whole]
+    if head_grads is not None:
+        specs.append(pl.BlockSpec((GRAD_ROWS, HW), lambda i: (i, 0)))
+    return pl.pallas_call(
+        lambda *refs: hidden_grads_body(head_grads is not None, *refs),
+        grid=(DP // GRAD_ROWS,),
+        in_specs=specs,
+        out_specs=pl.BlockSpec((GRAD_ROWS, wide), lambda i: (i, 0)),
+        out_shape=jax.ShapeDtypeStruct((DP, wide), BF),
+        compiler_params=pltpu.CompilerParams(vmem_limit_bytes=48 << 20),
+        cost_estimate=pl.CostEstimate(
+            flops=4 * rows * DP * FC, bytes_accessed=2 * DP * wide, transcendentals=0
+        ),
+        name="hidden_grads",
+    )(*args)
 
 
 def shards(
@@ -206,19 +282,31 @@
         gap = ((0, WIDE - CHUNK), (0, 0))
         return jnp.concatenate([jnp.pad(top, gap), jnp.pad(low, gap)], axis=0)
 
-    packs = []
-    for l in range(LAYERS):
-        packs.append(
-            (
-                exchanged([heads_first(w_qkv[l, 0], w_out[l, 0], h) for h in range(2)]),
-                exchanged([hidden_first(w_fc[l], w_down[l], h) for h in range(2)]),
-            )
-        )
+    def exchanged_hidden(w_fc, w_down):
+        raw = jnp.concatenate([w_fc, w_down.T], axis=1)
+        raw = jnp.pad(raw, ((0, WIDE - CHUNK), (0, 0)))
+        p = [raw] + [swap_x(raw, m) for m in (1, 2, 3)]
+        own, other = [
+            jnp.concatenate([jnp.where(first, a, b), jnp.where(first, b, a)], axis=0)
+            for a, b in ((p[0], p[1]), (p[2], p[3]))
+        ]
+        return jnp.concatenate([own[:, :FR], other[:, :FR], own[:, FR:], other[:, FR:]], axis=1)
 
     def fetch(pack):
         return lax.all_gather(pack, "shard", axis=0, tiled=True)
 
-    weights = [(fetch(a), fetch(b)) for a, b in packs]
+    halves_a = head_halves(w_qkv[0, 0], w_out[0, 0])
+    pack_a = exchanged(halves_a)
+    w_fc_a, w_down_a, w_qkv_b, w_out_b, pack_a = lax.optimization_barrier(
+        (w_fc[0], w_down[0], w_qkv[1, 0], w_out[1, 0], pack_a)
+    )
+    hidden_a = exchanged_hidden(w_fc_a, w_down_a)
+    heads_b = exchanged(head_halves(w_qkv_b, w_out_b))
+    fetched_a = fetch(jnp.concatenate([hidden_a, heads_b], axis=1))
+    weights = [
+        (gather_shards(pack_a), fetched_a[:, : 2 * FC]),
+        (fetched_a[:, 2 * FC :], None),
+    ]
 
     core = tp % 2
     x = (tp // 2) * 2 + ctx
@@ -237,9 +325,10 @@
 
     head_bias = jnp.pad(b_qv[:, 0], ((0, 0), (0, 1), (0, 0)))
     head_bias = jnp.where(first, head_bias[:, :3], head_bias[:, 3:])
-    q_bias = head_bias[:, :, :HD].reshape(LAYERS, QW)
-    v_bias = head_bias[:, :, HD:].reshape(LAYERS, QW)
-    fc_bias = jnp.where(first, b_fc[:, :FH], b_fc[:, FH:])
+    head_bias = jnp.concatenate(
+        [head_bias[..., :HD], jnp.zeros_like(head_bias[..., :HD]), head_bias[..., HD:]], axis=-1
+    ).reshape(LAYERS, 3 * QW)
+    fc_bias = jnp.concatenate([b_fc, swap_x(b_fc, 2)], axis=1)
 
     vectors = widen(
         jnp.concatenate([ln_gain.reshape(4, D), ln_bias.reshape(4, D), b_out, b_down], axis=0)
@@ -255,20 +344,23 @@
         w_heads, w_hidden = weights[l]
         normed, xhat, rstd = norm_forward(hidden, gains[l, 0], shifts[l, 0], mask)
         normed_all = gather_rows(normed)
+        if l == 0:
+            normed_all, w_fc_b, w_down_b = lax.optimization_barrier(
+                (normed_all, w_fc[1], w_down[1])
+            )
+            weights[1] = (weights[1][0], fetch(exchanged_hidden(w_fc_b, w_down_b)))
         projected = dot(normed_all, w_heads[:, : 3 * QW], ((1,), (0,)))
-        queries = split_heads((projected[:, :QW] + q_bias[l]).astype(BF))
-        keys = split_heads(projected[:, QW : 2 * QW].astype(BF))
-        values = split_heads((projected[:, 2 * QW :] + v_bias[l]).astype(BF))
+        queries, keys, values = split_heads((projected + head_bias[l]).astype(BF))
         attended, log_total = attend_forward(queries, keys, values, allowed, live)
         attended = join_heads(attended)
         mixed_out = dot(attended, w_heads[:, 3 * QW :], ((1,), (1,)))
         middle = hidden + (sum_rows(mixed_out) + out_bias[l])
         normed_two, xhat_two, rstd_two = norm_forward(middle, gains[l, 1], shifts[l, 1], mask)
-        normed_two_all = gather_rows(normed_two)
-        inner = dot(normed_two_all, w_hidden[:, :FH], ((1,), (0,))) + fc_bias[l]
+        normed_two_all = gather_pair(normed_two)
+        inner = dot(normed_two_all, w_hidden[:, :FC], ((1,), (0,))) + fc_bias[l]
         activated = gelu_exact(inner).astype(BF)
-        down_out = dot(activated, w_hidden[:, FP : FP + FH], ((1,), (1,)))
-        hidden = middle + (sum_rows(down_out) + down_bias[l])
+        down_out = dot(activated, w_hidden[:, FC:], ((1,), (1,)))
+        hidden = middle + (sum_pair(down_out) + down_bias[l])
         stored.append(
             (
                 normed_all,
@@ -289,12 +381,14 @@
     mixed = narrow(hidden.astype(BF)).astype(BF)
 
     small = [None] * LAYERS
-    biases = [None] * LAYERS
-    head_sums = [None] * LAYERS
+    fc_biases, head_biases = [], []
+    high = tp // 2 == 1
     hidden_sums = [None] * LAYERS
 
-    def to_owner(v):
-        return lax.psum_scatter(v, "shard", scatter_dimension=0, tiled=True)
+    def to_owner(v, dim):
+        v = v.reshape((1,) * dim + v.shape)
+        v = lax.psum_scatter(v, "shard", scatter_dimension=dim, tiled=True)
+        return lax.optimization_barrier(v).reshape(v.shape[-2:])
 
     for l in reversed(range(LAYERS)):
         w_heads, w_hidden = weights[l]
@@ -314,59 +408,56 @@
             activated,
         ) = stored[l]
         g_low = gradient.astype(BF)
-        g_all = gather_rows(g_low)
+        g_all = gather_pair(g_low)
         grad_down_b = jnp.sum(g_low.astype(F32), axis=0)
-        grad_down_w = dot(g_all, activated, ((0,), (0,))).astype(BF)
-        grad_activated = dot(g_all, w_hidden[:, FP : FP + FH], ((1,), (0,)))
+        grad_activated = dot(g_all, w_hidden[:, FC:], ((1,), (0,)))
         grad_inner = jax.vjp(gelu_exact, inner)[1](grad_activated)[0].astype(BF)
-        grad_fc_w = dot(normed_two_all, grad_inner, ((0,), (0,))).astype(BF)
         grad_fc_b = jnp.sum(grad_inner.astype(F32), axis=0)
-        grad_two = sum_rows(dot(grad_inner, w_hidden[:, :FH], ((1,), (1,))))
+        hidden_sums[l] = to_owner(
+            hidden_grads(
+                normed_two_all, grad_inner, g_all, activated, head_grads if l == 0 else None
+            ),
+            1 - l,
+        )
+        grad_two = sum_pair(dot(grad_inner, w_hidden[:, :FC], ((1,), (1,))))
         dx, gain_two, shift_two = norm_backward(grad_two, xhat_two, rstd_two, gains[l, 1], mask)
         grad_middle = gradient + dx
         m_low = grad_middle.astype(BF)
         m_all = gather_rows(m_low)
         grad_out_b = jnp.sum(m_low.astype(F32), axis=0)
         grad_out_w = dot(m_all, attended, ((0,), (0,))).astype(BF)
-        gap = ((0, 0), (0, FP - FH))
-        hidden_sums[l] = to_owner(
-            jnp.concatenate(
-                [jnp.pad(grad_fc_w, gap), jnp.pad(grad_down_w, gap), grad_out_w], axis=1
-            )
-        )
-        grad_heads = split_heads(dot(m_all, w_heads[:, 3 * QW :], ((1,), (0,))).astype(BF))
+        (grad_heads,) = split_heads(dot(m_all, w_heads[:, 3 * QW :], ((1,), (0,))).astype(BF))
         grad_heads = grad_heads * live[:, None, None].astype(BF)
         grad_q, grad_k, grad_v = attend_backward(
             queries, keys, values, log_total, grad_heads, allowed
         )
-        grad_qkv = jnp.concatenate([join_heads(a) for a in (grad_q, grad_k, grad_v)], axis=1)
-        head_sums[l] = to_owner(dot(normed_all, grad_qkv, ((0,), (0,))).astype(BF))
+        grad_qkv = join_heads(grad_q, grad_k, grad_v)
+        grad_qkv_w = dot(normed_all, grad_qkv, ((0,), (0,))).astype(BF)
+        head_grads = jnp.concatenate([grad_qkv_w, grad_out_w], axis=1)
         qkv_b = jnp.sum(grad_qkv.astype(F32), axis=0)
         grad_one = sum_rows(dot(grad_qkv, w_heads[:, : 3 * QW], ((1,), (1,))))
         dx, gain_one, shift_one = norm_backward(grad_one, xhat, rstd, gains[l, 0], mask)
         gradient = grad_middle + dx
         small[l] = [gain_one, gain_two, shift_one, shift_two, grad_out_b, grad_down_b]
-        biases[l] = jnp.pad(
-            jnp.concatenate([grad_fc_b, qkv_b[:QW], qkv_b[2 * QW :]]), (0, DP - FH - 2 * QW)
-        )
-
-    line = sum_line(jnp.stack(small[0] + small[1]))
-    own = jnp.stack(biases)
+        fc_biases.append(
+            jnp.where(high, jnp.roll(grad_fc_b, FR), grad_fc_b)
+        )
+        head_biases.append(qkv_b)
+
+    line = sum_line_parts(
+        jnp.stack(small[0] + small[1]),
+        jnp.pad(jnp.stack(fc_biases[::-1]), ((0, 0), (0, 2 * DP - FC))).reshape(4, DP),
+    )
+    own = jnp.pad(jnp.stack(head_biases[::-1]), ((0, 0), (0, DP - 3 * QW)))
     other = swap_ctx(own)
     both = jnp.concatenate([jnp.where(first, own, other), jnp.where(first, other, own)], axis=0)
     sums = sum_shards(jnp.concatenate([line, both], axis=0))
     vectors = narrow(sums[:12]).reshape(LAYERS, 6, D)
-    halves = sums[12:].reshape(2, LAYERS, DP)
-    fc_sum = jnp.concatenate([halves[0, :, :FH], halves[1, :, :FH]], axis=1)
-
-    def slots_of(v):
-        v = v.reshape(2, LAYERS, HEADS_HERE, HD)
-        return jnp.concatenate([v[0], v[1, :, :2]], axis=1)
-
-    head_sum = jnp.concatenate(
-        [slots_of(halves[:, :, FH : FH + QW]), slots_of(halves[:, :, FH + QW : FH + 2 * QW])],
-        axis=-1,
-    )
+    fc_sum = sums[12:16].reshape(LAYERS, 2 * DP)
+    fc_sum = jnp.where(high, fc_sum[:, FR : 2 * FR], fc_sum[:, :FR])
+    halves = sums[16:].reshape(2, LAYERS, DP)[:, :, : 3 * QW].reshape(2, LAYERS, 3, 3, HD)
+    head_sum = jnp.concatenate([halves[0], halves[1, :, :2]], axis=1)
+    head_sum = jnp.concatenate([head_sum[:, :, 0], head_sum[:, :, 2]], axis=-1)
 
     def own_features(v):
         keep = jnp.where(first, v[:WIDE], v[WIDE:])
@@ -376,20 +467,29 @@
             jnp.where(first, recv, keep)[:CHUNK].astype(F32),
         )
 
+    def own_hidden(v):
+        mine = jnp.where(first, v[:WIDE], v[WIDE:])
+        theirs = jnp.where(first, v[WIDE:], v[:WIDE])
+
+        def piece(rows, h):
+            return jnp.concatenate(
+                [rows[:, h * FR : (h + 1) * FR], rows[:, FC + h * FR : FC + (h + 1) * FR]], axis=1
+            )
+
+        came = [swap_x(piece(theirs if m % 2 else mine, m // 2), m).astype(F32) for m in (1, 2, 3)]
+        return ((piece(mine, 0).astype(F32) + came[0]) + (came[1] + came[2]))[:CHUNK]
+
+    head_sums = [to_shards(head_grads).astype(BF), hidden_sums[0][:, 2 * FC :]]
     grads = [[], [], [], []]
     for l in range(LAYERS):
         a, b = own_features(head_sums[l])
-
-        def slot_major(v, count):
-            return jnp.transpose(v.reshape(CHUNK, 3, HEADS_HERE, HD)[:, :, :count], (2, 0, 1, 3))
-
-        qkv = jnp.concatenate([slot_major(a, 3), slot_major(b, 2)], axis=0)
-        grads[0].append(qkv.reshape(5, CHUNK, 3 * HD))
-        a, b = own_features(hidden_sums[l])
-        outs = jnp.concatenate([a[:, 2 * FP :], b[:, 2 * FP : 2 * FP + 2 * HD]], axis=1)
+        qkv = jnp.concatenate([a[:, : 3 * QW], b[:, : 2 * QW]], axis=1).reshape(CHUNK, 5, 3 * HD)
+        grads[0].append(jnp.moveaxis(qkv, 1, 0))
+        outs = jnp.concatenate([a[:, 3 * QW :], b[:, 3 * QW : 3 * QW + 2 * HD]], axis=1)
         grads[1].append(outs.T.reshape(5, HD, CHUNK))
-        grads[2].append(jnp.concatenate([a[:, :FH], b[:, :FH]], axis=1))
-        grads[3].append(jnp.concatenate([a[:, FP : FP + FH], b[:, FP : FP + FH]], axis=1).T)
+        both = own_hidden(hidden_sums[l][:, : 2 * FC])
+        grads[2].append(both[:, :FR])
+        grads[3].append(both[:, FR:].T)
 
     return (
         mixed[None],

time: 716 us -> 544 us (0.76)
  waiting for transfers between devices: 318 us -> 169 us
  other arithmetic: 77.7 us -> 54.1 us
  local copies, waits for them, and re-layouts: 69.8 us -> 57.3 us
  Pallas kernels: 0 us -> 12 us
    unnamed x6, waiting for transfers between devices: 75.4 us -> 0.09 us
    ppermute x51 -> x40, waiting for transfers between devices: 162 us -> 98.4 us  [swap_x(): return lax.ppermute(v, LINE, line_perm(lambda x, k: (x ^ m, k)))]
    ppermute x6 -> x24, waiting for transfers between devices: 7.02 us -> 54.6 us  [swap_shard(): return lax.ppermute(v, 'shard', [(i, i ^ m) for i in range(SHARDS)])]
    all_gather x4 -> x2, waiting for transfers between devices: 39.5 us -> 0.04 us  [fetch(): return lax.all_gather(pack, 'shard', axis=0, tiled=True)]
    ppermute x6 -> x24, starting transfers between devices: 8.5 us -> 32 us  [swap_shard(): return lax.ppermute(v, 'shard', [(i, i ^ m) for i in range(SHARDS)])]
    ppermute x9 -> x5, waiting for transfers between devices: 23.7 us -> 2.11 us  [swap_ctx(): return lax.ppermute(v, 'ctx', [(0, 1), (1, 0)])]
    concatenate x7 -> x22, other arithmetic: 18.4 us -> 2.19 us  [the longest x6 0.58 us: piece(): jnp.concatenate([rows[:, h * FR:(h + 1) * FR], rows[:, FC + h * FR:FC + (...]
    ppermute x51 -> x40, starting transfers between devices: 72 us -> 56 us  [swap_x(): return lax.ppermute(v, LINE, line_perm(lambda x, k: (x ^ m, k)))]
  transfers between devices with their start and end apart: 88 -> 90, of which waited for: 47 -> 53; matrix products, arithmetic and copies ran while one was open for 25% -> 38% of each run, Pallas kernels for 0% -> 1%
where the time goes in v2:
time: 544 us; the launch traced here: 534 us
  waiting for transfers between devices  169 us (31%)
  matrix products  127 us (23%)
  starting transfers between devices  96.1 us (18%)
  local copies, waits for them, and re-layouts  57.3 us (11%)
  other arithmetic  54.1 us (10%)
  between operations  19.4 us (4%)
  Pallas kernels  12 us (2%)
    ppermute x40, waiting for transfers between devices, swap_x(): return lax.ppermute(v, LINE, line_perm(lambda x, k: (x ^ m, k)))  98.4 us
    dot_general x20, matrix products, dot(): return lax.dot_general(a, b, (dims, ((), ())), preferred_element_type=F32)  66.4 us
    ppermute x40, starting transfers between devices, swap_x(): return lax.ppermute(v, LINE, line_perm(lambda x, k: (x ^ m, k)))  56 us
    ppermute x24, waiting for transfers between devices, swap_shard(): return lax.ppermute(v, 'shard', [(i, i ^ m) for i in range(SHARDS)])  54.6 us
    ppermute x24, starting transfers between devices, swap_shard(): return lax.ppermute(v, 'shard', [(i, i ^ m) for i in range(SHARDS)])  32 us
    unnamed x286, local copies, waits for them, and re-layouts  22.2 us
    dot_general x2, matrix products, attend_backward(): jnp.einsum('hqe,hke->hqk', grad_heads, values, preferred_element_type=F32)  13.4 us
    ppermute x17, waiting for transfers between devices, swap_core(): return lax.ppermute(v, LINE, line_perm(lambda x, k: (x, 1 - k)))  13.3 us
  transfers between devices with their start and end apart: 90, of which 53 were waited for; matrix products, arithmetic and copies ran while one was open for 38% of the time, Pallas kernels for 1%

profile of v2, /device:TPU:0, one launch (start us, length us, event | category | flops | bytes accessed | tf_op | source)
XLA Modules:
  0.0 534.0 jit_solution(14600599741044482170)
XLA Ops:
  21.3 5.7 %collective-permute-done.16 = bf16[36,2176]{1,0:T(8,128)(2,1)S(1)} collective-permute-done((bf16[36,2176]{1,0:T(8,128)(2,1)S(1)}, bf16[36,2176]{1,0:T(8,128)(2,1)S(1)}, u32[]{:S(2)}, u32[]{:S(2)}) %collective-permute-start.16) | collective-permute-done | bytes 156704 | tf_op jit(solution)/shard_map/ppermute | solution.py:42
  50.9 6.1 %collective-permute-done.6 = bf16[72,768]{1,0:T(8,128)(2,1)S(1)} collective-permute-done((bf16[72,768]{1,0:T(8,128)(2,1)S(1)}, bf16[72,768]{1,0:T(8,128)(2,1)S(1)}, u32[]{:S(2)}, u32[]{:S(2)}) %collective-permute-start.6) | collective-permute-done | bytes 110624 | tf_op jit(solution)/shard_map/ppermute | solution.py:50
  63.5 7.9 %collective-permute-done.10 = bf16[288,768]{1,0:T(8,128)(2,1)S(1)} collective-permute-done((bf16[288,768]{1,0:T(8,128)(2,1)S(1)}, bf16[288,768]{1,0:T(8,128)(2,1)S(1)}, u32[]{:S(2)}, u32[]{:S(2)}) %collective-permute-start.10) | collective-permute-done | bytes 442400 | tf_op jit(solution)/shard_map/ppermute | solution.py:50
  71.4 16.8 %collective-permute-done.9 = bf16[288,768]{1,0:T(8,128)(2,1)S(1)} collective-permute-done((bf16[288,768]{1,0:T(8,128)(2,1)S(1)}, bf16[288,768]{1,0:T(8,128)(2,1)S(1)}, u32[]{:S(2)}, u32[]{:S(2)}) %collective-permute-start.9) | collective-permute-done | bytes 442400 | tf_op jit(solution)/shard_map/ppermute | solution.py:50
  120.2 7.9 %collective-permute-done.14 = bf16[128,1152]{1,0:T(8,128)(2,1)S(1)} collective-permute-done((bf16[128,1152]{1,0:T(8,128)(2,1)S(1)}, bf16[128,1152]{1,0:T(8,128)(2,1)S(1)}, u32[]{:S(2)}, u32[]{:S(2)}) %collective-permute-start.14) | collective-permute-done | bytes 294944 | tf_op jit(solution)/shard_map/ppermute | solution.py:42
  134.4 9.6 %multiply_convert_fusion.3 = (bf16[256,2176]{1,0:T(8,128)(2,1)S(1)}, f32[256,2176]{1,0:T(8,128)}, f32[256,2176]{1,0:T(8,128)}) fusion(f32[2176]{0:T(1024)S(1)} %get-tuple-element.141, bf16[1152,5120]{1,0:T(8,128)(2,1)} %all-gather.3.cloned.1.call-done, bf16[128,1152]{1,0:T(8,128)(2,1)S(1)} %collective-permute-done.15, ...), kind=kOutput, calls=%fused_computation.94 | convolution fusion | flops 1321402368 | bytes 11182592 | tf_op jit(solution)/shard_map/dot_general | solution.py:117
  155.3 12.5 %collective-permute-done.24 = bf16[128,1152]{1,0:T(8,128)(2,1)S(1)} collective-permute-done((bf16[128,1152]{1,0:T(8,128)(2,1)S(1)}, bf16[128,1152]{1,0:T(8,128)(2,1)S(1)}, u32[]{:S(2)}, u32[]{:S(2)}) %collective-permute-start.24) | collective-permute-done | bytes 294944 | tf_op jit(solution)/shard_map/ppermute | solution.py:42
  202.6 5.7 %collective-permute-done.29 = bf16[128,1152]{1,0:T(8,128)(2,1)S(1)} collective-permute-done((bf16[128,1152]{1,0:T(8,128)(2,1)S(1)}, bf16[128,1152]{1,0:T(8,128)(2,1)S(1)}, u32[]{:S(2)}, u32[]{:S(2)}) %collective-permute-start.29) | collective-permute-done | bytes 294944 | tf_op jit(solution)/shard_map/ppermute | solution.py:42
  213.4 8.5 %multiply_convert_fusion.2 = (bf16[256,2176]{1,0:T(8,128)(2,1)S(1)}, f32[256,2176]{1,0:T(8,128)S(1)}, f32[256,2176]{1,0:T(8,128)S(1)}) fusion(f32[2176]{0:T(1024)S(1)} %get-tuple-element.140, bf16[1152,4352]{1,0:T(8,128)(2,1)} %all-gather.5.cloned.1.call-done, bf16[128,1152]{1,0:T(8,128)(2,1)} %copy-done.61, bf16[128,1152]{1,0:T(8,128)(2,1)} %copy-done.47), kind=kOutput, calls=%fused_computation.81 | convolution fusion | flops 1321402368 | bytes 11182592 | tf_op jit(solution)/shard_map/dot_general | solution.py:117
  223.9 5.8 %hidden_grads.3 = bf16[1152,4352]{1,0:T(8,128)(2,1)} custom-call(bf16[256,1152]{1,0:T(8,128)(2,1)S(1)} %pad_maximum_fusion.9.refs_0_, bf16[256,2176]{1,0:T(8,128)(2,1)S(1)} %get-tuple-element.314.refs_1_, bf16[256,1152]{1,0:T(8,128)(2,1)S(1)} %pad_maximum_fusion.10.refs_2_, bf16[256,2176]{1,0:T(8,128)(2,1)S(1)} %get-tuple-element.171.refs_3_), custom_call_target="tpu_custom_call" | custom-call | flops 2566914048 | bytes 10027008 | tf_op jit(solution)/shard_map/hidden_grads/pallas_call | solution.py:216
  245.3 11.9 %collective-permute-done.39 = bf16[128,1152]{1,0:T(8,128)(2,1)S(1)} collective-permute-done((bf16[128,1152]{1,0:T(8,128)(2,1)S(1)}, bf16[128,1152]{1,0:T(8,128)(2,1)S(1)}, u32[]{:S(2)}, u32[]{:S(2)}) %collective-permute-start.39) | collective-permute-done | bytes 294944 | tf_op jit(solution)/shard_map/ppermute | solution.py:42
  264.1 6.9 %multiply_reduce_fusion.1 = (f32[3,1024]{1,0:T(4,128)S(1)}, f32[3,1024,1024]{1,2,0:T(8,128)S(1)}) fusion(f32[3,1024,1024]{1,2,0:T(8,128)} %copy-done.5, f32[3,1024]{1,0:T(4,128)S(1)} %log_add_fusion.1, bf16[1024,3,3,64]{0,3,2,1:T(8,128)(2,1)} %bitcast.327, bf16[1024,3,64]{0,2,1:T(8,128)(2,1)S(1)} %bitcast.312, bf16[3]{0:T(256)(128)(2,1)S(1)} %get-tuple-element.169), kind=kOutput, calls=%fused_computation.4 | convolution fusion | flops 412283904 | bytes 25976838 | tf_op jit(solution)/shard_map/hqe,hke->hqk/dot_general | solution.py:166
  273.3 5.0 multiply_convert_fusion.1
  278.3 4.8 fusion.93
  298.1 4.3 fusion.20
  319.4 5.4 %collective-permute-done.44 = bf16[128,1152]{1,0:T(8,128)(2,1)} collective-permute-done((bf16[128,1152]{1,0:T(8,128)(2,1)}, bf16[128,1152]{1,0:T(8,128)(2,1)}, u32[]{:S(2)}, u32[]{:S(2)}) %collective-permute-start.44) | collective-permute-done | bytes 294944 | tf_op jit(solution)/shard_map/ppermute | solution.py:42
  333.0 4.3 convert_reduce_fusion.3
  337.3 6.2 %hidden_grads.2 = bf16[1152,5120]{1,0:T(8,128)(2,1)} custom-call(bf16[256,1152]{1,0:T(8,128)(2,1)S(1)} %pad_maximum_fusion.8.refs_0_, bf16[256,2176]{1,0:T(8,128)(2,1)S(1)} %get-tuple-element.316.refs_1_, bf16[256,1152]{1,0:T(8,128)(2,1)S(1)} %pad_maximum_fusion.11.refs_2_, bf16[256,2176]{1,0:T(8,128)(2,1)S(1)} %get-tuple-element.181.refs_3_, ...), custom_call_target="tpu_custom_call" | custom-call | flops 2566914048 | bytes 11796480 | tf_op jit(solution)/shard_map/hidden_grads/pallas_call | solution.py:216
  363.8 12.2 %collective-permute-done.49 = bf16[128,1152]{1,0:T(8,128)(2,1)S(1)} collective-permute-done((bf16[128,1152]{1,0:T(8,128)(2,1)S(1)}, bf16[128,1152]{1,0:T(8,128)(2,1)S(1)}, u32[]{:S(2)}, u32[]{:S(2)}) %collective-permute-start.49) | collective-permute-done | bytes 294944 | tf_op jit(solution)/shard_map/ppermute | solution.py:42
  383.6 6.5 %multiply_reduce_fusion = (f32[3,1024]{1,0:T(4,128)S(1)}, f32[3,1024,1024]{1,2,0:T(8,128)S(1)}) fusion(f32[3,1024,1024]{1,2,0:T(8,128)} %copy-done.4, f32[3,1024]{1,0:T(4,128)S(1)} %copy-done.50, bf16[1024,3,3,64]{0,3,2,1:T(8,128)(2,1)} %bitcast.322, bf16[1024,3,64]{0,2,1:T(8,128)(2,1)S(1)} %bitcast.314, bf16[3]{0:T(256)(128)(2,1)S(1)} %get-tuple-element.169), kind=kOutput, calls=%fused_computation.1 | convolution fusion | flops 412283904 | bytes 25976838 | tf_op jit(solution)/shard_map/hqe,hke->hqk/dot_general | solution.py:166
  392.7 5.0 multiply_convert_fusion
  397.8 5.2 fusion.92
  431.8 6.4 %collective-permute-done.67 = bf16[4,72,384]{2,1,0:T(8,128)(2,1)S(1)} collective-permute-done((bf16[4,72,384]{2,1,0:T(8,128)(2,1)S(1)}, bf16[4,72,384]{2,1,0:T(8,128)(2,1)S(1)}, u32[]{:S(2)}, u32[]{:S(2)}) %collective-permute-start.67) | collective-permute-done | bytes 221216 | tf_op jit(solution)/shard_map/ppermute | solution.py:50
  457.9 5.6 %collective-permute-done.52 = bf16[128,1152]{1,0:T(8,128)(2,1)S(1)} collective-permute-done((bf16[128,1152]{1,0:T(8,128)(2,1)S(1)}, bf16[128,1152]{1,0:T(8,128)(2,1)S(1)}, u32[]{:S(2)}, u32[]{:S(2)}) %collective-permute-start.52) | collective-permute-done | bytes 294944 | tf_op jit(solution)/shard_map/ppermute | solution.py:42
  (737 shorter events, 338.5 us)
Async XLA Ops:
  7.2 127.2 %all-gather.3.cloned.1.call-start = ((), (), s32[]{:S(2)}) async-start(), calls=%async_computation.2 | async-start | bytes 12533760 | tf_op jit(solution)/shard_map/all_gather | solution.py:296
  29.3 183.5 %all-gather.5.cloned.1.call-start = ((), (), s32[]{:S(2)}) async-start(), calls=%async_computation.3 | async-start | bytes 10653696 | tf_op jit(solution)/shard_map/all_gather | solution.py:296
  34.5 28.4 %collective-permute-start.2 = (bf16[128,1152]{1,0:T(8,128)(2,1)S(1)}, bf16[128,1152]{1,0:T(8,128)(2,1)S(1)}, u32[]{:S(2)}, u32[]{:S(2)}) collective-permute-start(bf16[128,1152]{1,0:T(8,128)(2,1)S(1)} %get-tuple-element.188), channel_id=1, source_target_pairs={{0,6},{1,7},{2,4},{3,5},{4,2},{5,3},{6,0},{7,1},{8,14},{9,15},{10,... | collective-permute-start | bytes 884744 | tf_op jit(solution)/shard_map/ppermute | solution.py:42
  36.8 26.1 %collective-permute-start.1 = (bf16[128,1152]{1,0:T(8,128)(2,1)S(1)}, bf16[128,1152]{1,0:T(8,128)(2,1)S(1)}, u32[]{:S(2)}, u32[]{:S(2)}) collective-permute-start(bf16[128,1152]{1,0:T(8,128)(2,1)S(1)} %get-tuple-element.188), channel_id=1, source_target_pairs={{0,2},{1,3},{2,0},{3,1},{4,6},{5,7},{6,4},{7,5},{8,10},{9,11},{10,... | collective-permute-start | bytes 884744 | tf_op jit(solution)/shard_map/ppermute | solution.py:42
  59.3 28.9 %collective-permute-start.9 = (bf16[288,768]{1,0:T(8,128)(2,1)S(1)}, bf16[288,768]{1,0:T(8,128)(2,1)S(1)}, u32[]{:S(2)}, u32[]{:S(2)}) collective-permute-start(bf16[288,768]{1,0:T(8,128)(2,1)S(1)} %pad_maximum_fusion.12), channel_id=1, source_target_pairs={{0,64},{8,72},{16,80},{24,88},{32,96},{40,104},{48,112},{56,120},{... | collective-permute-start | bytes 1327112 | tf_op jit(solution)/shard_map/ppermute | solution.py:50
  62.9 25.3 %collective-permute-start.8 = (bf16[288,768]{1,0:T(8,128)(2,1)S(1)}, bf16[288,768]{1,0:T(8,128)(2,1)S(1)}, u32[]{:S(2)}, u32[]{:S(2)}) collective-permute-start(bf16[288,768]{1,0:T(8,128)(2,1)S(1)} %pad_maximum_fusion.12), channel_id=1, source_target_pairs={{0,96},{8,104},{16,112},{24,120},{32,64},{40,72},{48,80},{56,88},{... | collective-permute-start | bytes 1327112 | tf_op jit(solution)/shard_map/ppermute | solution.py:50
  63.0 26.0 %collective-permute-start.3 = (bf16[512,1152]{1,0:T(8,128)(2,1)S(1)}, bf16[512,1152]{1,0:T(8,128)(2,1)S(1)}, u32[]{:S(2)}, u32[]{:S(2)}) collective-permute-start(bf16[512,1152]{1,0:T(8,128)(2,1)S(1)} %pad_maximum_fusion.3), channel_id=1, source_target_pairs={{0,1},{1,0},{2,3},{3,2},{4,5},{5,4},{6,7},{7,6},{8,9},{9,8},{10,11... | collective-permute-start | bytes 3538952 | tf_op jit(solution)/shard_map/ppermute | solution.py:38
  89.3 16.0 %collective-permute-start.32 = (bf16[36,2176]{1,0:T(8,128)(2,1)S(1)}, bf16[36,2176]{1,0:T(8,128)(2,1)S(1)}, u32[]{:S(2)}, u32[]{:S(2)}) collective-permute-start(bf16[36,2176]{1,0:T(8,128)(2,1)S(1)} %fusion.158), channel_id=1, source_target_pairs={{0,2},{1,3},{2,0},{3,1},{4,6},{5,7},{6,4},{7,5},{8,10},{9,11},{10,... | collective-permute-start | bytes 470024 | tf_op jit(solution)/shard_map/ppermute | solution.py:42
  107.9 393.6 %reduce-scatter.10.cloned.1.call-start = ((), (), s32[]{:S(2)}) async-start(), calls=%async_computation.5 | async-start | bytes 10653696
  111.4 16.7 %collective-permute-start.14 = (bf16[128,1152]{1,0:T(8,128)(2,1)S(1)}, bf16[128,1152]{1,0:T(8,128)(2,1)S(1)}, u32[]{:S(2)}, u32[]{:S(2)}) collective-permute-start(bf16[128,1152]{1,0:T(8,128)(2,1)S(1)} %get-tuple-element.204), channel_id=1, source_target_pairs={{0,6},{1,7},{2,4},{3,5},{4,2},{5,3},{6,0},{7,1},{8,14},{9,15},{10,... | collective-permute-start | bytes 884744 | tf_op jit(solution)/shard_map/ppermute | solution.py:42
  151.2 16.6 %collective-permute-start.24 = (bf16[128,1152]{1,0:T(8,128)(2,1)S(1)}, bf16[128,1152]{1,0:T(8,128)(2,1)S(1)}, u32[]{:S(2)}, u32[]{:S(2)}) collective-permute-start(bf16[128,1152]{1,0:T(8,128)(2,1)S(1)} %get-tuple-element.178), channel_id=1, source_target_pairs={{0,6},{1,7},{2,4},{3,5},{4,2},{5,3},{6,0},{7,1},{8,14},{9,15},{10,... | collective-permute-start | bytes 884744 | tf_op jit(solution)/shard_map/ppermute | solution.py:42
  193.5 14.8 %collective-permute-start.29 = (bf16[128,1152]{1,0:T(8,128)(2,1)S(1)}, bf16[128,1152]{1,0:T(8,128)(2,1)S(1)}, u32[]{:S(2)}, u32[]{:S(2)}) collective-permute-start(bf16[128,1152]{1,0:T(8,128)(2,1)S(1)} %get-tuple-element.201), channel_id=1, source_target_pairs={{0,6},{1,7},{2,4},{3,5},{4,2},{5,3},{6,0},{7,1},{8,14},{9,15},{10,... | collective-permute-start | bytes 884744 | tf_op jit(solution)/shard_map/ppermute | solution.py:42
  195.4 14.7 %collective-permute-start.28 = (bf16[128,1152]{1,0:T(8,128)(2,1)S(1)}, bf16[128,1152]{1,0:T(8,128)(2,1)S(1)}, u32[]{:S(2)}, u32[]{:S(2)}) collective-permute-start(bf16[128,1152]{1,0:T(8,128)(2,1)S(1)} %get-tuple-element.202), channel_id=1, source_target_pairs={{0,2},{1,3},{2,0},{3,1},{4,6},{5,7},{6,4},{7,5},{8,10},{9,11},{10,... | collective-permute-start | bytes 884744 | tf_op jit(solution)/shard_map/ppermute | solution.py:42
  230.8 281.3 %reduce-scatter.8.cloned.1.call-start = ((), (), s32[]{:S(2)}) async-start(), calls=%async_computation.4 | async-start | bytes 12533760
  240.6 16.6 %collective-permute-start.39 = (bf16[128,1152]{1,0:T(8,128)(2,1)S(1)}, bf16[128,1152]{1,0:T(8,128)(2,1)S(1)}, u32[]{:S(2)}, u32[]{:S(2)}) collective-permute-start(bf16[128,1152]{1,0:T(8,128)(2,1)S(1)} %get-tuple-element.151), channel_id=1, source_target_pairs={{0,6},{1,7},{2,4},{3,5},{4,2},{5,3},{6,0},{7,1},{8,14},{9,15},{10,... | collective-permute-start | bytes 884744 | tf_op jit(solution)/shard_map/ppermute | solution.py:42
  242.6 15.2 %collective-permute-start.37 = (bf16[128,1152]{1,0:T(8,128)(2,1)S(1)}, bf16[128,1152]{1,0:T(8,128)(2,1)S(1)}, u32[]{:S(2)}, u32[]{:S(2)}) collective-permute-start(bf16[128,1152]{1,0:T(8,128)(2,1)S(1)} %get-tuple-element.151), channel_id=1, source_target_pairs={{0,4},{1,5},{2,6},{3,7},{4,0},{5,1},{6,2},{7,3},{8,12},{9,13},{10,... | collective-permute-start | bytes 884744 | tf_op jit(solution)/shard_map/ppermute | solution.py:42
  303.2 45.0 %collective-permute-start.34 = (bf16[128,1152]{1,0:T(8,128)(2,1)}, bf16[128,1152]{1,0:T(8,128)(2,1)}, u32[]{:S(2)}, u32[]{:S(2)}) collective-permute-start(bf16[128,1152]{1,0:T(8,128)(2,1)} %slice.1033), channel_id=1, source_target_pairs={{0,1},{1,0},{2,3},{3,2},{4,5},{5,4},{6,7},{7,6},{8,9},{9,8},{10,11... | collective-permute-start | bytes 884744 | tf_op jit(solution)/shard_map/ppermute | solution.py:38
  309.4 15.4 %collective-permute-start.44 = (bf16[128,1152]{1,0:T(8,128)(2,1)}, bf16[128,1152]{1,0:T(8,128)(2,1)}, u32[]{:S(2)}, u32[]{:S(2)}) collective-permute-start(bf16[128,1152]{1,0:T(8,128)(2,1)} %get-tuple-element.198), channel_id=1, source_target_pairs={{0,6},{1,7},{2,4},{3,5},{4,2},{5,3},{6,0},{7,1},{8,14},{9,15},{10,... | collective-permute-start | bytes 884744 | tf_op jit(solution)/shard_map/ppermute | solution.py:42
  311.6 14.9 %collective-permute-start.43 = (bf16[128,1152]{1,0:T(8,128)(2,1)}, bf16[128,1152]{1,0:T(8,128)(2,1)}, u32[]{:S(2)}, u32[]{:S(2)}) collective-permute-start(bf16[128,1152]{1,0:T(8,128)(2,1)} %get-tuple-element.199), channel_id=1, source_target_pairs={{0,2},{1,3},{2,0},{3,1},{4,6},{5,7},{6,4},{7,5},{8,10},{9,11},{10,... | collective-permute-start | bytes 884744 | tf_op jit(solution)/shard_map/ppermute | solution.py:42
  359.5 16.5 %collective-permute-start.49 = (bf16[128,1152]{1,0:T(8,128)(2,1)S(1)}, bf16[128,1152]{1,0:T(8,128)(2,1)S(1)}, u32[]{:S(2)}, u32[]{:S(2)}) collective-permute-start(bf16[128,1152]{1,0:T(8,128)(2,1)S(1)} %get-tuple-element.157), channel_id=1, source_target_pairs={{0,6},{1,7},{2,4},{3,5},{4,2},{5,3},{6,0},{7,1},{8,14},{9,15},{10,... | collective-permute-start | bytes 884744 | tf_op jit(solution)/shard_map/ppermute | solution.py:42
  418.7 19.5 %collective-permute-start.67 = (bf16[4,72,384]{2,1,0:T(8,128)(2,1)S(1)}, bf16[4,72,384]{2,1,0:T(8,128)(2,1)S(1)}, u32[]{:S(2)}, u32[]{:S(2)}) collective-permute-start(bf16[4,72,384]{2,1,0:T(8,128)(2,1)S(1)} %get-tuple-element.207), channel_id=1, source_target_pairs={{0,16},{8,24},{16,0},{24,8},{32,48},{40,56},{48,32},{56,40},{64,80... | collective-permute-start | bytes 663560 | tf_op jit(solution)/shard_map/ppermute | solution.py:50
  419.6 19.6 %collective-permute-start.68 = (bf16[4,72,384]{2,1,0:T(8,128)(2,1)S(1)}, bf16[4,72,384]{2,1,0:T(8,128)(2,1)S(1)}, u32[]{:S(2)}, u32[]{:S(2)}) collective-permute-start(bf16[4,72,384]{2,1,0:T(8,128)(2,1)S(1)} %get-tuple-element.208), channel_id=1, source_target_pairs={{0,24},{8,16},{16,8},{24,0},{32,56},{40,48},{48,40},{56,32},{64,88... | collective-permute-start | bytes 663560 | tf_op jit(solution)/shard_map/ppermute | solution.py:50
  426.4 15.4 %collective-permute-start.74 = (bf16[4,72,384]{2,1,0:T(8,128)(2,1)S(1)}, bf16[4,72,384]{2,1,0:T(8,128)(2,1)S(1)}, u32[]{:S(2)}, u32[]{:S(2)}) collective-permute-start(bf16[4,72,384]{2,1,0:T(8,128)(2,1)S(1)} %get-tuple-element.210), channel_id=1, source_target_pairs={{0,96},{8,104},{16,112},{24,120},{32,64},{40,72},{48,80},{56,88},{... | collective-permute-start | bytes 663560 | tf_op jit(solution)/shard_map/ppermute | solution.py:50
  438.3 14.8 %collective-permute-start.51 = (bf16[512,1152]{1,0:T(8,128)(2,1)S(1)}, bf16[512,1152]{1,0:T(8,128)(2,1)S(1)}, u32[]{:S(2)}, u32[]{:S(2)}) collective-permute-start(bf16[512,1152]{1,0:T(8,128)(2,1)S(1)} %slice.1027), channel_id=1, source_target_pairs={{0,1},{1,0},{2,3},{3,2},{4,5},{5,4},{6,7},{7,6},{8,9},{9,8},{10,11... | collective-permute-start | bytes 3538952 | tf_op jit(solution)/shard_map/ppermute | solution.py:38
  (195 other events, 1963.1 us)
Sparse Core Ops, SparseCore 0:
  29.4 100.5 all-gather.2
  132.2 75.9 all-gather.4
  230.9 87.4 reduce-scatter.9
  343.6 99.1 reduce-scatter.7

commit v3 on v2

--- a/solution.py
+++ b/solution.py
@@ -50,35 +50,14 @@
     return lax.ppermute(v, "shard", [(i, i ^ m) for i in range(SHARDS)])
 
 
-def ordered(parts, place):
-    odd, high = place % 2 == 1, place // 2 == 1
-    parts = [jnp.where(odd, parts[i ^ 1], parts[i]) for i in range(4)]
-    return jnp.concatenate([jnp.where(high, parts[i ^ 2], parts[i]) for i in range(4)], axis=0)
-
-
 def gather_shards(v):
-    shard = lax.axis_index("shard")
-    v = ordered([v] + [swap_shard(v, m) for m in (1, 2, 3)], shard % 4)
-    return ordered([v] + [swap_shard(v, 4 * m) for m in (1, 2, 3)], shard // 4)
+    copies = jnp.broadcast_to(v, (SHARDS, *v.shape))
+    return lax.all_to_all(copies, "shard", 0, 0, tiled=True).reshape(-1, v.shape[1])
 
 
 def to_shards(v):
-    shard = lax.axis_index("shard")
-
-    def stage(v, axis, step):
-        place = shard // step % 4
-
-        def part(m):
-            return lax.dynamic_index_in_dim(v, place ^ m, axis, keepdims=False)
-
-        came = [swap_shard(part(m).astype(BF), m * step).astype(F32) for m in (1, 2, 3)]
-        return (part(0).astype(F32) + came[0]) + (came[1] + came[2])
-
-    v = v.reshape(4, 4, v.shape[0] // SHARDS, v.shape[1])
-    half = v.shape[3] // 2
-    a = stage(stage(v[..., :half], 1, 1), 0, 4)
-    b = stage(stage(v[..., half:], 0, 4), 0, 1)
-    return jnp.concatenate([a, b], axis=1)
+    v = v.reshape(SHARDS, v.shape[0] // SHARDS, v.shape[1])
+    return lax.all_to_all(v, "shard", 0, 0, tiled=True)
 
 
 def gather_pair(piece):
@@ -91,16 +70,14 @@
 
 def gather_rows(piece):
     mine = jnp.concatenate([piece] + [swap_x(piece, m) for m in (1, 2, 3)], axis=0)
-    return jnp.concatenate([mine, swap_core(mine)], axis=0)
-
-
-def sum_rows(partial):
-    half = 4 * ROWS
-    arrived = swap_core(partial[half:].astype(BF))
-    chip = partial[:half] + arrived.astype(F32)
-    low = chip.astype(BF)
-    parts = [swap_x(low[m * ROWS : (m + 1) * ROWS], m).astype(F32) for m in (1, 2, 3)]
-    return (chip[:ROWS] + parts[0]) + (parts[1] + parts[2])
+    return mine, swap_core(mine)
+
+
+def sum_rows(rows, w, lo, hi):
+    arrived = swap_core(dot(rows[HALF:], w[:, lo:hi], ((1,), (1,))).astype(BF))
+    own, *others = chip_sum(rows, w, arrived, lo, hi)
+    parts = [swap_x(v, m).astype(F32) for m, v in zip((1, 2, 3), others)]
+    return (own + parts[0]) + (parts[1] + parts[2])
 
 
 def sum_shards(v):
@@ -138,42 +115,125 @@
     return jax.nn.gelu(v, approximate=False)
 
 
-def split_heads(v):
-    parts = v.shape[1] // QW
-    v = v.reshape(v.shape[0], HEADS_HERE, parts, HD)
-    return [jnp.moveaxis(v[:, :, i], 1, 0) for i in range(parts)]
-
-
-def join_heads(*parts):
-    v = jnp.stack(parts, axis=2)
-    return jnp.moveaxis(v, 0, 1).reshape(v.shape[1], -1)
-
-
-def attend_forward(queries, keys, values, allowed, live):
-    scores = jnp.einsum("hqe,hke->hqk", queries, keys, preferred_element_type=F32) * HD**-0.5
-    masked = jnp.where(allowed, scores, -1e30)
-    highest = jnp.max(masked, axis=-1, keepdims=True)
-    exponent = jnp.exp(masked - highest)
-    totals = jnp.sum(exponent, axis=-1, keepdims=True)
-    probs = (exponent / totals).astype(BF)
-    heads = jnp.einsum("hqk,hke->hqe", probs, values, preferred_element_type=F32)
-    return (heads * live[:, None, None]).astype(BF), highest + jnp.log(totals)
-
-
-def attend_backward(queries, keys, values, log_total, grad_heads, allowed):
-    scores = jnp.einsum("hqe,hke->hqk", queries, keys, preferred_element_type=F32) * HD**-0.5
-    probs = jnp.exp(jnp.where(allowed, scores, -1e30) - log_total)
-    grad_probs = jnp.einsum("hqe,hke->hqk", grad_heads, values, preferred_element_type=F32)
-    centred = grad_probs - jnp.sum(grad_probs * probs, axis=-1, keepdims=True)
-    grad_scores = (probs * centred).astype(BF)
-    grad_q = jnp.einsum("hqk,hke->hqe", grad_scores, keys, preferred_element_type=F32)
-    grad_k = jnp.einsum("hqk,hqe->hke", grad_scores, queries, preferred_element_type=F32)
-    grad_v = jnp.einsum("hqk,hqe->hke", probs.astype(BF), grad_heads, preferred_element_type=F32)
-    return (
-        (grad_q * HD**-0.5).astype(BF),
-        (grad_k * HD**-0.5).astype(BF),
-        grad_v.astype(BF),
-    )
+LINE_ROWS = 8 * ROWS
+Q_ROWS = 256
+PLAIN = (((1,), (0,)), ((), ()))
+TURN_RIGHT = (((1,), (1,)), ((), ()))
+TURN_LEFT = (((0,), (0,)), ((), ()))
+
+
+def mul(a, b, dims):
+    return lax.dot_general(a, b, dims, preferred_element_type=F32)
+
+
+def head_parts(ref, rows, j):
+    at = 3 * HD * j
+    return [ref[rows, at + i * HD : at + (i + 1) * HD] for i in range(3)]
+
+
+def attend_body(live_ref, kp_ref, qp_ref, qkv_ref, out_ref, lse_ref):
+    mine = pl.ds(pl.multiple_of(pl.program_id(0) * Q_ROWS, Q_ROWS), Q_ROWS)
+    allowed = kp_ref[...] <= qp_ref[...]
+    for j in range(HEADS_HERE):
+        queries = qkv_ref[mine, 3 * HD * j : 3 * HD * j + HD]
+        _, keys, values = head_parts(qkv_ref, slice(None), j)
+        scores = jnp.where(allowed, mul(keys, queries, TURN_RIGHT) * HD**-0.5, -1e30)
+        highest = jnp.max(scores, axis=0, keepdims=True)
+        exponent = jnp.exp(scores - highest)
+        totals = jnp.sum(exponent, axis=0, keepdims=True)
+        probs = (exponent * (1.0 / totals)).astype(BF)
+        heads = mul(values, probs, TURN_LEFT) * live_ref[j]
+        out_ref[:, j * HD : (j + 1) * HD] = heads.T.astype(BF)
+        lse_ref[j : j + 1, :] = highest + jnp.log(totals)
+    lse_ref[HEADS_HERE:, :] = jnp.zeros((8 - HEADS_HERE, Q_ROWS), F32)
+
+
+def attend_back_body(
+    live_ref, kp_ref, qp_ref, lse_ref, dout_ref, qkv_ref, out_ref, key_sum, value_sum
+):
+    step = pl.program_id(0)
+    mine = pl.ds(pl.multiple_of(step * Q_ROWS, Q_ROWS), Q_ROWS)
+    allowed = kp_ref[...] <= qp_ref[...]
+
+    @pl.when(step == 0)
+    def _():
+        key_sum[...] = jnp.zeros_like(key_sum)
+        value_sum[...] = jnp.zeros_like(value_sum)
+
+    for j in range(HEADS_HERE):
+        queries = qkv_ref[mine, 3 * HD * j : 3 * HD * j + HD]
+        _, keys, values = head_parts(qkv_ref, slice(None), j)
+        dout = dout_ref[:, j * HD : (j + 1) * HD] * live_ref[j].astype(BF)
+        scores = jnp.where(allowed, mul(keys, queries, TURN_RIGHT) * HD**-0.5, -1e30)
+        probs = jnp.exp(scores - lse_ref[j : j + 1, :])
+        dprobs = mul(values, dout, TURN_RIGHT)
+        dscores = probs * (dprobs - jnp.sum(dprobs * probs, axis=0, keepdims=True))
+        dscores = dscores.astype(BF)
+        value_sum[j] += mul(probs.astype(BF), dout, PLAIN)
+        key_sum[j] += mul(dscores, queries, PLAIN)
+        dqueries = mul(keys, dscores, TURN_LEFT) * HD**-0.5
+        out_ref[mine, 3 * HD * j : 3 * HD * j + HD] = dqueries.T.astype(BF)
+
+    @pl.when(step == LINE_ROWS // Q_ROWS - 1)
+    def _():
+        for j in range(HEADS_HERE):
+            at = 3 * HD * j
+            out_ref[:, at + HD : at + 2 * HD] = (key_sum[j] * HD**-0.5).astype(BF)
+            out_ref[:, at + 2 * HD : at + 3 * HD] = value_sum[j].astype(BF)
+
+
+def attend_specs():
+    return [
+        pl.BlockSpec(memory_space=pltpu.SMEM),
+        pl.BlockSpec((LINE_ROWS, 1), lambda i: (0, 0)),
+        pl.BlockSpec((1, Q_ROWS), lambda i: (0, i)),
+    ]
+
+
+def attend_forward(live, places, qkv):
+    return pl.pallas_call(
+        attend_body,
+        grid=(LINE_ROWS // Q_ROWS,),
+        in_specs=attend_specs() + [pl.BlockSpec((LINE_ROWS, 3 * QW), lambda i: (0, 0))],
+        out_specs=[
+            pl.BlockSpec((Q_ROWS, QW), lambda i: (i, 0)),
+            pl.BlockSpec((8, Q_ROWS), lambda i: (0, i)),
+        ],
+        out_shape=[
+            jax.ShapeDtypeStruct((LINE_ROWS, QW), BF),
+            jax.ShapeDtypeStruct((8, LINE_ROWS), F32),
+        ],
+        compiler_params=pltpu.CompilerParams(vmem_limit_bytes=48 << 20),
+        cost_estimate=pl.CostEstimate(
+            flops=4 * HEADS_HERE * LINE_ROWS * LINE_ROWS * HD * 4,
+            bytes_accessed=LINE_ROWS * 4 * QW * 2,
+            transcendentals=HEADS_HERE * LINE_ROWS * LINE_ROWS,
+        ),
+        name="attend",
+    )(live, places[:, None], places[None, :], qkv)
+
+
+def attend_backward(live, places, lse, dout, qkv):
+    return pl.pallas_call(
+        attend_back_body,
+        grid=(LINE_ROWS // Q_ROWS,),
+        in_specs=attend_specs()
+        + [
+            pl.BlockSpec((8, Q_ROWS), lambda i: (0, i)),
+            pl.BlockSpec((Q_ROWS, QW), lambda i: (i, 0)),
+            pl.BlockSpec((LINE_ROWS, 3 * QW), lambda i: (0, 0)),
+        ],
+        out_specs=pl.BlockSpec((LINE_ROWS, 3 * QW), lambda i: (0, 0)),
+        out_shape=jax.ShapeDtypeStruct((LINE_ROWS, 3 * QW), BF),
+        scratch_shapes=[pltpu.VMEM((HEADS_HERE, LINE_ROWS, HD), F32)] * 2,
+        compiler_params=pltpu.CompilerParams(vmem_limit_bytes=48 << 20),
+        cost_estimate=pl.CostEstimate(
+            flops=10 * HEADS_HERE * LINE_ROWS * LINE_ROWS * HD * 4,
+            bytes_accessed=LINE_ROWS * 7 * QW * 2,
+            transcendentals=HEADS_HERE * LINE_ROWS * LINE_ROWS,
+        ),
+        name="attend_back",
+    )(live, places[:, None], places[None, :], lse, dout, qkv)
 
 
 def head_halves(w_qkv, w_out):
@@ -188,7 +248,79 @@
     )
 
 
+HALF = 4 * ROWS
 GRAD_ROWS = 384
+
+
+def project(pair, w, lo, hi, bias):
+    def body(mine, other, w_ref, bias_ref, out_ref):
+        for at, x in ((0, mine), (HALF, other)):
+            got = mul(x[...], w_ref[:, lo:hi], PLAIN) + bias_ref[...]
+            out_ref[at : at + HALF, :] = got.astype(BF)
+
+    return pl.pallas_call(
+        body,
+        out_shape=jax.ShapeDtypeStruct((2 * HALF, hi - lo), BF),
+        compiler_params=pltpu.CompilerParams(vmem_limit_bytes=48 << 20),
+        cost_estimate=pl.CostEstimate(
+            flops=4 * HALF * DP * (hi - lo), bytes_accessed=8 << 20, transcendentals=0
+        ),
+        name="project",
+    )(*pair, w, bias.reshape(1, hi - lo))
+
+
+def chip_sum(rows, w, arrived, lo, hi):
+    def body(rows_ref, w_ref, arrived_ref, *outs):
+        w_part = w_ref[:, lo:hi]
+        for m, out in enumerate(outs):
+            block = slice(m * ROWS, (m + 1) * ROWS)
+            got = mul(rows_ref[block, :], w_part, TURN_RIGHT) + arrived_ref[block, :].astype(F32)
+            out[...] = got.astype(out.dtype)
+
+    return pl.pallas_call(
+        body,
+        grid=(1,),
+        in_specs=[
+            pl.BlockSpec((HALF, hi - lo), lambda i: (0, 0)),
+            pl.BlockSpec((DP, HW), lambda i: (0, 0)),
+            pl.BlockSpec((HALF, DP), lambda i: (0, 0)),
+        ],
+        out_specs=[pl.BlockSpec((ROWS, DP), lambda i: (0, 0))] * 4,
+        out_shape=[jax.ShapeDtypeStruct((ROWS, DP), F32 if m == 0 else BF) for m in range(4)],
+        compiler_params=pltpu.CompilerParams(vmem_limit_bytes=48 << 20),
+        cost_estimate=pl.CostEstimate(
+            flops=2 * HALF * DP * (hi - lo), bytes_accessed=6 << 20, transcendentals=0
+        ),
+        name="chip_sum",
+    )(rows, w, arrived)
+
+
+def head_grads_of(pair, dqkv, m_pair, attended):
+    def body(x0, x1, m0, m1, dqkv_ref, att_ref, out_ref):
+        got = mul(x0[...], dqkv_ref[:HALF, :], TURN_LEFT)
+        got += mul(x1[...], dqkv_ref[HALF:, :], TURN_LEFT)
+        out_ref[:, : 3 * QW] = got.astype(BF)
+        got = mul(m0[...], att_ref[:HALF, :], TURN_LEFT)
+        got += mul(m1[...], att_ref[HALF:, :], TURN_LEFT)
+        out_ref[:, 3 * QW :] = got.astype(BF)
+
+    feature = pl.BlockSpec((HALF, GRAD_ROWS), lambda i: (0, i))
+    return pl.pallas_call(
+        body,
+        grid=(DP // GRAD_ROWS,),
+        in_specs=[feature] * 4
+        + [
+            pl.BlockSpec((2 * HALF, 3 * QW), lambda i: (0, 0)),
+            pl.BlockSpec((2 * HALF, QW), lambda i: (0, 0)),
+        ],
+        out_specs=pl.BlockSpec((GRAD_ROWS, HW), lambda i: (i, 0)),
+        out_shape=jax.ShapeDtypeStruct((DP, HW), BF),
+        compiler_params=pltpu.CompilerParams(vmem_limit_bytes=48 << 20),
+        cost_estimate=pl.CostEstimate(
+            flops=4 * HALF * DP * HW, bytes_accessed=8 << 20, transcendentals=0
+        ),
+        name="head_grads",
+    )(*pair, *m_pair, dqkv, attended)
 
 
 def hidden_grads_body(heads, x_ref, dinner_ref, g_ref, act_ref, *refs):
@@ -297,14 +429,13 @@
 
     halves_a = head_halves(w_qkv[0, 0], w_out[0, 0])
     pack_a = exchanged(halves_a)
-    w_fc_a, w_down_a, w_qkv_b, w_out_b, pack_a = lax.optimization_barrier(
-        (w_fc[0], w_down[0], w_qkv[1, 0], w_out[1, 0], pack_a)
-    )
-    hidden_a = exchanged_hidden(w_fc_a, w_down_a)
+    w_qkv_b, w_out_b, pack_a = lax.optimization_barrier((w_qkv[1, 0], w_out[1, 0], pack_a))
+    hidden_a = exchanged_hidden(w_fc[0], w_down[0])
     heads_b = exchanged(head_halves(w_qkv_b, w_out_b))
+    heads_a, tokens = lax.optimization_barrier((gather_shards(pack_a), tokens))
     fetched_a = fetch(jnp.concatenate([hidden_a, heads_b], axis=1))
     weights = [
-        (gather_shards(pack_a), fetched_a[:, : 2 * FC]),
+        (heads_a, fetched_a[:, : 2 * FC]),
         (fetched_a[:, 2 * FC :], None),
     ]
 
@@ -318,7 +449,6 @@
             start = jnp.sum(jnp.where(jnp.arange(4) == block, block_order, 0)) * 256
             units.append(start + (core ^ j) * ROWS + jnp.arange(ROWS, dtype=jnp.int32))
     places = jnp.concatenate(units)
-    allowed = places[None, :] <= places[:, None]
     my_count = jnp.sum(jnp.where(jnp.arange(4) == tp, head_count, 0))
     slot = jnp.arange(HEADS_HERE, dtype=jnp.int32) + ctx * HEADS_HERE
     live = ((slot < my_count) & (slot < 5)).astype(F32)
@@ -349,12 +479,9 @@
                 (normed_all, w_fc[1], w_down[1])
             )
             weights[1] = (weights[1][0], fetch(exchanged_hidden(w_fc_b, w_down_b)))
-        projected = dot(normed_all, w_heads[:, : 3 * QW], ((1,), (0,)))
-        queries, keys, values = split_heads((projected + head_bias[l]).astype(BF))
-        attended, log_total = attend_forward(queries, keys, values, allowed, live)
-        attended = join_heads(attended)
-        mixed_out = dot(attended, w_heads[:, 3 * QW :], ((1,), (1,)))
-        middle = hidden + (sum_rows(mixed_out) + out_bias[l])
+        qkv = project(normed_all, w_heads, 0, 3 * QW, head_bias[l])
+        attended, log_total = attend_forward(live, places, qkv)
+        middle = hidden + (sum_rows(attended, w_heads, 3 * QW, HW) + out_bias[l])
         normed_two, xhat_two, rstd_two = norm_forward(middle, gains[l, 1], shifts[l, 1], mask)
         normed_two_all = gather_pair(normed_two)
         inner = dot(normed_two_all, w_hidden[:, :FC], ((1,), (0,))) + fc_bias[l]
@@ -366,9 +493,7 @@
                 normed_all,
                 xhat,
                 rstd,
-                queries,
-                keys,
-                values,
+                qkv,
                 log_total,
                 attended,
                 normed_two_all,
@@ -385,6 +510,18 @@
     high = tp // 2 == 1
     hidden_sums = [None] * LAYERS
 
+    def own_hidden(v):
+        mine = jnp.where(first, v[:WIDE], v[WIDE:])
+        theirs = jnp.where(first, v[WIDE:], v[:WIDE])
+
+        def piece(rows, h):
+            return jnp.concatenate(
+                [rows[:, h * FR : (h + 1) * FR], rows[:, FC + h * FR : FC + (h + 1) * FR]], axis=1
+            )
+
+        came = [swap_x(piece(theirs if m % 2 else mine, m // 2), m).astype(F32) for m in (1, 2, 3)]
+        return ((piece(mine, 0).astype(F32) + came[0]) + (came[1] + came[2]))[:CHUNK]
+
     def to_owner(v, dim):
         v = v.reshape((1,) * dim + v.shape)
         v = lax.psum_scatter(v, "shard", scatter_dimension=dim, tiled=True)
@@ -396,9 +533,7 @@
             normed_all,
             xhat,
             rstd,
-            queries,
-            keys,
-            values,
+            qkv,
             log_total,
             attended,
             normed_two_all,
@@ -425,17 +560,14 @@
         m_low = grad_middle.astype(BF)
         m_all = gather_rows(m_low)
         grad_out_b = jnp.sum(m_low.astype(F32), axis=0)
-        grad_out_w = dot(m_all, attended, ((0,), (0,))).astype(BF)
-        (grad_heads,) = split_heads(dot(m_all, w_heads[:, 3 * QW :], ((1,), (0,))).astype(BF))
-        grad_heads = grad_heads * live[:, None, None].astype(BF)
-        grad_q, grad_k, grad_v = attend_backward(
-            queries, keys, values, log_total, grad_heads, allowed
-        )
-        grad_qkv = join_heads(grad_q, grad_k, grad_v)
-        grad_qkv_w = dot(normed_all, grad_qkv, ((0,), (0,))).astype(BF)
-        head_grads = jnp.concatenate([grad_qkv_w, grad_out_w], axis=1)
+        grad_heads = project(m_all, w_heads, 3 * QW, HW, jnp.zeros((QW,), F32))
+        grad_qkv = attend_backward(live, places, log_total, grad_heads, qkv)
+        if l == 0:
+            hidden_own = [None, own_hidden(hidden_sums[1])]
+            grad_qkv, hidden_own[1] = lax.optimization_barrier((grad_qkv, hidden_own[1]))
+        head_grads = head_grads_of(normed_all, grad_qkv, m_all, attended)
         qkv_b = jnp.sum(grad_qkv.astype(F32), axis=0)
-        grad_one = sum_rows(dot(grad_qkv, w_heads[:, : 3 * QW], ((1,), (1,))))
+        grad_one = sum_rows(grad_qkv, w_heads, 0, 3 * QW)
         dx, gain_one, shift_one = norm_backward(grad_one, xhat, rstd, gains[l, 0], mask)
         gradient = grad_middle + dx
         small[l] = [gain_one, gain_two, shift_one, shift_two, grad_out_b, grad_down_b]
@@ -447,6 +579,10 @@
     line = sum_line_parts(
         jnp.stack(small[0] + small[1]),
         jnp.pad(jnp.stack(fc_biases[::-1]), ((0, 0), (0, 2 * DP - FC))).reshape(4, DP),
+    )
+    head_sum_a = to_shards(head_grads)
+    line, head_sum_a, hidden_sums[0] = lax.optimization_barrier(
+        (line, head_sum_a, hidden_sums[0])
     )
     own = jnp.pad(jnp.stack(head_biases[::-1]), ((0, 0), (0, DP - 3 * QW)))
     other = swap_ctx(own)
@@ -467,19 +603,8 @@
             jnp.where(first, recv, keep)[:CHUNK].astype(F32),
         )
 
-    def own_hidden(v):
-        mine = jnp.where(first, v[:WIDE], v[WIDE:])
-        theirs = jnp.where(first, v[WIDE:], v[:WIDE])
-
-        def piece(rows, h):
-            return jnp.concatenate(
-                [rows[:, h * FR : (h + 1) * FR], rows[:, FC + h * FR : FC + (h + 1) * FR]], axis=1
-            )
-
-        came = [swap_x(piece(theirs if m % 2 else mine, m // 2), m).astype(F32) for m in (1, 2, 3)]
-        return ((piece(mine, 0).astype(F32) + came[0]) + (came[1] + came[2]))[:CHUNK]
-
-    head_sums = [to_shards(head_grads).astype(BF), hidden_sums[0][:, 2 * FC :]]
+    head_sums = [jnp.sum(head_sum_a.astype(F32), axis=0).astype(BF), hidden_sums[0][:, 2 * FC :]]
+    hidden_own[0] = own_hidden(hidden_sums[0][:, : 2 * FC])
     grads = [[], [], [], []]
     for l in range(LAYERS):
         a, b = own_features(head_sums[l])
@@ -487,7 +612,7 @@
         grads[0].append(jnp.moveaxis(qkv, 1, 0))
         outs = jnp.concatenate([a[:, 3 * QW :], b[:, 3 * QW : 3 * QW + 2 * HD]], axis=1)
         grads[1].append(outs.T.reshape(5, HD, CHUNK))
-        both = own_hidden(hidden_sums[l][:, : 2 * FC])
+        both = hidden_own[l]
         grads[2].append(both[:, :FR])
         grads[3].append(both[:, FR:].T)
 

time: 544 us -> 509 us (0.936)
  Pallas kernels: 12 us -> 88.3 us
  matrix products: 127 us -> 62.3 us
  other arithmetic: 54.1 us -> 23.9 us
  local copies, waits for them, and re-layouts: 57.3 us -> 43.5 us
  starting transfers between devices: 96.1 us -> 87.8 us
  waiting for transfers between devices: 169 us -> 175 us
    pallas_call x0 -> x14, Pallas kernels: none -> 76.3 us  [the longest x2 27 us: attend_backward(): pl.pallas_call(attend_back_body, grid=(LINE_ROWS // Q_ROWS,), in_specs=at...]
    ppermute x24 -> x6, waiting for transfers between devices: 54.6 us -> 2.2 us  [swap_shard(): return lax.ppermute(v, 'shard', [(i, i ^ m) for i in range(SHARDS)])]
    dot_general x12 -> x0, matrix products: 45.8 us -> none  [the longest x2 13.4 us: attend_backward(): jnp.einsum('hqe,hke->hqk', grad_heads, values, preferred_element_type=F32)]
    all_to_all x0 -> x2, waiting for transfers between devices: none -> 32.1 us  [the longest x1 32.1 us: gather_shards(): lax.all_to_all(copies, 'shard', 0, 0, tiled=True).reshape(-1, v.shape[1])]
    ppermute x24 -> x6, starting transfers between devices: 32 us -> 7.27 us  [swap_shard(): return lax.ppermute(v, 'shard', [(i, i ^ m) for i in range(SHARDS)])]
    dot_general x20 -> x12, matrix products: 66.4 us -> 49.9 us  [dot(): return lax.dot_general(a, b, (dims, ((), ())), preferred_element_type=F32)]
    convert_element_type x7 -> x1, other arithmetic: 17 us -> 0.65 us  [shards(): live = ((slot < my_count) & (slot < 5)).astype(F32)]
    ppermute x40, waiting for transfers between devices: 98.4 us -> 112 us  [swap_x(): return lax.ppermute(v, LINE, line_perm(lambda x, k: (x ^ m, k)))]
  transfers between devices with their start and end apart: 90 -> 74, of which waited for: 53 -> 40; matrix products, arithmetic and copies ran while one was open for 38% -> 19% of each run, Pallas kernels for 1% -> 16%
where the time goes in v3:
time: 509 us; the launch traced here: 500 us
  waiting for transfers between devices  175 us (34%)
  Pallas kernels  88.3 us (17%)
  starting transfers between devices  87.8 us (17%)
  matrix products  62.3 us (12%)
  local copies, waits for them, and re-layouts  43.5 us (9%)
  other arithmetic  23.9 us (5%)
  between operations  19.2 us (4%)
    ppermute x40, waiting for transfers between devices, swap_x(): return lax.ppermute(v, LINE, line_perm(lambda x, k: (x ^ m, k)))  112 us
    ppermute x40, starting transfers between devices, swap_x(): return lax.ppermute(v, LINE, line_perm(lambda x, k: (x ^ m, k)))  58.8 us
    dot_general x12, matrix products, dot(): return lax.dot_general(a, b, (dims, ((), ())), preferred_element_type=F32)  49.9 us
    all_to_all x1, waiting for transfers between devices, gather_shards(): lax.all_to_all(copies, 'shard', 0, 0, tiled=True).reshape(-1, v.shape[1])  32.1 us
    pallas_call x2, Pallas kernels, attend_backward(): pl.pallas_call(attend_back_body, grid=(LINE_ROWS // Q_ROWS,), in_specs=at...  27 us
    pallas_call x2, Pallas kernels, attend_forward(): pl.pallas_call(attend_body, grid=(LINE_ROWS // Q_ROWS,), in_specs=attend_...  22.9 us
    ppermute x17, waiting for transfers between devices, swap_core(): return lax.ppermute(v, LINE, line_perm(lambda x, k: (x, 1 - k)))  21.5 us
    unnamed x214, local copies, waits for them, and re-layouts  21.1 us
  transfers between devices with their start and end apart: 74, of which 40 were waited for; matrix products, arithmetic and copies ran while one was open for 19% of the time, Pallas kernels for 16%

profile of v3, /device:TPU:0, one launch (start us, length us, event | category | flops | bytes accessed | tf_op | source)
XLA Modules:
  0.0 500.0 jit_solution(7011245642446261160)
XLA Ops:
  21.3 6.1 %collective-permute-done.10 = bf16[36,2176]{1,0:T(8,128)(2,1)S(1)} collective-permute-done((bf16[36,2176]{1,0:T(8,128)(2,1)S(1)}, bf16[36,2176]{1,0:T(8,128)(2,1)S(1)}, u32[]{:S(2)}, u32[]{:S(2)}) %collective-permute-start.10) | collective-permute-done | bytes 156704 | tf_op jit(solution)/shard_map/ppermute | solution.py:42
  30.7 8.2 %all-to-all-start = ((bf16[16,72,768]{2,1,0:T(8,128)(2,1)}), bf16[16,72,768]{2,1,0:T(8,128)(2,1)S(1)}, u32[]{:S(2)}, u32[]{:S(2)}) async-start(bf16[16,72,768]{2,1,0:T(8,128)(2,1)} %broadcast_in_dim.32), calls=%async_computation | async-start | bytes 3538944 | tf_op jit(solution)/shard_map/all_to_all | solution.py:55
  41.0 32.1 %all-to-all-done = bf16[16,72,768]{2,1,0:T(8,128)(2,1)S(1)} async-done(((bf16[16,72,768]{2,1,0:T(8,128)(2,1)}), bf16[16,72,768]{2,1,0:T(8,128)(2,1)S(1)}, u32[]{:S(2)}, u32[]{:S(2)}) %all-to-all-start) | async-done | bytes 1769504 | tf_op jit(solution)/shard_map/all_to_all | solution.py:55
  79.0 6.3 %collective-permute-done.3 = bf16[128,1152]{1,0:T(8,128)(2,1)S(1)} collective-permute-done((bf16[128,1152]{1,0:T(8,128)(2,1)S(1)}, bf16[128,1152]{1,0:T(8,128)(2,1)S(1)}, u32[]{:S(2)}, u32[]{:S(2)}) %collective-permute-start.3) | collective-permute-done | bytes 294944 | tf_op jit(solution)/shard_map/ppermute | solution.py:42
  98.2 5.7 %collective-permute-done.27 = bf16[36,2176]{1,0:T(8,128)(2,1)S(1)} collective-permute-done((bf16[36,2176]{1,0:T(8,128)(2,1)S(1)}, bf16[36,2176]{1,0:T(8,128)(2,1)S(1)}, u32[]{:S(2)}, u32[]{:S(2)}) %collective-permute-start.27) | collective-permute-done | bytes 156704 | tf_op jit(solution)/shard_map/ppermute | solution.py:42
  117.2 11.5 %attend.2 = (bf16[1024,192]{1,0:T(8,128)(2,1)S(1)}, f32[8,1024]{1,0:T(8,128)S(1)}) custom-call(f32[3]{0:T(128)S(1)} %and_convert_fusion.live_ref, s32[1024,1]{1,0:T(8,128)S(1)} %copy-done.36, s32[1,1024]{1,0:T(1,128)S(1)} %bitcast.119, bf16[1024,576]{1,0:T(8,128)(2,1)S(1)} %project.4.qkv_ref), custom_call_target="tpu_custom_call" | custom-call | flops 3221225472 | bytes 1572864 | tf_op jit(solution)/shard_map/attend/pallas_call | solution.py:194
  137.4 12.4 %collective-permute-done.8 = bf16[128,1152]{1,0:T(8,128)(2,1)S(1)} collective-permute-done((bf16[128,1152]{1,0:T(8,128)(2,1)S(1)}, bf16[128,1152]{1,0:T(8,128)(2,1)S(1)}, u32[]{:S(2)}, u32[]{:S(2)}) %collective-permute-start.8) | collective-permute-done | bytes 294944 | tf_op jit(solution)/shard_map/ppermute | solution.py:42
  156.9 9.6 %multiply_convert_fusion.1 = (bf16[256,2176]{1,0:T(8,128)(2,1)S(1)}, f32[256,2176]{1,0:T(8,128)}, f32[256,2176]{1,0:T(8,128)}) fusion(f32[2176]{0:T(1024)S(1)} %get-tuple-element.169, bf16[1152,5120]{1,0:T(8,128)(2,1)} %all-gather.3.cloned.1.call-done, bf16[128,1152]{1,0:T(8,128)(2,1)S(1)} %collective-permute-done.9, ...), kind=kOutput, calls=%fused_computation.62 | convolution fusion | flops 1321402368 | bytes 11182592 | tf_op jit(solution)/shard_map/dot_general | solution.py:94
  166.5 4.8 fusion.16
  177.9 12.5 %collective-permute-done.18 = bf16[128,1152]{1,0:T(8,128)(2,1)S(1)} collective-permute-done((bf16[128,1152]{1,0:T(8,128)(2,1)S(1)}, bf16[128,1152]{1,0:T(8,128)(2,1)S(1)}, u32[]{:S(2)}, u32[]{:S(2)}) %collective-permute-start.18) | collective-permute-done | bytes 294944 | tf_op jit(solution)/shard_map/ppermute | solution.py:42
  197.7 11.5 %attend.3 = (bf16[1024,192]{1,0:T(8,128)(2,1)S(1)}, f32[8,1024]{1,0:T(8,128)S(1)}) custom-call(f32[3]{0:T(128)S(1)} %and_convert_fusion.live_ref, s32[1024,1]{1,0:T(8,128)S(1)} %copy-done.37, s32[1,1024]{1,0:T(1,128)S(1)} %bitcast.120, bf16[1024,576]{1,0:T(8,128)(2,1)S(1)} %project.5.qkv_ref), custom_call_target="tpu_custom_call" | custom-call | flops 3221225472 | bytes 1572864 | tf_op jit(solution)/shard_map/attend/pallas_call | solution.py:194
  221.3 10.5 %collective-permute-done.23 = bf16[128,1152]{1,0:T(8,128)(2,1)S(1)} collective-permute-done((bf16[128,1152]{1,0:T(8,128)(2,1)S(1)}, bf16[128,1152]{1,0:T(8,128)(2,1)S(1)}, u32[]{:S(2)}, u32[]{:S(2)}) %collective-permute-start.23) | collective-permute-done | bytes 294944 | tf_op jit(solution)/shard_map/ppermute | solution.py:42
  235.7 8.4 %multiply_convert_fusion = (bf16[256,2176]{1,0:T(8,128)(2,1)S(1)}, f32[256,2176]{1,0:T(8,128)S(1)}, f32[256,2176]{1,0:T(8,128)S(1)}) fusion(f32[2176]{0:T(1024)S(1)} %get-tuple-element.168, bf16[1152,4352]{1,0:T(8,128)(2,1)} %all-gather.5.cloned.1.call-done, bf16[128,1152]{1,0:T(8,128)(2,1)} %copy-done.69, bf16[128,1152]{1,0:T(8,128)(2,1)} %copy-done.56), kind=kOutput, calls=%fused_computation.49 | convolution fusion | flops 1321402368 | bytes 11182592 | tf_op jit(solution)/shard_map/dot_general | solution.py:94
  246.2 5.9 %hidden_grads.2 = bf16[1152,4352]{1,0:T(8,128)(2,1)} custom-call(bf16[256,1152]{1,0:T(8,128)(2,1)S(1)} %pad_maximum_fusion.5.refs_0_, bf16[256,2176]{1,0:T(8,128)(2,1)S(1)} %get-tuple-element.283.refs_1_, bf16[256,1152]{1,0:T(8,128)(2,1)S(1)} %pad_maximum_fusion.6.refs_2_, bf16[256,2176]{1,0:T(8,128)(2,1)S(1)} %get-tuple-element.189.refs_3_), custom_call_target="tpu_custom_call" | custom-call | flops 2566914048 | bytes 10027008 | tf_op jit(solution)/shard_map/hidden_grads/pallas_call | solution.py:348
  265.2 12.5 %collective-permute-done.33 = bf16[128,1152]{1,0:T(8,128)(2,1)S(1)} collective-permute-done((bf16[128,1152]{1,0:T(8,128)(2,1)S(1)}, bf16[128,1152]{1,0:T(8,128)(2,1)S(1)}, u32[]{:S(2)}, u32[]{:S(2)}) %collective-permute-start.33) | collective-permute-done | bytes 294944 | tf_op jit(solution)/shard_map/ppermute | solution.py:42
  283.2 13.5 %attend_back.2.rows_ref.dqkv_ref = bf16[1024,576]{1,0:T(8,128)(2,1)S(1)} custom-call(f32[3]{0:T(128)S(1)} %and_convert_fusion.live_ref, s32[1024,1]{1,0:T(8,128)S(1)} %copy-done.38, s32[1,1024]{1,0:T(1,128)S(1)} %bitcast.121, f32[8,1024]{1,0:T(8,128)S(1)} %get-tuple-element.65.lse_ref, bf16[1024,192]{1,0:T(8,128)(2,1)S(1)} %project.6.dout_ref, ...), custom_call_target="tpu_custom_call" | custom-call | flops 8053063680 | bytes 2752512 | tf_op jit(solution)/shard_map/attend_back/pallas_call | solution.py:217
  308.7 12.5 %collective-permute-done.38 = bf16[128,1152]{1,0:T(8,128)(2,1)S(1)} collective-permute-done((bf16[128,1152]{1,0:T(8,128)(2,1)S(1)}, bf16[128,1152]{1,0:T(8,128)(2,1)S(1)}, u32[]{:S(2)}, u32[]{:S(2)}) %collective-permute-start.38) | collective-permute-done | bytes 294944 | tf_op jit(solution)/shard_map/ppermute | solution.py:42
  323.9 6.1 %head_grads.3.refs_4_ = bf16[1152,768]{1,0:T(8,128)(2,1)} custom-call(bf16[512,1152]{1,0:T(8,128)(2,1)S(1)} %copy-done.13, bf16[512,1152]{1,0:T(8,128)(2,1)} %collective-permute-done.19.other.x1, bf16[512,1152]{1,0:T(8,128)(2,1)S(1)} %pad_maximum_fusion.2.mine.m0, bf16[512,1152]{1,0:T(8,128)(2,1)S(1)} %collective-permute-done.34.other.m1, ...), custom_call_target="tpu_custom_call" | custom-call | flops 1811939328 | bytes 8388608 | tf_op jit(solution)/shard_map/head_grads/pallas_call | solution.py:308
  334.9 6.1 %hidden_grads.3 = bf16[1152,5120]{1,0:T(8,128)(2,1)} custom-call(bf16[256,1152]{1,0:T(8,128)(2,1)S(1)} %pad_maximum_fusion.4.refs_0_, bf16[256,2176]{1,0:T(8,128)(2,1)S(1)} %get-tuple-element.285.refs_1_, bf16[256,1152]{1,0:T(8,128)(2,1)S(1)} %pad_maximum_fusion.7.refs_2_, bf16[256,2176]{1,0:T(8,128)(2,1)S(1)} %copy-done.29, bf16[1152,768]{1,0:T(8,128)(2,1)S(1)} %copy-done.14), custom_call_target="tpu_custom_call" | custom-call | flops 2566914048 | bytes 11796480 | tf_op jit(solution)/shard_map/hidden_grads/pallas_call | solution.py:348
  361.4 8.1 %collective-permute-done.43 = bf16[128,1152]{1,0:T(8,128)(2,1)S(1)} collective-permute-done((bf16[128,1152]{1,0:T(8,128)(2,1)S(1)}, bf16[128,1152]{1,0:T(8,128)(2,1)S(1)}, u32[]{:S(2)}, u32[]{:S(2)}) %collective-permute-start.43) | collective-permute-done | bytes 294944 | tf_op jit(solution)/shard_map/ppermute | solution.py:42
  385.6 13.5 %attend_back.3.rows_ref.dqkv_ref = bf16[1024,576]{1,0:T(8,128)(2,1)S(1)} custom-call(f32[3]{0:T(128)S(1)} %and_convert_fusion.live_ref, s32[1024,1]{1,0:T(8,128)S(1)} %copy-done.39, s32[1,1024]{1,0:T(1,128)S(1)} %bitcast.122, f32[8,1024]{1,0:T(8,128)S(1)} %get-tuple-element.70.lse_ref, bf16[1024,192]{1,0:T(8,128)(2,1)S(1)} %copy-done.35, ...), custom_call_target="tpu_custom_call" | custom-call | flops 8053063680 | bytes 2752512 | tf_op jit(solution)/shard_map/attend_back/pallas_call | solution.py:217
  409.7 5.8 %head_grads.2 = bf16[1152,768]{1,0:T(8,128)(2,1)} custom-call(bf16[512,1152]{1,0:T(8,128)(2,1)S(1)} %copy-done.11, bf16[512,1152]{1,0:T(8,128)(2,1)S(1)} %copy-done.19, bf16[512,1152]{1,0:T(8,128)(2,1)S(1)} %copy-done.9, bf16[512,1152]{1,0:T(8,128)(2,1)S(1)} %copy-done.16, bf16[1024,576]{1,0:T(8,128)(2,1)} %copy-done.6, bf16[1024,192]{1,0:T(8,128)(2,1)S(1)} %copy-done.21), custom_call_target="tpu_custom_call" | custom-call | flops 1811939328 | bytes 8388608 | tf_op jit(solution)/shard_map/head_grads/pallas_call | solution.py:308
  429.4 12.5 %collective-permute-done.51 = bf16[128,1152]{1,0:T(8,128)(2,1)S(1)} collective-permute-done((bf16[128,1152]{1,0:T(8,128)(2,1)S(1)}, bf16[128,1152]{1,0:T(8,128)(2,1)S(1)}, u32[]{:S(2)}, u32[]{:S(2)}) %collective-permute-start.51) | collective-permute-done | bytes 294944 | tf_op jit(solution)/shard_map/ppermute | solution.py:42
  453.4 5.1 %reduce-scatter.10.cloned.1.call-done = bf16[1,72,5120]{2,1,0:T(8,128)(2,1)} async-done(((bf16[1,1152,5120]{2,1,0:T(8,128)(2,1)}), bf16[1,72,5120]{2,1,0:T(8,128)(2,1)}) %reduce-scatter.10.cloned.1.call-update) | async-done | bytes 737296
  (585 shorter events, 239.7 us)
Async XLA Ops:
  7.2 149.6 %all-gather.3.cloned.1.call-start = ((), (), s32[]{:S(2)}) async-start(), calls=%async_computation.4 | async-start | bytes 12533760 | tf_op jit(solution)/shard_map/all_gather | solution.py:428
  30.7 42.3 %all-to-all-start = ((bf16[16,72,768]{2,1,0:T(8,128)(2,1)}), bf16[16,72,768]{2,1,0:T(8,128)(2,1)S(1)}, u32[]{:S(2)}, u32[]{:S(2)}) async-start(bf16[16,72,768]{2,1,0:T(8,128)(2,1)} %broadcast_in_dim.32), calls=%async_computation | async-start | bytes 3538944 | tf_op jit(solution)/shard_map/all_to_all | solution.py:55
  38.9 196.7 %all-gather.5.cloned.1.call-start = ((), (), s32[]{:S(2)}) async-start(), calls=%async_computation.5 | async-start | bytes 10653696 | tf_op jit(solution)/shard_map/all_gather | solution.py:428
  107.0 272.1 %reduce-scatter.8.cloned.1.call-start = ((), (), s32[]{:S(2)}) async-start(), calls=%async_computation.6 | async-start | bytes 10653696
  133.1 16.7 %collective-permute-start.8 = (bf16[128,1152]{1,0:T(8,128)(2,1)S(1)}, bf16[128,1152]{1,0:T(8,128)(2,1)S(1)}, u32[]{:S(2)}, u32[]{:S(2)}) collective-permute-start(bf16[128,1152]{1,0:T(8,128)(2,1)S(1)} %get-tuple-element.55), channel_id=1, source_target_pairs={{0,6},{1,7},{2,4},{3,5},{4,2},{5,3},{6,0},{7,1},{8,14},{9,15},{10,... | collective-permute-start | bytes 884744 | tf_op jit(solution)/shard_map/ppermute | solution.py:42
  134.9 14.9 %collective-permute-start.7 = (bf16[128,1152]{1,0:T(8,128)(2,1)S(1)}, bf16[128,1152]{1,0:T(8,128)(2,1)S(1)}, u32[]{:S(2)}, u32[]{:S(2)}) collective-permute-start(bf16[128,1152]{1,0:T(8,128)(2,1)S(1)} %get-tuple-element.54), channel_id=1, source_target_pairs={{0,2},{1,3},{2,0},{3,1},{4,6},{5,7},{6,4},{7,5},{8,10},{9,11},{10,... | collective-permute-start | bytes 884744 | tf_op jit(solution)/shard_map/ppermute | solution.py:42
  135.1 15.3 %collective-permute-start.6 = (bf16[128,1152]{1,0:T(8,128)(2,1)S(1)}, bf16[128,1152]{1,0:T(8,128)(2,1)S(1)}, u32[]{:S(2)}, u32[]{:S(2)}) collective-permute-start(bf16[128,1152]{1,0:T(8,128)(2,1)S(1)} %get-tuple-element.53), channel_id=1, source_target_pairs={{0,4},{1,5},{2,6},{3,7},{4,0},{5,1},{6,2},{7,3},{8,12},{9,13},{10,... | collective-permute-start | bytes 884744 | tf_op jit(solution)/shard_map/ppermute | solution.py:42
  173.7 16.7 %collective-permute-start.18 = (bf16[128,1152]{1,0:T(8,128)(2,1)S(1)}, bf16[128,1152]{1,0:T(8,128)(2,1)S(1)}, u32[]{:S(2)}, u32[]{:S(2)}) collective-permute-start(bf16[128,1152]{1,0:T(8,128)(2,1)S(1)} %add_convert_fusion.3), channel_id=1, source_target_pairs={{0,6},{1,7},{2,4},{3,5},{4,2},{5,3},{6,0},{7,1},{8,14},{9,15},{10,... | collective-permute-start | bytes 884744 | tf_op jit(solution)/shard_map/ppermute | solution.py:42
  214.9 16.9 %collective-permute-start.23 = (bf16[128,1152]{1,0:T(8,128)(2,1)S(1)}, bf16[128,1152]{1,0:T(8,128)(2,1)S(1)}, u32[]{:S(2)}, u32[]{:S(2)}) collective-permute-start(bf16[128,1152]{1,0:T(8,128)(2,1)S(1)} %get-tuple-element.62), channel_id=1, source_target_pairs={{0,6},{1,7},{2,4},{3,5},{4,2},{5,3},{6,0},{7,1},{8,14},{9,15},{10,... | collective-permute-start | bytes 884744 | tf_op jit(solution)/shard_map/ppermute | solution.py:42
  253.1 205.4 %reduce-scatter.10.cloned.1.call-start = ((), (), s32[]{:S(2)}) async-start(), calls=%async_computation.7 | async-start | bytes 12533760
  261.0 16.7 %collective-permute-start.33 = (bf16[128,1152]{1,0:T(8,128)(2,1)S(1)}, bf16[128,1152]{1,0:T(8,128)(2,1)S(1)}, u32[]{:S(2)}, u32[]{:S(2)}) collective-permute-start(bf16[128,1152]{1,0:T(8,128)(2,1)S(1)} %get-tuple-element.179), channel_id=1, source_target_pairs={{0,6},{1,7},{2,4},{3,5},{4,2},{5,3},{6,0},{7,1},{8,14},{9,15},{10,... | collective-permute-start | bytes 884744 | tf_op jit(solution)/shard_map/ppermute | solution.py:42
  304.6 16.7 %collective-permute-start.38 = (bf16[128,1152]{1,0:T(8,128)(2,1)S(1)}, bf16[128,1152]{1,0:T(8,128)(2,1)S(1)}, u32[]{:S(2)}, u32[]{:S(2)}) collective-permute-start(bf16[128,1152]{1,0:T(8,128)(2,1)S(1)} %get-tuple-element.69), channel_id=1, source_target_pairs={{0,6},{1,7},{2,4},{3,5},{4,2},{5,3},{6,0},{7,1},{8,14},{9,15},{10,... | collective-permute-start | bytes 884744 | tf_op jit(solution)/shard_map/ppermute | solution.py:42
  352.9 16.6 %collective-permute-start.43 = (bf16[128,1152]{1,0:T(8,128)(2,1)S(1)}, bf16[128,1152]{1,0:T(8,128)(2,1)S(1)}, u32[]{:S(2)}, u32[]{:S(2)}) collective-permute-start(bf16[128,1152]{1,0:T(8,128)(2,1)S(1)} %get-tuple-element.185), channel_id=1, source_target_pairs={{0,6},{1,7},{2,4},{3,5},{4,2},{5,3},{6,0},{7,1},{8,14},{9,15},{10,... | collective-permute-start | bytes 884744 | tf_op jit(solution)/shard_map/ppermute | solution.py:42
  355.3 14.9 %collective-permute-start.41 = (bf16[128,1152]{1,0:T(8,128)(2,1)S(1)}, bf16[128,1152]{1,0:T(8,128)(2,1)S(1)}, u32[]{:S(2)}, u32[]{:S(2)}) collective-permute-start(bf16[128,1152]{1,0:T(8,128)(2,1)S(1)} %get-tuple-element.185), channel_id=1, source_target_pairs={{0,4},{1,5},{2,6},{3,7},{4,0},{5,1},{6,2},{7,3},{8,12},{9,13},{10,... | collective-permute-start | bytes 884744 | tf_op jit(solution)/shard_map/ppermute | solution.py:42
  380.7 18.4 %collective-permute-start.47 = (bf16[36,2176]{1,0:T(8,128)(2,1)S(1)}, bf16[36,2176]{1,0:T(8,128)(2,1)S(1)}, u32[]{:S(2)}, u32[]{:S(2)}) collective-permute-start(bf16[36,2176]{1,0:T(8,128)(2,1)S(1)} %pad_maximum_fusion.13), channel_id=1, source_target_pairs={{0,6},{1,7},{2,4},{3,5},{4,2},{5,3},{6,0},{7,1},{8,14},{9,15},{10,... | collective-permute-start | bytes 470024 | tf_op jit(solution)/shard_map/ppermute | solution.py:42
  383.4 15.7 %collective-permute-start.46 = (bf16[36,2176]{1,0:T(8,128)(2,1)S(1)}, bf16[36,2176]{1,0:T(8,128)(2,1)S(1)}, u32[]{:S(2)}, u32[]{:S(2)}) collective-permute-start(bf16[36,2176]{1,0:T(8,128)(2,1)S(1)} %pad_maximum_fusion.12), channel_id=1, source_target_pairs={{0,2},{1,3},{2,0},{3,1},{4,6},{5,7},{6,4},{7,5},{8,10},{9,11},{10,... | collective-permute-start | bytes 470024 | tf_op jit(solution)/shard_map/ppermute | solution.py:42
  383.9 15.3 %collective-permute-start.45 = (bf16[36,2176]{1,0:T(8,128)(2,1)S(1)}, bf16[36,2176]{1,0:T(8,128)(2,1)S(1)}, u32[]{:S(2)}, u32[]{:S(2)}) collective-permute-start(bf16[36,2176]{1,0:T(8,128)(2,1)S(1)} %pad_maximum_fusion.11), channel_id=1, source_target_pairs={{0,4},{1,5},{2,6},{3,7},{4,0},{5,1},{6,2},{7,3},{8,12},{9,13},{10,... | collective-permute-start | bytes 470024 | tf_op jit(solution)/shard_map/ppermute | solution.py:42
  402.4 19.4 %collective-permute-start.48 = (bf16[512,1152]{1,0:T(8,128)(2,1)}, bf16[512,1152]{1,0:T(8,128)(2,1)}, u32[]{:S(2)}, u32[]{:S(2)}) collective-permute-start(bf16[512,1152]{1,0:T(8,128)(2,1)} %convolution_convert_fusion), channel_id=1, source_target_pairs={{0,1},{1,0},{2,3},{3,2},{4,5},{5,4},{6,7},{7,6},{8,9},{9,8},{10,11... | collective-permute-start | bytes 3538952 | tf_op jit(solution)/shard_map/ppermute | solution.py:38
  402.8 26.6 %collective-permute-start.56 = (f32[2,1152]{1,0:T(2,128)S(1)}, f32[2,1152]{1,0:T(2,128)S(1)}, u32[]{:S(2)}, u32[]{:S(2)}) collective-permute-start(f32[2,1152]{1,0:T(2,128)S(1)} %select_maximum_fusion.1), channel_id=1, source_target_pairs={{0,4},{4,0},{1,5},{5,1},{2,6},{6,2},{3,7},{7,3},{8,12},{12,8},{9,1... | collective-permute-start | bytes 27656 | tf_op jit(solution)/shard_map/ppermute | solution.py:46
  415.5 43.0 %all-to-all-start.1 = ((bf16[16,72,768]{2,1,0:T(8,128)(2,1)}), bf16[16,72,768]{2,1,0:T(8,128)(2,1)}, u32[]{:S(2)}, u32[]{:S(2)}) async-start(bf16[16,72,768]{2,1,0:T(8,128)(2,1)} %bitcast.124), calls=%async_computation.1 | async-start | bytes 3538944 | tf_op jit(solution)/shard_map/all_to_all | solution.py:60
  425.2 16.7 %collective-permute-start.51 = (bf16[128,1152]{1,0:T(8,128)(2,1)S(1)}, bf16[128,1152]{1,0:T(8,128)(2,1)S(1)}, u32[]{:S(2)}, u32[]{:S(2)}) collective-permute-start(bf16[128,1152]{1,0:T(8,128)(2,1)S(1)} %get-tuple-element.75), channel_id=1, source_target_pairs={{0,6},{1,7},{2,4},{3,5},{4,2},{5,3},{6,0},{7,1},{8,14},{9,15},{10,... | collective-permute-start | bytes 884744 | tf_op jit(solution)/shard_map/ppermute | solution.py:42
  458.6 18.8 %collective-permute-start.58 = (f32[20,1152]{1,0:T(8,128)S(1)}, f32[20,1152]{1,0:T(8,128)S(1)}, u32[]{:S(2)}, u32[]{:S(2)}) collective-permute-start(f32[20,1152]{1,0:T(8,128)S(1)} %pad_maximum_fusion.23), channel_id=1, source_target_pairs={{0,16},{8,24},{16,0},{24,8},{32,48},{40,56},{48,32},{56,40},{64,80... | collective-permute-start | bytes 276488 | tf_op jit(solution)/shard_map/ppermute | solution.py:50
  459.0 18.8 %collective-permute-start.59 = (f32[20,1152]{1,0:T(8,128)S(1)}, f32[20,1152]{1,0:T(8,128)S(1)}, u32[]{:S(2)}, u32[]{:S(2)}) collective-permute-start(f32[20,1152]{1,0:T(8,128)S(1)} %pad_maximum_fusion.23), channel_id=1, source_target_pairs={{0,24},{8,16},{16,8},{24,0},{32,56},{40,48},{48,40},{56,32},{64,88... | collective-permute-start | bytes 276488 | tf_op jit(solution)/shard_map/ppermute | solution.py:50
  461.3 16.4 %collective-permute-start.57 = (f32[20,1152]{1,0:T(8,128)S(1)}, f32[20,1152]{1,0:T(8,128)}, u32[]{:S(2)}, u32[]{:S(2)}) collective-permute-start(f32[20,1152]{1,0:T(8,128)S(1)} %pad_maximum_fusion.23), channel_id=1, source_target_pairs={{0,8},{8,0},{16,24},{24,16},{32,40},{40,32},{48,56},{56,48},{64,72... | collective-permute-start | bytes 276488 | tf_op jit(solution)/shard_map/ppermute | solution.py:50
  (150 other events, 1952.2 us)
Sparse Core Ops, SparseCore 0:
  29.5 100.8 all-gather.2
  132.6 78.1 all-gather.4
  253.2 88.7 reduce-scatter.7
  345.8 112.7 reduce-scatter.9

commit v4 on v3

--- a/solution.py
+++ b/solution.py
@@ -50,9 +50,8 @@
     return lax.ppermute(v, "shard", [(i, i ^ m) for i in range(SHARDS)])
 
 
-def gather_shards(v):
-    copies = jnp.broadcast_to(v, (SHARDS, *v.shape))
-    return lax.all_to_all(copies, "shard", 0, 0, tiled=True).reshape(-1, v.shape[1])
+def gather_shards(copies):
+    return lax.all_to_all(copies, "shard", 0, 0, tiled=True).reshape(-1, copies.shape[2])
 
 
 def to_shards(v):
@@ -73,16 +72,22 @@
     return mine, swap_core(mine)
 
 
-def sum_rows(rows, w, lo, hi):
+def sum_rows(rows, w, lo, hi, beside=None, apart=False):
     arrived = swap_core(dot(rows[HALF:], w[:, lo:hi], ((1,), (1,))).astype(BF))
     own, *others = chip_sum(rows, w, arrived, lo, hi)
-    parts = [swap_x(v, m).astype(F32) for m, v in zip((1, 2, 3), others)]
-    return (own + parts[0]) + (parts[1] + parts[2])
-
-
-def sum_shards(v):
-    v = (v + swap_shard(v, 1)) + (swap_shard(v, 2) + swap_shard(v, 3))
-    return (v + swap_shard(v, 4)) + (swap_shard(v, 8) + swap_shard(v, 12))
+    parts = [swap_x(v, m) for m, v in zip((1, 2, 3), others)]
+    extra = None
+    if beside is not None:
+        own, rows = lax.optimization_barrier((own, rows))
+        extra = beside(rows)
+        if not apart:
+            parts, extra = lax.optimization_barrier((parts, extra))
+    parts = [v.astype(F32) for v in parts]
+    return (own + parts[0]) + (parts[1] + parts[2]), extra
+
+
+def sum_shards(v, step):
+    return (v + swap_shard(v, step)) + (swap_shard(v, 2 * step) + swap_shard(v, 3 * step))
 
 
 def sum_line_parts(both_cores, each_core):
@@ -111,8 +116,12 @@
     return dx, jnp.sum(dy * xhat, axis=0), jnp.sum(dy, axis=0)
 
 
-def gelu_exact(v):
-    return jax.nn.gelu(v, approximate=False)
+def normal_cdf(v):
+    return 0.5 + 0.5 * lax.erf(v * 0.5**0.5)
+
+
+def gelu_slope(v):
+    return normal_cdf(v) + v * jnp.exp(-0.5 * v * v) * (2 * jnp.pi) ** -0.5
 
 
 LINE_ROWS = 8 * ROWS
@@ -258,8 +267,17 @@
             got = mul(x[...], w_ref[:, lo:hi], PLAIN) + bias_ref[...]
             out_ref[at : at + HALF, :] = got.astype(BF)
 
+    half = pl.BlockSpec((HALF, DP), lambda i: (0, 0))
     return pl.pallas_call(
         body,
+        grid=(1,),
+        in_specs=[
+            half,
+            half,
+            pl.BlockSpec((DP, HW), lambda i: (0, 0)),
+            pl.BlockSpec((1, hi - lo), lambda i: (0, 0)),
+        ],
+        out_specs=pl.BlockSpec((2 * HALF, hi - lo), lambda i: (0, 0)),
         out_shape=jax.ShapeDtypeStruct((2 * HALF, hi - lo), BF),
         compiler_params=pltpu.CompilerParams(vmem_limit_bytes=48 << 20),
         cost_estimate=pl.CostEstimate(
@@ -415,7 +433,7 @@
         return jnp.concatenate([jnp.pad(top, gap), jnp.pad(low, gap)], axis=0)
 
     def exchanged_hidden(w_fc, w_down):
-        raw = jnp.concatenate([w_fc, w_down.T], axis=1)
+        raw = jnp.concatenate([w_fc, w_down], axis=1)
         raw = jnp.pad(raw, ((0, WIDE - CHUNK), (0, 0)))
         p = [raw] + [swap_x(raw, m) for m in (1, 2, 3)]
         own, other = [
@@ -427,16 +445,18 @@
     def fetch(pack):
         return lax.all_gather(pack, "shard", axis=0, tiled=True)
 
-    halves_a = head_halves(w_qkv[0, 0], w_out[0, 0])
-    pack_a = exchanged(halves_a)
+    w_fc_a, w_down_a, w_qkv_a, w_out_a = lax.optimization_barrier(
+        (w_fc[0], w_down[0].T, w_qkv[0, 0], w_out[0, 0])
+    )
+    pack_a = exchanged(head_halves(w_qkv_a, w_out_a))
     w_qkv_b, w_out_b, pack_a = lax.optimization_barrier((w_qkv[1, 0], w_out[1, 0], pack_a))
-    hidden_a = exchanged_hidden(w_fc[0], w_down[0])
+    hidden_a = exchanged_hidden(w_fc_a, w_down_a)
     heads_b = exchanged(head_halves(w_qkv_b, w_out_b))
-    heads_a, tokens = lax.optimization_barrier((gather_shards(pack_a), tokens))
-    fetched_a = fetch(jnp.concatenate([hidden_a, heads_b], axis=1))
+    copies = jnp.broadcast_to(pack_a, (SHARDS, *pack_a.shape))
+    fetched_a = fetch(jnp.concatenate([heads_b, hidden_a], axis=1))
     weights = [
-        (heads_a, fetched_a[:, : 2 * FC]),
-        (fetched_a[:, 2 * FC :], None),
+        (None, fetched_a[:, HW : HW + FC], fetched_a[:, HW + FC :]),
+        (fetched_a, None, None),
     ]
 
     core = tp % 2
@@ -471,22 +491,30 @@
     gradient = widen(cotangent[0])
     stored = []
     for l in range(LAYERS):
-        w_heads, w_hidden = weights[l]
+        w_heads = weights[l][0]
         normed, xhat, rstd = norm_forward(hidden, gains[l, 0], shifts[l, 0], mask)
+        if l == 0:
+            normed, copies = lax.optimization_barrier((normed, copies))
+            w_heads, w_fc_b, w_down_b = lax.optimization_barrier(
+                (gather_shards(copies), w_fc[1], w_down[1].T)
+            )
+            hidden_b = exchanged_hidden(w_fc_b, w_down_b)
+            weights[0] = (w_heads, *weights[0][1:])
         normed_all = gather_rows(normed)
-        if l == 0:
-            normed_all, w_fc_b, w_down_b = lax.optimization_barrier(
-                (normed_all, w_fc[1], w_down[1])
-            )
-            weights[1] = (weights[1][0], fetch(exchanged_hidden(w_fc_b, w_down_b)))
         qkv = project(normed_all, w_heads, 0, 3 * QW, head_bias[l])
         attended, log_total = attend_forward(live, places, qkv)
-        middle = hidden + (sum_rows(attended, w_heads, 3 * QW, HW) + out_bias[l])
+        if l == 0:
+            attended, hidden_b = lax.optimization_barrier((attended, hidden_b))
+            fetched_b = fetch(hidden_b)
+            weights[1] = (fetched_a, fetched_b[:, :FC], fetched_b[:, FC:])
+        summed, _ = sum_rows(attended, w_heads, 3 * QW, HW)
+        middle = hidden + (summed + out_bias[l])
         normed_two, xhat_two, rstd_two = norm_forward(middle, gains[l, 1], shifts[l, 1], mask)
         normed_two_all = gather_pair(normed_two)
-        inner = dot(normed_two_all, w_hidden[:, :FC], ((1,), (0,))) + fc_bias[l]
-        activated = gelu_exact(inner).astype(BF)
-        down_out = dot(activated, w_hidden[:, FC:], ((1,), (1,)))
+        _, w_up, w_back = weights[l]
+        inner = dot(normed_two_all, w_up, ((1,), (0,))) + fc_bias[l]
+        activated = (inner * normal_cdf(inner)).astype(BF)
+        down_out = dot(activated, w_back, ((1,), (1,)))
         hidden = middle + (sum_pair(down_out) + down_bias[l])
         stored.append(
             (
@@ -528,7 +556,7 @@
         return lax.optimization_barrier(v).reshape(v.shape[-2:])
 
     for l in reversed(range(LAYERS)):
-        w_heads, w_hidden = weights[l]
+        w_heads, w_up, w_back = weights[l]
         (
             normed_all,
             xhat,
@@ -545,8 +573,8 @@
         g_low = gradient.astype(BF)
         g_all = gather_pair(g_low)
         grad_down_b = jnp.sum(g_low.astype(F32), axis=0)
-        grad_activated = dot(g_all, w_hidden[:, FC:], ((1,), (0,)))
-        grad_inner = jax.vjp(gelu_exact, inner)[1](grad_activated)[0].astype(BF)
+        grad_activated = dot(g_all, w_back, ((1,), (0,)))
+        grad_inner = (grad_activated * gelu_slope(inner)).astype(BF)
         grad_fc_b = jnp.sum(grad_inner.astype(F32), axis=0)
         hidden_sums[l] = to_owner(
             hidden_grads(
@@ -554,7 +582,7 @@
             ),
             1 - l,
         )
-        grad_two = sum_pair(dot(grad_inner, w_hidden[:, :FC], ((1,), (1,))))
+        grad_two = sum_pair(dot(grad_inner, w_up, ((1,), (1,))))
         dx, gain_two, shift_two = norm_backward(grad_two, xhat_two, rstd_two, gains[l, 1], mask)
         grad_middle = gradient + dx
         m_low = grad_middle.astype(BF)
@@ -565,9 +593,15 @@
         if l == 0:
             hidden_own = [None, own_hidden(hidden_sums[1])]
             grad_qkv, hidden_own[1] = lax.optimization_barrier((grad_qkv, hidden_own[1]))
-        head_grads = head_grads_of(normed_all, grad_qkv, m_all, attended)
         qkv_b = jnp.sum(grad_qkv.astype(F32), axis=0)
-        grad_one = sum_rows(grad_qkv, w_heads, 0, 3 * QW)
+        grad_one, head_grads = sum_rows(
+            grad_qkv,
+            w_heads,
+            0,
+            3 * QW,
+            lambda rows: head_grads_of(normed_all, rows, m_all, attended),
+            apart=l == 0,
+        )
         dx, gain_one, shift_one = norm_backward(grad_one, xhat, rstd, gains[l, 0], mask)
         gradient = grad_middle + dx
         small[l] = [gain_one, gain_two, shift_one, shift_two, grad_out_b, grad_down_b]
@@ -576,18 +610,20 @@
         )
         head_biases.append(qkv_b)
 
+    head_sum_a = to_shards(head_grads)
+
     line = sum_line_parts(
         jnp.stack(small[0] + small[1]),
         jnp.pad(jnp.stack(fc_biases[::-1]), ((0, 0), (0, 2 * DP - FC))).reshape(4, DP),
     )
-    head_sum_a = to_shards(head_grads)
-    line, head_sum_a, hidden_sums[0] = lax.optimization_barrier(
-        (line, head_sum_a, hidden_sums[0])
-    )
     own = jnp.pad(jnp.stack(head_biases[::-1]), ((0, 0), (0, DP - 3 * QW)))
     other = swap_ctx(own)
     both = jnp.concatenate([jnp.where(first, own, other), jnp.where(first, other, own)], axis=0)
-    sums = sum_shards(jnp.concatenate([line, both], axis=0))
+    sums = sum_shards(jnp.concatenate([line, both], axis=0), 1)
+    sums, head_sum_a, hidden_sums[0] = lax.optimization_barrier(
+        (sums, head_sum_a, hidden_sums[0])
+    )
+    sums = sum_shards(sums, 4)
     vectors = narrow(sums[:12]).reshape(LAYERS, 6, D)
     fc_sum = sums[12:16].reshape(LAYERS, 2 * DP)
     fc_sum = jnp.where(high, fc_sum[:, FR : 2 * FR], fc_sum[:, :FR])

time: 509 us -> 486 us (0.955)
  waiting for transfers between devices: 175 us -> 156 us
  Pallas kernels: 88.3 us -> 96.2 us
  matrix products: 62.3 us -> 54.5 us
  local copies, waits for them, and re-layouts: 43.5 us -> 37.7 us
    ppermute x40, waiting for transfers between devices: 112 us -> 87.6 us  [swap_x(): return lax.ppermute(v, LINE, line_perm(lambda x, k: (x ^ m, k)))]
    all_to_all x1, waiting for transfers between devices: 32.1 us -> 15.2 us  [gather_shards(): lax.all_to_all(copies, 'shard', 0, 0, tiled=True)]
    ppermute x6, waiting for transfers between devices: 2.2 us -> 16.4 us  [swap_shard(): return lax.ppermute(v, 'shard', [(i, i ^ m) for i in range(SHARDS)])]
    dot_general x12, matrix products: 49.9 us -> 40.9 us  [dot(): return lax.dot_general(a, b, (dims, ((), ())), preferred_element_type=F32)]
    all_gather x2, waiting for transfers between devices: 0.04 us -> 8.35 us  [fetch(): return lax.all_gather(pack, 'shard', axis=0, tiled=True)]
    unnamed x214 -> x165, local copies, waits for them, and re-layouts: 21.1 us -> 18.6 us
  transfers between devices with their start and end apart: 74 -> 74, of which waited for: 40 -> 40; matrix products, arithmetic and copies ran while one was open for 19% -> 19% of each run, Pallas kernels for 16% -> 19%
where the time goes in v4:
time: 486 us; the launch traced here: 477 us
  waiting for transfers between devices  156 us (32%)
  Pallas kernels  96.2 us (20%)
  starting transfers between devices  89 us (18%)
  matrix products  54.5 us (11%)
  local copies, waits for them, and re-layouts  37.7 us (8%)
  other arithmetic  24.2 us (5%)
  between operations  18.9 us (4%)
    ppermute x40, waiting for transfers between devices, swap_x(): return lax.ppermute(v, LINE, line_perm(lambda x, k: (x ^ m, k)))  87.6 us
    ppermute x40, starting transfers between devices, swap_x(): return lax.ppermute(v, LINE, line_perm(lambda x, k: (x ^ m, k)))  59.3 us
    dot_general x12, matrix products, dot(): return lax.dot_general(a, b, (dims, ((), ())), preferred_element_type=F32)  40.9 us
    pallas_call x2, Pallas kernels, attend_backward(): pl.pallas_call(attend_back_body, grid=(LINE_ROWS // Q_ROWS,), in_specs=at...  27 us
    ppermute x17, waiting for transfers between devices, swap_core(): return lax.ppermute(v, LINE, line_perm(lambda x, k: (x, 1 - k)))  24.2 us
    pallas_call x2, Pallas kernels, attend_forward(): pl.pallas_call(attend_body, grid=(LINE_ROWS // Q_ROWS,), in_specs=attend_...  22.9 us
    unnamed x165, local copies, waits for them, and re-layouts  18.6 us
    ppermute x6, waiting for transfers between devices, swap_shard(): return lax.ppermute(v, 'shard', [(i, i ^ m) for i in range(SHARDS)])  16.4 us
  transfers between devices with their start and end apart: 74, of which 40 were waited for; matrix products, arithmetic and copies ran while one was open for 19% of the time, Pallas kernels for 19%

profile of v4, /device:TPU:0, one launch (start us, length us, event | category | flops | bytes accessed | tf_op | source)
XLA Modules:
  0.0 476.9 jit_solution(12680803153965458010)
XLA Ops:
  45.5 8.0 %all-to-all-start = ((bf16[16,72,768]{2,1,0:T(8,128)(2,1)}), bf16[16,72,768]{2,1,0:T(8,128)(2,1)S(1)}, u32[]{:S(2)}, u32[]{:S(2)}) async-start(bf16[16,72,768]{2,1,0:T(8,128)(2,1)} %broadcast_in_dim.35), calls=%async_computation | async-start | bytes 3538944 | tf_op jit(solution)/shard_map/all_to_all | solution.py:54
  58.1 4.7 collective-permute-done.3
  67.5 15.2 %all-to-all-done = bf16[16,72,768]{2,1,0:T(8,128)(2,1)S(1)} async-done(((bf16[16,72,768]{2,1,0:T(8,128)(2,1)}), bf16[16,72,768]{2,1,0:T(8,128)(2,1)S(1)}, u32[]{:S(2)}, u32[]{:S(2)}) %all-to-all-start) | async-done | bytes 1769504 | tf_op jit(solution)/shard_map/all_to_all | solution.py:54
  91.7 11.5 %attend.2 = (bf16[1024,192]{1,0:T(8,128)(2,1)S(1)}, f32[8,1024]{1,0:T(8,128)S(1)}) custom-call(f32[3]{0:T(128)S(1)} %and_convert_fusion.live_ref, s32[1024,1]{1,0:T(8,128)S(1)} %copy-done.32, s32[1,1024]{1,0:T(1,128)S(1)} %bitcast.136, bf16[1024,576]{1,0:T(8,128)(2,1)S(1)} %project.4.qkv_ref), custom_call_target="tpu_custom_call" | custom-call | flops 3221225472 | bytes 1572864 | tf_op jit(solution)/shard_map/attend/pallas_call | solution.py:203
  116.1 11.5 %collective-permute-done.11 = bf16[128,1152]{1,0:T(8,128)(2,1)S(1)} collective-permute-done((bf16[128,1152]{1,0:T(8,128)(2,1)S(1)}, bf16[128,1152]{1,0:T(8,128)(2,1)S(1)}, u32[]{:S(2)}, u32[]{:S(2)}) %collective-permute-start.11) | collective-permute-done | bytes 294944 | tf_op jit(solution)/shard_map/ppermute | solution.py:42
  134.5 4.6 all-gather.3.cloned.1.call-done.w_ref
  139.1 5.6 %multiply_convert_fusion.1 = (bf16[256,2176]{1,0:T(8,128)(2,1)S(1)}, f32[256,2176]{1,0:T(8,128)}) fusion(f32[2176]{0:T(1024)S(1)} %get-tuple-element.195, bf16[1152,5120]{1,0:T(8,128)(2,1)} %all-gather.3.cloned.1.call-done.w_ref, bf16[128,1152]{1,0:T(8,128)(2,1)S(1)} %collective-permute-done.12, bf16[128,1152]{1,0:T(8,128)(2,1)S(1)} %add_convert_fusion.2), kind=kOutput, calls=%fused_computation.59 | convolution fusion | flops 1287979008 | bytes 8954368 | tf_op jit(solution)/shard_map/dot_general | solution.py:99
  144.6 4.5 fusion.16
  155.9 12.3 %collective-permute-done.21 = bf16[128,1152]{1,0:T(8,128)(2,1)S(1)} collective-permute-done((bf16[128,1152]{1,0:T(8,128)(2,1)S(1)}, bf16[128,1152]{1,0:T(8,128)(2,1)S(1)}, u32[]{:S(2)}, u32[]{:S(2)}) %collective-permute-start.21) | collective-permute-done | bytes 294944 | tf_op jit(solution)/shard_map/ppermute | solution.py:42
  176.0 11.5 %attend.3 = (bf16[1024,192]{1,0:T(8,128)(2,1)S(1)}, f32[8,1024]{1,0:T(8,128)S(1)}) custom-call(f32[3]{0:T(128)S(1)} %and_convert_fusion.live_ref, s32[1024,1]{1,0:T(8,128)S(1)} %copy-done.33, s32[1,1024]{1,0:T(1,128)S(1)} %bitcast.137, bf16[1024,576]{1,0:T(8,128)(2,1)S(1)} %project.5.qkv_ref), custom_call_target="tpu_custom_call" | custom-call | flops 3221225472 | bytes 1572864 | tf_op jit(solution)/shard_map/attend/pallas_call | solution.py:203
  201.1 10.5 %collective-permute-done.26 = bf16[128,1152]{1,0:T(8,128)(2,1)S(1)} collective-permute-done((bf16[128,1152]{1,0:T(8,128)(2,1)S(1)}, bf16[128,1152]{1,0:T(8,128)(2,1)S(1)}, u32[]{:S(2)}, u32[]{:S(2)}) %collective-permute-start.26) | collective-permute-done | bytes 294944 | tf_op jit(solution)/shard_map/ppermute | solution.py:42
  227.4 5.9 %hidden_grads.2 = bf16[1152,4352]{1,0:T(8,128)(2,1)} custom-call(bf16[256,1152]{1,0:T(8,128)(2,1)S(1)} %pad_maximum_fusion.4.refs_0_, bf16[256,2176]{1,0:T(8,128)(2,1)S(1)} %get-tuple-element.307.refs_1_, bf16[256,1152]{1,0:T(8,128)(2,1)S(1)} %pad_maximum_fusion.5.refs_2_, bf16[256,2176]{1,0:T(8,128)(2,1)S(1)} %get-tuple-element.303.refs_3_), custom_call_target="tpu_custom_call" | custom-call | flops 2566914048 | bytes 10027008 | tf_op jit(solution)/shard_map/hidden_grads/pallas_call | solution.py:366
  246.5 12.5 %collective-permute-done.33 = bf16[128,1152]{1,0:T(8,128)(2,1)S(1)} collective-permute-done((bf16[128,1152]{1,0:T(8,128)(2,1)S(1)}, bf16[128,1152]{1,0:T(8,128)(2,1)S(1)}, u32[]{:S(2)}, u32[]{:S(2)}) %collective-permute-start.33) | collective-permute-done | bytes 294944 | tf_op jit(solution)/shard_map/ppermute | solution.py:42
  265.6 13.5 %attend_back.2.rows_ref.dqkv_ref = bf16[1024,576]{1,0:T(8,128)(2,1)S(1)} custom-call(f32[3]{0:T(128)S(1)} %and_convert_fusion.live_ref, s32[1024,1]{1,0:T(8,128)S(1)} %copy-done.34, s32[1,1024]{1,0:T(1,128)S(1)} %bitcast.138, f32[8,1024]{1,0:T(8,128)S(1)} %get-tuple-element.83.lse_ref, bf16[1024,192]{1,0:T(8,128)(2,1)S(1)} %project.6.dout_ref, ...), custom_call_target="tpu_custom_call" | custom-call | flops 8053063680 | bytes 2752512 | tf_op jit(solution)/shard_map/attend_back/pallas_call | solution.py:226
  293.3 5.9 %head_grads.2.refs_4_ = bf16[1152,768]{1,0:T(8,128)(2,1)} custom-call(bf16[512,1152]{1,0:T(8,128)(2,1)S(1)} %copy-done.6, bf16[512,1152]{1,0:T(8,128)(2,1)} %collective-permute-done.22.other.x1, bf16[512,1152]{1,0:T(8,128)(2,1)S(1)} %pad_maximum_fusion.1.mine.m0, bf16[512,1152]{1,0:T(8,128)(2,1)S(1)} %collective-permute-done.34.other.m1, ...), custom_call_target="tpu_custom_call" | custom-call | flops 1811939328 | bytes 8388608 | tf_op jit(solution)/shard_map/head_grads/pallas_call | solution.py:326
  299.2 7.1 %collective-permute-done.37 = bf16[128,1152]{1,0:T(8,128)(2,1)S(1)} collective-permute-done((bf16[128,1152]{1,0:T(8,128)(2,1)S(1)}, bf16[128,1152]{1,0:T(8,128)(2,1)S(1)}, u32[]{:S(2)}, u32[]{:S(2)}) %collective-permute-start.37) | collective-permute-done | bytes 294944 | tf_op jit(solution)/shard_map/ppermute | solution.py:42
  316.7 6.1 %hidden_grads.3 = bf16[1152,5120]{1,0:T(8,128)(2,1)} custom-call(bf16[256,1152]{1,0:T(8,128)(2,1)S(1)} %pad_maximum_fusion.3.refs_0_, bf16[256,2176]{1,0:T(8,128)(2,1)S(1)} %get-tuple-element.309.refs_1_, bf16[256,1152]{1,0:T(8,128)(2,1)S(1)} %pad_maximum_fusion.6.refs_2_, bf16[256,2176]{1,0:T(8,128)(2,1)S(1)} %copy-done.23, bf16[1152,768]{1,0:T(8,128)(2,1)S(1)} %copy-done.9), custom_call_target="tpu_custom_call" | custom-call | flops 2566914048 | bytes 11796480 | tf_op jit(solution)/shard_map/hidden_grads/pallas_call | solution.py:366
  343.5 8.2 %collective-permute-done.43 = bf16[128,1152]{1,0:T(8,128)(2,1)S(1)} collective-permute-done((bf16[128,1152]{1,0:T(8,128)(2,1)S(1)}, bf16[128,1152]{1,0:T(8,128)(2,1)S(1)}, u32[]{:S(2)}, u32[]{:S(2)}) %collective-permute-start.43) | collective-permute-done | bytes 294944 | tf_op jit(solution)/shard_map/ppermute | solution.py:42
  364.7 13.5 %attend_back.3.rows_ref.dqkv_ref = bf16[1024,576]{1,0:T(8,128)(2,1)S(1)} custom-call(f32[3]{0:T(128)S(1)} %and_convert_fusion.live_ref, s32[1024,1]{1,0:T(8,128)S(1)} %copy-done.35, s32[1,1024]{1,0:T(1,128)S(1)} %bitcast.139, f32[8,1024]{1,0:T(8,128)S(1)} %get-tuple-element.93.lse_ref, bf16[1024,192]{1,0:T(8,128)(2,1)S(1)} %copy-done.31, ...), custom_call_target="tpu_custom_call" | custom-call | flops 8053063680 | bytes 2752512 | tf_op jit(solution)/shard_map/attend_back/pallas_call | solution.py:226
  384.6 4.6 chip_sum.7
  393.4 5.8 %head_grads.3 = bf16[1152,768]{1,0:T(8,128)(2,1)} custom-call(bf16[512,1152]{1,0:T(8,128)(2,1)S(1)} %copy-done.11, bf16[512,1152]{1,0:T(8,128)(2,1)} %collective-permute-done.4.other.x1, bf16[512,1152]{1,0:T(8,128)(2,1)S(1)} %copy-done.8, bf16[512,1152]{1,0:T(8,128)(2,1)S(1)} %copy-done.13, bf16[1024,576]{1,0:T(8,128)(2,1)} %copy-done.4, ...), custom_call_target="tpu_custom_call" | custom-call | flops 1811939328 | bytes 8388608 | tf_op jit(solution)/shard_map/head_grads/pallas_call | solution.py:326
  399.1 5.3 %all-to-all-start.1 = ((bf16[16,72,768]{2,1,0:T(8,128)(2,1)}), bf16[16,72,768]{2,1,0:T(8,128)(2,1)S(1)}, u32[]{:S(2)}, u32[]{:S(2)}) async-start(bf16[16,72,768]{2,1,0:T(8,128)(2,1)} %bitcast.141), calls=%async_computation.1 | async-start | bytes 3538944 | tf_op jit(solution)/shard_map/all_to_all | solution.py:59
  422.8 4.7 fusion.47
  427.5 16.3 %collective-permute-done.58 = f32[20,1152]{1,0:T(8,128)S(1)} collective-permute-done((f32[20,1152]{1,0:T(8,128)S(1)}, f32[20,1152]{1,0:T(8,128)S(1)}, u32[]{:S(2)}, u32[]{:S(2)}) %collective-permute-start.58) | collective-permute-done | bytes 92192 | tf_op jit(solution)/shard_map/ppermute | solution.py:50
  (539 shorter events, 248.8 us)
Async XLA Ops:
  7.2 131.9 %all-gather.3.cloned.1.call-start = ((), (), s32[]{:S(2)}) async-start(), calls=%async_computation.4 | async-start | bytes 12533760 | tf_op jit(solution)/shard_map/all_gather | solution.py:446
  45.5 37.2 %all-to-all-start = ((bf16[16,72,768]{2,1,0:T(8,128)(2,1)}), bf16[16,72,768]{2,1,0:T(8,128)(2,1)S(1)}, u32[]{:S(2)}, u32[]{:S(2)}) async-start(bf16[16,72,768]{2,1,0:T(8,128)(2,1)} %broadcast_in_dim.35), calls=%async_computation | async-start | bytes 3538944 | tf_op jit(solution)/shard_map/all_to_all | solution.py:54
  53.6 165.8 %all-gather.5.cloned.1.call-start = ((), (), s32[]{:S(2)}) async-start(), calls=%async_computation.5 | async-start | bytes 10653696 | tf_op jit(solution)/shard_map/all_gather | solution.py:446
  62.9 25.0 %collective-permute-start.4 = (bf16[512,1152]{1,0:T(8,128)(2,1)S(1)}, bf16[512,1152]{1,0:T(8,128)(2,1)}, u32[]{:S(2)}, u32[]{:S(2)}) collective-permute-start(bf16[512,1152]{1,0:T(8,128)(2,1)S(1)} %constant_dynamic-update-slice_fusion.1.mine.x0), channel_id=1, source_target_pairs={{0,1},{1,0},{2,3},{3,2},{4,5},{5,4},{6,7},{7,6},{8,9},{9,8},{10,11... | collective-permute-start | bytes 3538952 | tf_op jit(solution)/shard_map/ppermute | solution.py:38
  82.8 20.4 %collective-permute-start.5 = (bf16[36,2176]{1,0:T(8,128)(2,1)S(1)}, bf16[36,2176]{1,0:T(8,128)(2,1)S(1)}, u32[]{:S(2)}, u32[]{:S(2)}) collective-permute-start(bf16[36,2176]{1,0:T(8,128)(2,1)S(1)} %fusion.100), channel_id=1, source_target_pairs={{0,4},{1,5},{2,6},{3,7},{4,0},{5,1},{6,2},{7,3},{8,12},{9,13},{10,... | collective-permute-start | bytes 470024 | tf_op jit(solution)/shard_map/ppermute | solution.py:42
  84.5 19.0 %collective-permute-start.7 = (bf16[36,2176]{1,0:T(8,128)(2,1)S(1)}, bf16[36,2176]{1,0:T(8,128)(2,1)S(1)}, u32[]{:S(2)}, u32[]{:S(2)}) collective-permute-start(bf16[36,2176]{1,0:T(8,128)(2,1)S(1)} %fusion.100), channel_id=1, source_target_pairs={{0,6},{1,7},{2,4},{3,5},{4,2},{5,3},{6,0},{7,1},{8,14},{9,15},{10,... | collective-permute-start | bytes 470024 | tf_op jit(solution)/shard_map/ppermute | solution.py:42
  86.6 16.8 %collective-permute-start.6 = (bf16[36,2176]{1,0:T(8,128)(2,1)S(1)}, bf16[36,2176]{1,0:T(8,128)(2,1)S(1)}, u32[]{:S(2)}, u32[]{:S(2)}) collective-permute-start(bf16[36,2176]{1,0:T(8,128)(2,1)S(1)} %fusion.100), channel_id=1, source_target_pairs={{0,2},{1,3},{2,0},{3,1},{4,6},{5,7},{6,4},{7,5},{8,10},{9,11},{10,... | collective-permute-start | bytes 470024 | tf_op jit(solution)/shard_map/ppermute | solution.py:42
  106.4 251.8 %reduce-scatter.8.cloned.1.call-start = ((), (), s32[]{:S(2)}) async-start(), calls=%async_computation.6 | async-start | bytes 10653696
  111.0 16.7 %collective-permute-start.11 = (bf16[128,1152]{1,0:T(8,128)(2,1)S(1)}, bf16[128,1152]{1,0:T(8,128)(2,1)S(1)}, u32[]{:S(2)}, u32[]{:S(2)}) collective-permute-start(bf16[128,1152]{1,0:T(8,128)(2,1)S(1)} %get-tuple-element.72), channel_id=1, source_target_pairs={{0,6},{1,7},{2,4},{3,5},{4,2},{5,3},{6,0},{7,1},{8,14},{9,15},{10,... | collective-permute-start | bytes 884744 | tf_op jit(solution)/shard_map/ppermute | solution.py:42
  151.5 16.7 %collective-permute-start.21 = (bf16[128,1152]{1,0:T(8,128)(2,1)S(1)}, bf16[128,1152]{1,0:T(8,128)(2,1)S(1)}, u32[]{:S(2)}, u32[]{:S(2)}) collective-permute-start(bf16[128,1152]{1,0:T(8,128)(2,1)S(1)} %add_convert_fusion.1), channel_id=1, source_target_pairs={{0,6},{1,7},{2,4},{3,5},{4,2},{5,3},{6,0},{7,1},{8,14},{9,15},{10,... | collective-permute-start | bytes 884744 | tf_op jit(solution)/shard_map/ppermute | solution.py:42
  194.9 16.7 %collective-permute-start.26 = (bf16[128,1152]{1,0:T(8,128)(2,1)S(1)}, bf16[128,1152]{1,0:T(8,128)(2,1)S(1)}, u32[]{:S(2)}, u32[]{:S(2)}) collective-permute-start(bf16[128,1152]{1,0:T(8,128)(2,1)S(1)} %get-tuple-element.81), channel_id=1, source_target_pairs={{0,6},{1,7},{2,4},{3,5},{4,2},{5,3},{6,0},{7,1},{8,14},{9,15},{10,... | collective-permute-start | bytes 884744 | tf_op jit(solution)/shard_map/ppermute | solution.py:42
  234.3 209.6 %reduce-scatter.10.cloned.1.call-start = ((), (), s32[]{:S(2)}) async-start(), calls=%async_computation.7 | async-start | bytes 12533760
  242.3 16.7 %collective-permute-start.33 = (bf16[128,1152]{1,0:T(8,128)(2,1)S(1)}, bf16[128,1152]{1,0:T(8,128)(2,1)S(1)}, u32[]{:S(2)}, u32[]{:S(2)}) collective-permute-start(bf16[128,1152]{1,0:T(8,128)(2,1)S(1)} %get-tuple-element.205), channel_id=1, source_target_pairs={{0,6},{1,7},{2,4},{3,5},{4,2},{5,3},{6,0},{7,1},{8,14},{9,15},{10,... | collective-permute-start | bytes 884744 | tf_op jit(solution)/shard_map/ppermute | solution.py:42
  290.0 16.3 %collective-permute-start.37 = (bf16[128,1152]{1,0:T(8,128)(2,1)S(1)}, bf16[128,1152]{1,0:T(8,128)(2,1)S(1)}, u32[]{:S(2)}, u32[]{:S(2)}) collective-permute-start(bf16[128,1152]{1,0:T(8,128)(2,1)S(1)} %get-tuple-element.87), channel_id=1, source_target_pairs={{0,2},{1,3},{2,0},{3,1},{4,6},{5,7},{6,4},{7,5},{8,10},{9,11},{10,... | collective-permute-start | bytes 884744 | tf_op jit(solution)/shard_map/ppermute | solution.py:42
  335.0 16.6 %collective-permute-start.43 = (bf16[128,1152]{1,0:T(8,128)(2,1)S(1)}, bf16[128,1152]{1,0:T(8,128)(2,1)S(1)}, u32[]{:S(2)}, u32[]{:S(2)}) collective-permute-start(bf16[128,1152]{1,0:T(8,128)(2,1)S(1)} %get-tuple-element.211), channel_id=1, source_target_pairs={{0,6},{1,7},{2,4},{3,5},{4,2},{5,3},{6,0},{7,1},{8,14},{9,15},{10,... | collective-permute-start | bytes 884744 | tf_op jit(solution)/shard_map/ppermute | solution.py:42
  359.8 18.4 %collective-permute-start.47 = (bf16[36,2176]{1,0:T(8,128)(2,1)S(1)}, bf16[36,2176]{1,0:T(8,128)(2,1)S(1)}, u32[]{:S(2)}, u32[]{:S(2)}) collective-permute-start(bf16[36,2176]{1,0:T(8,128)(2,1)S(1)} %pad_maximum_fusion.12), channel_id=1, source_target_pairs={{0,6},{1,7},{2,4},{3,5},{4,2},{5,3},{6,0},{7,1},{8,14},{9,15},{10,... | collective-permute-start | bytes 470024 | tf_op jit(solution)/shard_map/ppermute | solution.py:42
  360.8 17.3 %collective-permute-start.46 = (bf16[36,2176]{1,0:T(8,128)(2,1)S(1)}, bf16[36,2176]{1,0:T(8,128)(2,1)S(1)}, u32[]{:S(2)}, u32[]{:S(2)}) collective-permute-start(bf16[36,2176]{1,0:T(8,128)(2,1)S(1)} %pad_maximum_fusion.11), channel_id=1, source_target_pairs={{0,2},{1,3},{2,0},{3,1},{4,6},{5,7},{6,4},{7,5},{8,10},{9,11},{10,... | collective-permute-start | bytes 470024 | tf_op jit(solution)/shard_map/ppermute | solution.py:42
  389.2 16.6 %collective-permute-start.51 = (bf16[128,1152]{1,0:T(8,128)(2,1)}, bf16[128,1152]{1,0:T(8,128)(2,1)}, u32[]{:S(2)}, u32[]{:S(2)}) collective-permute-start(bf16[128,1152]{1,0:T(8,128)(2,1)} %get-tuple-element.99), channel_id=1, source_target_pairs={{0,6},{1,7},{2,4},{3,5},{4,2},{5,3},{6,0},{7,1},{8,14},{9,15},{10,... | collective-permute-start | bytes 884744 | tf_op jit(solution)/shard_map/ppermute | solution.py:42
  389.5 16.2 %collective-permute-start.50 = (bf16[128,1152]{1,0:T(8,128)(2,1)}, bf16[128,1152]{1,0:T(8,128)(2,1)}, u32[]{:S(2)}, u32[]{:S(2)}) collective-permute-start(bf16[128,1152]{1,0:T(8,128)(2,1)} %get-tuple-element.98), channel_id=1, source_target_pairs={{0,2},{1,3},{2,0},{3,1},{4,6},{5,7},{6,4},{7,5},{8,10},{9,11},{10,... | collective-permute-start | bytes 884744 | tf_op jit(solution)/shard_map/ppermute | solution.py:42
  399.1 44.8 %all-to-all-start.1 = ((bf16[16,72,768]{2,1,0:T(8,128)(2,1)}), bf16[16,72,768]{2,1,0:T(8,128)(2,1)S(1)}, u32[]{:S(2)}, u32[]{:S(2)}) async-start(bf16[16,72,768]{2,1,0:T(8,128)(2,1)} %bitcast.141), calls=%async_computation.1 | async-start | bytes 3538944 | tf_op jit(solution)/shard_map/all_to_all | solution.py:59
  418.4 25.5 %collective-permute-start.58 = (f32[20,1152]{1,0:T(8,128)S(1)}, f32[20,1152]{1,0:T(8,128)S(1)}, u32[]{:S(2)}, u32[]{:S(2)}) collective-permute-start(f32[20,1152]{1,0:T(8,128)S(1)} %pad_maximum_fusion.22), channel_id=1, source_target_pairs={{0,16},{8,24},{16,0},{24,8},{32,48},{40,56},{48,32},{56,40},{64,80... | collective-permute-start | bytes 276488 | tf_op jit(solution)/shard_map/ppermute | solution.py:50
  421.5 22.4 %collective-permute-start.59 = (f32[20,1152]{1,0:T(8,128)S(1)}, f32[20,1152]{1,0:T(8,128)S(1)}, u32[]{:S(2)}, u32[]{:S(2)}) collective-permute-start(f32[20,1152]{1,0:T(8,128)S(1)} %pad_maximum_fusion.22), channel_id=1, source_target_pairs={{0,24},{8,16},{16,8},{24,0},{32,56},{40,48},{48,40},{56,32},{64,88... | collective-permute-start | bytes 276488 | tf_op jit(solution)/shard_map/ppermute | solution.py:50
  422.6 21.3 %collective-permute-start.57 = (f32[20,1152]{1,0:T(8,128)S(1)}, f32[20,1152]{1,0:T(8,128)S(1)}, u32[]{:S(2)}, u32[]{:S(2)}) collective-permute-start(f32[20,1152]{1,0:T(8,128)S(1)} %pad_maximum_fusion.22), channel_id=1, source_target_pairs={{0,8},{8,0},{16,24},{24,16},{32,40},{40,32},{48,56},{56,48},{64,72... | collective-permute-start | bytes 276488 | tf_op jit(solution)/shard_map/ppermute | solution.py:50
  443.9 16.8 %collective-permute-start.61 = (f32[20,1152]{1,0:T(8,128)S(1)}, f32[20,1152]{1,0:T(8,128)S(1)}, u32[]{:S(2)}, u32[]{:S(2)}) collective-permute-start(f32[20,1152]{1,0:T(8,128)S(1)} %add_add_fusion.6), channel_id=1, source_target_pairs={{0,64},{8,72},{16,80},{24,88},{32,96},{40,104},{48,112},{56,120},{... | collective-permute-start | bytes 276488 | tf_op jit(solution)/shard_map/ppermute | solution.py:50
  (125 other events, 1128.4 us)
Sparse Core Ops, SparseCore 0:
  32.8 106.1 all-gather.2
  141.2 78.1 all-gather.4
  234.4 91.7 reduce-scatter.7
  330.0 112.9 reduce-scatter.9

commit v5 on v4

--- a/solution.py
+++ b/solution.py
@@ -445,15 +445,17 @@
     def fetch(pack):
         return lax.all_gather(pack, "shard", axis=0, tiled=True)
 
-    w_fc_a, w_down_a, w_qkv_a, w_out_a = lax.optimization_barrier(
-        (w_fc[0], w_down[0].T, w_qkv[0, 0], w_out[0, 0])
-    )
-    pack_a = exchanged(head_halves(w_qkv_a, w_out_a))
-    w_qkv_b, w_out_b, pack_a = lax.optimization_barrier((w_qkv[1, 0], w_out[1, 0], pack_a))
+    w_fc_a, w_down_a, w_qkv_b, w_out_b = lax.optimization_barrier(
+        (w_fc[0], w_down[0].T, w_qkv[1, 0], w_out[1, 0])
+    )
     hidden_a = exchanged_hidden(w_fc_a, w_down_a)
     heads_b = exchanged(head_halves(w_qkv_b, w_out_b))
+    joined, w_qkv_a, w_out_a = lax.optimization_barrier(
+        (jnp.concatenate([heads_b, hidden_a], axis=1), w_qkv[0, 0], w_out[0, 0])
+    )
+    fetched_a = fetch(joined)
+    pack_a = exchanged(head_halves(w_qkv_a, w_out_a))
     copies = jnp.broadcast_to(pack_a, (SHARDS, *pack_a.shape))
-    fetched_a = fetch(jnp.concatenate([heads_b, hidden_a], axis=1))
     weights = [
         (None, fetched_a[:, HW : HW + FC], fetched_a[:, HW + FC :]),
         (fetched_a, None, None),
@@ -624,6 +626,10 @@
         (sums, head_sum_a, hidden_sums[0])
     )
     sums = sum_shards(sums, 4)
+    head_sums = jnp.concatenate(
+        [jnp.sum(head_sum_a.astype(F32), axis=0).astype(BF), hidden_sums[0][:, 2 * FC :]], axis=1
+    )
+    sums, head_sums = lax.optimization_barrier((sums, head_sums))
     vectors = narrow(sums[:12]).reshape(LAYERS, 6, D)
     fc_sum = sums[12:16].reshape(LAYERS, 2 * DP)
     fc_sum = jnp.where(high, fc_sum[:, FR : 2 * FR], fc_sum[:, :FR])
@@ -639,11 +645,11 @@
             jnp.where(first, recv, keep)[:CHUNK].astype(F32),
         )
 
-    head_sums = [jnp.sum(head_sum_a.astype(F32), axis=0).astype(BF), hidden_sums[0][:, 2 * FC :]]
+    halves = own_features(head_sums)
     hidden_own[0] = own_hidden(hidden_sums[0][:, : 2 * FC])
     grads = [[], [], [], []]
     for l in range(LAYERS):
-        a, b = own_features(head_sums[l])
+        a, b = [v[:, l * HW : (l + 1) * HW] for v in halves]
         qkv = jnp.concatenate([a[:, : 3 * QW], b[:, : 2 * QW]], axis=1).reshape(CHUNK, 5, 3 * HD)
         grads[0].append(jnp.moveaxis(qkv, 1, 0))
         outs = jnp.concatenate([a[:, 3 * QW :], b[:, 3 * QW : 3 * QW + 2 * HD]], axis=1)

time: 486 us -> 478 us (0.984)
  waiting for transfers between devices: 156 us -> 151 us
    all_to_all x1, waiting for transfers between devices: 15.2 us -> 9.68 us  [gather_shards(): lax.all_to_all(copies, 'shard', 0, 0, tiled=True)]
    unnamed x165 -> x167, local copies, waits for them, and re-layouts: 18.6 us -> 19.1 us
  transfers between devices with their start and end apart: 74 -> 73, of which waited for: 40 -> 43; matrix products, arithmetic and copies ran while one was open for 19% -> 20% of each run, Pallas kernels for 19% -> 19%
where the time goes in v5:
time: 478 us; the launch traced here: 470 us
  waiting for transfers between devices  151 us (32%)
  Pallas kernels  95.4 us (20%)
  starting transfers between devices  87.9 us (18%)
  matrix products  54.7 us (11%)
  local copies, waits for them, and re-layouts  37.9 us (8%)
  other arithmetic  24.2 us (5%)
  between operations  18.9 us (4%)
    ppermute x40, waiting for transfers between devices, swap_x(): return lax.ppermute(v, LINE, line_perm(lambda x, k: (x ^ m, k)))  88.2 us
    ppermute x40, starting transfers between devices, swap_x(): return lax.ppermute(v, LINE, line_perm(lambda x, k: (x ^ m, k)))  59.7 us
    dot_general x12, matrix products, dot(): return lax.dot_general(a, b, (dims, ((), ())), preferred_element_type=F32)  41.1 us
    pallas_call x2, Pallas kernels, attend_backward(): pl.pallas_call(attend_back_body, grid=(LINE_ROWS // Q_ROWS,), in_specs=at...  26.3 us
    ppermute x17, waiting for transfers between devices, swap_core(): return lax.ppermute(v, LINE, line_perm(lambda x, k: (x, 1 - k)))  24.2 us
    pallas_call x2, Pallas kernels, attend_forward(): pl.pallas_call(attend_body, grid=(LINE_ROWS // Q_ROWS,), in_specs=attend_...  22.8 us
    unnamed x167, local copies, waits for them, and re-layouts  19.1 us
    ppermute x6, waiting for transfers between devices, swap_shard(): return lax.ppermute(v, 'shard', [(i, i ^ m) for i in range(SHARDS)])  14.2 us
  transfers between devices with their start and end apart: 73, of which 43 were waited for; matrix products, arithmetic and copies ran while one was open for 20% of the time, Pallas kernels for 19%

profile of v5, /device:TPU:0, one launch (start us, length us, event | category | flops | bytes accessed | tf_op | source)
XLA Modules:
  0.0 469.7 jit_solution(14510839637197890742)
XLA Ops:
  46.1 8.0 %all-to-all-start = ((bf16[16,72,768]{2,1,0:T(8,128)(2,1)}), bf16[16,72,768]{2,1,0:T(8,128)(2,1)S(1)}, u32[]{:S(2)}, u32[]{:S(2)}) async-start(bf16[16,72,768]{2,1,0:T(8,128)(2,1)} %broadcast_in_dim.35), calls=%async_computation | async-start | bytes 3538944 | tf_op jit(solution)/shard_map/all_to_all | solution.py:54
  58.5 4.9 %collective-permute-done.7 = bf16[128,1152]{1,0:T(8,128)(2,1)S(1)} collective-permute-done((bf16[128,1152]{1,0:T(8,128)(2,1)}, bf16[128,1152]{1,0:T(8,128)(2,1)S(1)}, u32[]{:S(2)}, u32[]{:S(2)}) %collective-permute-start.7) | collective-permute-done | bytes 294944 | tf_op jit(solution)/shard_map/ppermute | solution.py:42
  68.1 9.7 %all-to-all-done = bf16[16,72,768]{2,1,0:T(8,128)(2,1)S(1)} async-done(((bf16[16,72,768]{2,1,0:T(8,128)(2,1)}), bf16[16,72,768]{2,1,0:T(8,128)(2,1)S(1)}, u32[]{:S(2)}, u32[]{:S(2)}) %all-to-all-start) | async-done | bytes 1769504 | tf_op jit(solution)/shard_map/all_to_all | solution.py:54
  86.7 11.4 %attend.2 = (bf16[1024,192]{1,0:T(8,128)(2,1)S(1)}, f32[8,1024]{1,0:T(8,128)S(1)}) custom-call(f32[3]{0:T(128)S(1)} %and_convert_fusion.live_ref, s32[1024,1]{1,0:T(8,128)S(1)} %copy-done.32, s32[1,1024]{1,0:T(1,128)S(1)} %bitcast.136, bf16[1024,576]{1,0:T(8,128)(2,1)S(1)} %project.4.qkv_ref), custom_call_target="tpu_custom_call" | custom-call | flops 3221225472 | bytes 1572864 | tf_op jit(solution)/shard_map/attend/pallas_call | solution.py:203
  111.1 11.5 %collective-permute-done.15 = bf16[128,1152]{1,0:T(8,128)(2,1)S(1)} collective-permute-done((bf16[128,1152]{1,0:T(8,128)(2,1)S(1)}, bf16[128,1152]{1,0:T(8,128)(2,1)S(1)}, u32[]{:S(2)}, u32[]{:S(2)}) %collective-permute-start.15) | collective-permute-done | bytes 294944 | tf_op jit(solution)/shard_map/ppermute | solution.py:42
  133.9 5.5 %multiply_convert_fusion.1 = (bf16[256,2176]{1,0:T(8,128)(2,1)S(1)}, f32[256,2176]{1,0:T(8,128)}) fusion(f32[2176]{0:T(1024)S(1)} %get-tuple-element.199, bf16[1152,5120]{1,0:T(8,128)(2,1)} %all-gather.3.cloned.1.call-done.w_ref, bf16[128,1152]{1,0:T(8,128)(2,1)S(1)} %collective-permute-done.16, bf16[128,1152]{1,0:T(8,128)(2,1)S(1)} %add_convert_fusion.2), kind=kOutput, calls=%fused_computation.59 | convolution fusion | flops 1287979008 | bytes 8954368 | tf_op jit(solution)/shard_map/dot_general | solution.py:99
  139.4 4.5 fusion.16
  150.7 12.3 %collective-permute-done.21 = bf16[128,1152]{1,0:T(8,128)(2,1)S(1)} collective-permute-done((bf16[128,1152]{1,0:T(8,128)(2,1)S(1)}, bf16[128,1152]{1,0:T(8,128)(2,1)S(1)}, u32[]{:S(2)}, u32[]{:S(2)}) %collective-permute-start.21) | collective-permute-done | bytes 294944 | tf_op jit(solution)/shard_map/ppermute | solution.py:42
  170.8 11.4 %attend.3 = (bf16[1024,192]{1,0:T(8,128)(2,1)S(1)}, f32[8,1024]{1,0:T(8,128)S(1)}) custom-call(f32[3]{0:T(128)S(1)} %and_convert_fusion.live_ref, s32[1024,1]{1,0:T(8,128)S(1)} %copy-done.33, s32[1,1024]{1,0:T(1,128)S(1)} %bitcast.137, bf16[1024,576]{1,0:T(8,128)(2,1)S(1)} %project.5.qkv_ref), custom_call_target="tpu_custom_call" | custom-call | flops 3221225472 | bytes 1572864 | tf_op jit(solution)/shard_map/attend/pallas_call | solution.py:203
  195.8 10.6 %collective-permute-done.26 = bf16[128,1152]{1,0:T(8,128)(2,1)S(1)} collective-permute-done((bf16[128,1152]{1,0:T(8,128)(2,1)S(1)}, bf16[128,1152]{1,0:T(8,128)(2,1)S(1)}, u32[]{:S(2)}, u32[]{:S(2)}) %collective-permute-start.26) | collective-permute-done | bytes 294944 | tf_op jit(solution)/shard_map/ppermute | solution.py:42
  222.2 5.9 %hidden_grads.2 = bf16[1152,4352]{1,0:T(8,128)(2,1)} custom-call(bf16[256,1152]{1,0:T(8,128)(2,1)S(1)} %pad_maximum_fusion.4.refs_0_, bf16[256,2176]{1,0:T(8,128)(2,1)S(1)} %get-tuple-element.315.refs_1_, bf16[256,1152]{1,0:T(8,128)(2,1)S(1)} %pad_maximum_fusion.5.refs_2_, bf16[256,2176]{1,0:T(8,128)(2,1)S(1)} %get-tuple-element.312.refs_3_), custom_call_target="tpu_custom_call" | custom-call | flops 2566914048 | bytes 10027008 | tf_op jit(solution)/shard_map/hidden_grads/pallas_call | solution.py:366
  241.2 12.5 %collective-permute-done.33 = bf16[128,1152]{1,0:T(8,128)(2,1)S(1)} collective-permute-done((bf16[128,1152]{1,0:T(8,128)(2,1)S(1)}, bf16[128,1152]{1,0:T(8,128)(2,1)S(1)}, u32[]{:S(2)}, u32[]{:S(2)}) %collective-permute-start.33) | collective-permute-done | bytes 294944 | tf_op jit(solution)/shard_map/ppermute | solution.py:42
  260.4 13.2 %attend_back.2.rows_ref.dqkv_ref = bf16[1024,576]{1,0:T(8,128)(2,1)S(1)} custom-call(f32[3]{0:T(128)S(1)} %and_convert_fusion.live_ref, s32[1024,1]{1,0:T(8,128)S(1)} %copy-done.34, s32[1,1024]{1,0:T(1,128)S(1)} %bitcast.138, f32[8,1024]{1,0:T(8,128)S(1)} %get-tuple-element.85.lse_ref, bf16[1024,192]{1,0:T(8,128)(2,1)S(1)} %project.6.dout_ref, ...), custom_call_target="tpu_custom_call" | custom-call | flops 8053063680 | bytes 2752512 | tf_op jit(solution)/shard_map/attend_back/pallas_call | solution.py:226
  287.7 5.8 %head_grads.2.refs_4_ = bf16[1152,768]{1,0:T(8,128)(2,1)} custom-call(bf16[512,1152]{1,0:T(8,128)(2,1)S(1)} %copy-done.6, bf16[512,1152]{1,0:T(8,128)(2,1)} %collective-permute-done.22.other.x1, bf16[512,1152]{1,0:T(8,128)(2,1)S(1)} %pad_maximum_fusion.1.mine.m0, bf16[512,1152]{1,0:T(8,128)(2,1)S(1)} %collective-permute-done.34.other.m1, ...), custom_call_target="tpu_custom_call" | custom-call | flops 1811939328 | bytes 8388608 | tf_op jit(solution)/shard_map/head_grads/pallas_call | solution.py:326
  293.6 7.2 %collective-permute-done.37 = bf16[128,1152]{1,0:T(8,128)(2,1)S(1)} collective-permute-done((bf16[128,1152]{1,0:T(8,128)(2,1)S(1)}, bf16[128,1152]{1,0:T(8,128)(2,1)S(1)}, u32[]{:S(2)}, u32[]{:S(2)}) %collective-permute-start.37) | collective-permute-done | bytes 294944 | tf_op jit(solution)/shard_map/ppermute | solution.py:42
  311.1 6.1 %hidden_grads.3 = bf16[1152,5120]{1,0:T(8,128)(2,1)} custom-call(bf16[256,1152]{1,0:T(8,128)(2,1)S(1)} %pad_maximum_fusion.3.refs_0_, bf16[256,2176]{1,0:T(8,128)(2,1)S(1)} %get-tuple-element.317.refs_1_, bf16[256,1152]{1,0:T(8,128)(2,1)S(1)} %pad_maximum_fusion.6.refs_2_, bf16[256,2176]{1,0:T(8,128)(2,1)S(1)} %copy-done.23, bf16[1152,768]{1,0:T(8,128)(2,1)S(1)} %copy-done.9), custom_call_target="tpu_custom_call" | custom-call | flops 2566914048 | bytes 11796480 | tf_op jit(solution)/shard_map/hidden_grads/pallas_call | solution.py:366
  333.4 4.5 fusion.8
  338.2 7.8 %collective-permute-done.43 = bf16[128,1152]{1,0:T(8,128)(2,1)S(1)} collective-permute-done((bf16[128,1152]{1,0:T(8,128)(2,1)S(1)}, bf16[128,1152]{1,0:T(8,128)(2,1)S(1)}, u32[]{:S(2)}, u32[]{:S(2)}) %collective-permute-start.43) | collective-permute-done | bytes 294944 | tf_op jit(solution)/shard_map/ppermute | solution.py:42
  359.0 13.2 %attend_back.3.rows_ref.dqkv_ref = bf16[1024,576]{1,0:T(8,128)(2,1)S(1)} custom-call(f32[3]{0:T(128)S(1)} %and_convert_fusion.live_ref, s32[1024,1]{1,0:T(8,128)S(1)} %copy-done.35, s32[1,1024]{1,0:T(1,128)S(1)} %bitcast.139, f32[8,1024]{1,0:T(8,128)S(1)} %get-tuple-element.95.lse_ref, bf16[1024,192]{1,0:T(8,128)(2,1)S(1)} %copy-done.31, ...), custom_call_target="tpu_custom_call" | custom-call | flops 8053063680 | bytes 2752512 | tf_op jit(solution)/shard_map/attend_back/pallas_call | solution.py:226
  378.7 4.7 chip_sum.7
  387.5 5.8 %head_grads.3 = bf16[1152,768]{1,0:T(8,128)(2,1)} custom-call(bf16[512,1152]{1,0:T(8,128)(2,1)S(1)} %copy-done.11, bf16[512,1152]{1,0:T(8,128)(2,1)} %collective-permute-done.8.other.x1, bf16[512,1152]{1,0:T(8,128)(2,1)S(1)} %copy-done.8, bf16[512,1152]{1,0:T(8,128)(2,1)S(1)} %copy-done.13, bf16[1024,576]{1,0:T(8,128)(2,1)} %copy-done.4, ...), custom_call_target="tpu_custom_call" | custom-call | flops 1811939328 | bytes 8388608 | tf_op jit(solution)/shard_map/head_grads/pallas_call | solution.py:326
  393.3 5.4 %all-to-all-start.1 = ((bf16[16,72,768]{2,1,0:T(8,128)(2,1)}), bf16[16,72,768]{2,1,0:T(8,128)(2,1)S(1)}, u32[]{:S(2)}, u32[]{:S(2)}) async-start(bf16[16,72,768]{2,1,0:T(8,128)(2,1)} %bitcast.141), calls=%async_computation.1 | async-start | bytes 3538944 | tf_op jit(solution)/shard_map/all_to_all | solution.py:59
  416.8 4.7 fusion.47
  421.5 13.7 %collective-permute-done.58 = f32[20,1152]{1,0:T(8,128)S(1)} collective-permute-done((f32[20,1152]{1,0:T(8,128)S(1)}, f32[20,1152]{1,0:T(8,128)S(1)}, u32[]{:S(2)}, u32[]{:S(2)}) %collective-permute-start.58) | collective-permute-done | bytes 92192 | tf_op jit(solution)/shard_map/ppermute | solution.py:50
  (535 shorter events, 250.5 us)
Async XLA Ops:
  7.2 126.7 %all-gather.3.cloned.1.call-start = ((), (), s32[]{:S(2)}) async-start(), calls=%async_computation.4 | async-start | bytes 12533760 | tf_op jit(solution)/shard_map/all_gather | solution.py:446
  46.1 31.7 %all-to-all-start = ((bf16[16,72,768]{2,1,0:T(8,128)(2,1)}), bf16[16,72,768]{2,1,0:T(8,128)(2,1)S(1)}, u32[]{:S(2)}, u32[]{:S(2)}) async-start(bf16[16,72,768]{2,1,0:T(8,128)(2,1)} %broadcast_in_dim.35), calls=%async_computation | async-start | bytes 3538944 | tf_op jit(solution)/shard_map/all_to_all | solution.py:54
  54.2 160.1 %all-gather.5.cloned.1.call-start = ((), (), s32[]{:S(2)}) async-start(), calls=%async_computation.5 | async-start | bytes 10653696 | tf_op jit(solution)/shard_map/all_gather | solution.py:446
  63.5 19.4 %collective-permute-start.8 = (bf16[512,1152]{1,0:T(8,128)(2,1)S(1)}, bf16[512,1152]{1,0:T(8,128)(2,1)}, u32[]{:S(2)}, u32[]{:S(2)}) collective-permute-start(bf16[512,1152]{1,0:T(8,128)(2,1)S(1)} %constant_dynamic-update-slice_fusion.1.mine.x0), channel_id=1, source_target_pairs={{0,1},{1,0},{2,3},{3,2},{4,5},{5,4},{6,7},{7,6},{8,9},{9,8},{10,11... | collective-permute-start | bytes 3538952 | tf_op jit(solution)/shard_map/ppermute | solution.py:38
  77.9 20.3 %collective-permute-start.9 = (bf16[36,2176]{1,0:T(8,128)(2,1)S(1)}, bf16[36,2176]{1,0:T(8,128)(2,1)S(1)}, u32[]{:S(2)}, u32[]{:S(2)}) collective-permute-start(bf16[36,2176]{1,0:T(8,128)(2,1)S(1)} %fusion.101), channel_id=1, source_target_pairs={{0,4},{1,5},{2,6},{3,7},{4,0},{5,1},{6,2},{7,3},{8,12},{9,13},{10,... | collective-permute-start | bytes 470024 | tf_op jit(solution)/shard_map/ppermute | solution.py:42
  79.7 18.7 %collective-permute-start.11 = (bf16[36,2176]{1,0:T(8,128)(2,1)S(1)}, bf16[36,2176]{1,0:T(8,128)(2,1)S(1)}, u32[]{:S(2)}, u32[]{:S(2)}) collective-permute-start(bf16[36,2176]{1,0:T(8,128)(2,1)S(1)} %fusion.101), channel_id=1, source_target_pairs={{0,6},{1,7},{2,4},{3,5},{4,2},{5,3},{6,0},{7,1},{8,14},{9,15},{10,... | collective-permute-start | bytes 470024 | tf_op jit(solution)/shard_map/ppermute | solution.py:42
  82.1 16.4 %collective-permute-start.10 = (bf16[36,2176]{1,0:T(8,128)(2,1)S(1)}, bf16[36,2176]{1,0:T(8,128)(2,1)S(1)}, u32[]{:S(2)}, u32[]{:S(2)}) collective-permute-start(bf16[36,2176]{1,0:T(8,128)(2,1)S(1)} %fusion.101), channel_id=1, source_target_pairs={{0,2},{1,3},{2,0},{3,1},{4,6},{5,7},{6,4},{7,5},{8,10},{9,11},{10,... | collective-permute-start | bytes 470024 | tf_op jit(solution)/shard_map/ppermute | solution.py:42
  101.4 251.2 %reduce-scatter.8.cloned.1.call-start = ((), (), s32[]{:S(2)}) async-start(), calls=%async_computation.6 | async-start | bytes 10653696
  105.9 16.7 %collective-permute-start.15 = (bf16[128,1152]{1,0:T(8,128)(2,1)S(1)}, bf16[128,1152]{1,0:T(8,128)(2,1)S(1)}, u32[]{:S(2)}, u32[]{:S(2)}) collective-permute-start(bf16[128,1152]{1,0:T(8,128)(2,1)S(1)} %get-tuple-element.77), channel_id=1, source_target_pairs={{0,6},{1,7},{2,4},{3,5},{4,2},{5,3},{6,0},{7,1},{8,14},{9,15},{10,... | collective-permute-start | bytes 884744 | tf_op jit(solution)/shard_map/ppermute | solution.py:42
  146.4 16.7 %collective-permute-start.21 = (bf16[128,1152]{1,0:T(8,128)(2,1)S(1)}, bf16[128,1152]{1,0:T(8,128)(2,1)S(1)}, u32[]{:S(2)}, u32[]{:S(2)}) collective-permute-start(bf16[128,1152]{1,0:T(8,128)(2,1)S(1)} %add_convert_fusion.1), channel_id=1, source_target_pairs={{0,6},{1,7},{2,4},{3,5},{4,2},{5,3},{6,0},{7,1},{8,14},{9,15},{10,... | collective-permute-start | bytes 884744 | tf_op jit(solution)/shard_map/ppermute | solution.py:42
  189.6 16.7 %collective-permute-start.26 = (bf16[128,1152]{1,0:T(8,128)(2,1)S(1)}, bf16[128,1152]{1,0:T(8,128)(2,1)S(1)}, u32[]{:S(2)}, u32[]{:S(2)}) collective-permute-start(bf16[128,1152]{1,0:T(8,128)(2,1)S(1)} %get-tuple-element.83), channel_id=1, source_target_pairs={{0,6},{1,7},{2,4},{3,5},{4,2},{5,3},{6,0},{7,1},{8,14},{9,15},{10,... | collective-permute-start | bytes 884744 | tf_op jit(solution)/shard_map/ppermute | solution.py:42
  229.1 208.9 %reduce-scatter.10.cloned.1.call-start = ((), (), s32[]{:S(2)}) async-start(), calls=%async_computation.7 | async-start | bytes 12533760
  237.1 16.7 %collective-permute-start.33 = (bf16[128,1152]{1,0:T(8,128)(2,1)S(1)}, bf16[128,1152]{1,0:T(8,128)(2,1)S(1)}, u32[]{:S(2)}, u32[]{:S(2)}) collective-permute-start(bf16[128,1152]{1,0:T(8,128)(2,1)S(1)} %get-tuple-element.209), channel_id=1, source_target_pairs={{0,6},{1,7},{2,4},{3,5},{4,2},{5,3},{6,0},{7,1},{8,14},{9,15},{10,... | collective-permute-start | bytes 884744 | tf_op jit(solution)/shard_map/ppermute | solution.py:42
  284.5 16.3 %collective-permute-start.37 = (bf16[128,1152]{1,0:T(8,128)(2,1)S(1)}, bf16[128,1152]{1,0:T(8,128)(2,1)S(1)}, u32[]{:S(2)}, u32[]{:S(2)}) collective-permute-start(bf16[128,1152]{1,0:T(8,128)(2,1)S(1)} %get-tuple-element.89), channel_id=1, source_target_pairs={{0,2},{1,3},{2,0},{3,1},{4,6},{5,7},{6,4},{7,5},{8,10},{9,11},{10,... | collective-permute-start | bytes 884744 | tf_op jit(solution)/shard_map/ppermute | solution.py:42
  287.2 16.2 %collective-permute-start.38 = (bf16[128,1152]{1,0:T(8,128)(2,1)S(1)}, bf16[128,1152]{1,0:T(8,128)(2,1)S(1)}, u32[]{:S(2)}, u32[]{:S(2)}) collective-permute-start(bf16[128,1152]{1,0:T(8,128)(2,1)S(1)} %get-tuple-element.90), channel_id=1, source_target_pairs={{0,6},{1,7},{2,4},{3,5},{4,2},{5,3},{6,0},{7,1},{8,14},{9,15},{10,... | collective-permute-start | bytes 884744 | tf_op jit(solution)/shard_map/ppermute | solution.py:42
  329.3 16.7 %collective-permute-start.43 = (bf16[128,1152]{1,0:T(8,128)(2,1)S(1)}, bf16[128,1152]{1,0:T(8,128)(2,1)S(1)}, u32[]{:S(2)}, u32[]{:S(2)}) collective-permute-start(bf16[128,1152]{1,0:T(8,128)(2,1)S(1)} %get-tuple-element.215), channel_id=1, source_target_pairs={{0,6},{1,7},{2,4},{3,5},{4,2},{5,3},{6,0},{7,1},{8,14},{9,15},{10,... | collective-permute-start | bytes 884744 | tf_op jit(solution)/shard_map/ppermute | solution.py:42
  354.2 18.1 %collective-permute-start.47 = (bf16[36,2176]{1,0:T(8,128)(2,1)S(1)}, bf16[36,2176]{1,0:T(8,128)(2,1)S(1)}, u32[]{:S(2)}, u32[]{:S(2)}) collective-permute-start(bf16[36,2176]{1,0:T(8,128)(2,1)S(1)} %pad_maximum_fusion.13), channel_id=1, source_target_pairs={{0,6},{1,7},{2,4},{3,5},{4,2},{5,3},{6,0},{7,1},{8,14},{9,15},{10,... | collective-permute-start | bytes 470024 | tf_op jit(solution)/shard_map/ppermute | solution.py:42
  355.0 17.3 %collective-permute-start.46 = (bf16[36,2176]{1,0:T(8,128)(2,1)S(1)}, bf16[36,2176]{1,0:T(8,128)(2,1)S(1)}, u32[]{:S(2)}, u32[]{:S(2)}) collective-permute-start(bf16[36,2176]{1,0:T(8,128)(2,1)S(1)} %pad_maximum_fusion.12), channel_id=1, source_target_pairs={{0,2},{1,3},{2,0},{3,1},{4,6},{5,7},{6,4},{7,5},{8,10},{9,11},{10,... | collective-permute-start | bytes 470024 | tf_op jit(solution)/shard_map/ppermute | solution.py:42
  383.4 16.5 %collective-permute-start.51 = (bf16[128,1152]{1,0:T(8,128)(2,1)}, bf16[128,1152]{1,0:T(8,128)(2,1)}, u32[]{:S(2)}, u32[]{:S(2)}) collective-permute-start(bf16[128,1152]{1,0:T(8,128)(2,1)} %get-tuple-element.101), channel_id=1, source_target_pairs={{0,6},{1,7},{2,4},{3,5},{4,2},{5,3},{6,0},{7,1},{8,14},{9,15},{10,... | collective-permute-start | bytes 884744 | tf_op jit(solution)/shard_map/ppermute | solution.py:42
  383.4 16.4 %collective-permute-start.50 = (bf16[128,1152]{1,0:T(8,128)(2,1)}, bf16[128,1152]{1,0:T(8,128)(2,1)}, u32[]{:S(2)}, u32[]{:S(2)}) collective-permute-start(bf16[128,1152]{1,0:T(8,128)(2,1)} %get-tuple-element.100), channel_id=1, source_target_pairs={{0,2},{1,3},{2,0},{3,1},{4,6},{5,7},{6,4},{7,5},{8,10},{9,11},{10,... | collective-permute-start | bytes 884744 | tf_op jit(solution)/shard_map/ppermute | solution.py:42
  393.3 44.7 %all-to-all-start.1 = ((bf16[16,72,768]{2,1,0:T(8,128)(2,1)}), bf16[16,72,768]{2,1,0:T(8,128)(2,1)S(1)}, u32[]{:S(2)}, u32[]{:S(2)}) async-start(bf16[16,72,768]{2,1,0:T(8,128)(2,1)} %bitcast.141), calls=%async_computation.1 | async-start | bytes 3538944 | tf_op jit(solution)/shard_map/all_to_all | solution.py:59
  412.4 22.8 %collective-permute-start.58 = (f32[20,1152]{1,0:T(8,128)S(1)}, f32[20,1152]{1,0:T(8,128)S(1)}, u32[]{:S(2)}, u32[]{:S(2)}) collective-permute-start(f32[20,1152]{1,0:T(8,128)S(1)} %pad_maximum_fusion.23), channel_id=1, source_target_pairs={{0,16},{8,24},{16,0},{24,8},{32,48},{40,56},{48,32},{56,40},{64,80... | collective-permute-start | bytes 276488 | tf_op jit(solution)/shard_map/ppermute | solution.py:50
  415.4 19.8 %collective-permute-start.59 = (f32[20,1152]{1,0:T(8,128)S(1)}, f32[20,1152]{1,0:T(8,128)S(1)}, u32[]{:S(2)}, u32[]{:S(2)}) collective-permute-start(f32[20,1152]{1,0:T(8,128)S(1)} %pad_maximum_fusion.23), channel_id=1, source_target_pairs={{0,24},{8,16},{16,8},{24,0},{32,56},{40,48},{48,40},{56,32},{64,88... | collective-permute-start | bytes 276488 | tf_op jit(solution)/shard_map/ppermute | solution.py:50
  416.6 19.1 %collective-permute-start.57 = (f32[20,1152]{1,0:T(8,128)S(1)}, f32[20,1152]{1,0:T(8,128)S(1)}, u32[]{:S(2)}, u32[]{:S(2)}) collective-permute-start(f32[20,1152]{1,0:T(8,128)S(1)} %pad_maximum_fusion.23), channel_id=1, source_target_pairs={{0,8},{8,0},{16,24},{24,16},{32,40},{40,32},{48,56},{56,48},{64,72... | collective-permute-start | bytes 276488 | tf_op jit(solution)/shard_map/ppermute | solution.py:50
  (125 other events, 1094.3 us)
Sparse Core Ops, SparseCore 0:
  27.8 106.0 all-gather.2
  136.0 78.1 all-gather.4
  229.2 92.4 reduce-scatter.7
  325.5 112.5 reduce-scatter.9

commit v6 on v5

--- a/solution.py
+++ b/solution.py
@@ -445,11 +445,8 @@
     def fetch(pack):
         return lax.all_gather(pack, "shard", axis=0, tiled=True)
 
-    w_fc_a, w_down_a, w_qkv_b, w_out_b = lax.optimization_barrier(
-        (w_fc[0], w_down[0].T, w_qkv[1, 0], w_out[1, 0])
-    )
-    hidden_a = exchanged_hidden(w_fc_a, w_down_a)
-    heads_b = exchanged(head_halves(w_qkv_b, w_out_b))
+    hidden_a = exchanged_hidden(w_fc[0], w_down[0].T)
+    heads_b = exchanged(head_halves(w_qkv[1, 0], w_out[1, 0]))
     joined, w_qkv_a, w_out_a = lax.optimization_barrier(
         (jnp.concatenate([heads_b, hidden_a], axis=1), w_qkv[0, 0], w_out[0, 0])
     )
@@ -550,7 +547,8 @@
             )
 
         came = [swap_x(piece(theirs if m % 2 else mine, m // 2), m).astype(F32) for m in (1, 2, 3)]
-        return ((piece(mine, 0).astype(F32) + came[0]) + (came[1] + came[2]))[:CHUNK]
+        both = ((piece(mine, 0).astype(F32) + came[0]) + (came[1] + came[2]))[:CHUNK]
+        return both[:, :FR], both[:, FR:].T
 
     def to_owner(v, dim):
         v = v.reshape((1,) * dim + v.shape)
@@ -654,9 +652,8 @@
         grads[0].append(jnp.moveaxis(qkv, 1, 0))
         outs = jnp.concatenate([a[:, 3 * QW :], b[:, 3 * QW : 3 * QW + 2 * HD]], axis=1)
         grads[1].append(outs.T.reshape(5, HD, CHUNK))
-        both = hidden_own[l]
-        grads[2].append(both[:, :FR])
-        grads[3].append(both[:, FR:].T)
+        grads[2].append(hidden_own[l][0])
+        grads[3].append(hidden_own[l][1])
 
     return (
         mixed[None],

time: 478 us -> 480 us (level)
    unnamed x167 -> x199, local copies, waits for them, and re-layouts: 19.1 us -> 17.1 us
  transfers between devices with their start and end apart: 73 -> 73, of which waited for: 43 -> 38; matrix products, arithmetic and copies ran while one was open for 20% -> 20% of each run, Pallas kernels for 19% -> 19%
where the time goes in v6:
time: 480 us; the launch traced here: 471 us
  waiting for transfers between devices  153 us (32%)
  Pallas kernels  95.4 us (20%)
  starting transfers between devices  89.3 us (19%)
  matrix products  55 us (11%)
  local copies, waits for them, and re-layouts  37.3 us (8%)
  other arithmetic  22.2 us (5%)
  between operations  19.2 us (4%)
    ppermute x40, waiting for transfers between devices, swap_x(): return lax.ppermute(v, LINE, line_perm(lambda x, k: (x ^ m, k)))  91.7 us
    ppermute x40, starting transfers between devices, swap_x(): return lax.ppermute(v, LINE, line_perm(lambda x, k: (x ^ m, k)))  59.2 us
    dot_general x12, matrix products, dot(): return lax.dot_general(a, b, (dims, ((), ())), preferred_element_type=F32)  41.3 us
    pallas_call x2, Pallas kernels, attend_backward(): pl.pallas_call(attend_back_body, grid=(LINE_ROWS // Q_ROWS,), in_specs=at...  27 us
    ppermute x17, waiting for transfers between devices, swap_core(): return lax.ppermute(v, LINE, line_perm(lambda x, k: (x, 1 - k)))  25.1 us
    pallas_call x2, Pallas kernels, attend_forward(): pl.pallas_call(attend_body, grid=(LINE_ROWS // Q_ROWS,), in_specs=attend_...  22.9 us
    unnamed x199, local copies, waits for them, and re-layouts  17.1 us
    ppermute x6, waiting for transfers between devices, swap_shard(): return lax.ppermute(v, 'shard', [(i, i ^ m) for i in range(SHARDS)])  12.2 us
  transfers between devices with their start and end apart: 73, of which 38 were waited for; matrix products, arithmetic and copies ran while one was open for 20% of the time, Pallas kernels for 19%

profile of v6, /device:TPU:0, one launch (start us, length us, event | category | flops | bytes accessed | tf_op | source)
XLA Modules:
  0.0 471.3 jit_solution(8288427790439610420)
XLA Ops:
  17.6 7.2 %collective-permute-done.1 = bf16[36,2176]{1,0:T(8,128)(2,1)S(1)} collective-permute-done((bf16[36,2176]{1,0:T(8,128)(2,1)S(1)}, bf16[36,2176]{1,0:T(8,128)(2,1)S(1)}, u32[]{:S(2)}, u32[]{:S(2)}) %collective-permute-start.1) | collective-permute-done | bytes 156704 | tf_op jit(solution)/shard_map/ppermute | solution.py:42
  45.8 8.0 %all-to-all-start = ((bf16[16,72,768]{2,1,0:T(8,128)(2,1)}), bf16[16,72,768]{2,1,0:T(8,128)(2,1)S(1)}, u32[]{:S(2)}, u32[]{:S(2)}) async-start(bf16[16,72,768]{2,1,0:T(8,128)(2,1)} %broadcast_in_dim.35), calls=%async_computation | async-start | bytes 3538944 | tf_op jit(solution)/shard_map/all_to_all | solution.py:54
  58.2 5.0 %collective-permute-done.7 = bf16[128,1152]{1,0:T(8,128)(2,1)S(1)} collective-permute-done((bf16[128,1152]{1,0:T(8,128)(2,1)}, bf16[128,1152]{1,0:T(8,128)(2,1)S(1)}, u32[]{:S(2)}, u32[]{:S(2)}) %collective-permute-start.7) | collective-permute-done | bytes 294944 | tf_op jit(solution)/shard_map/ppermute | solution.py:42
  66.9 10.6 %all-to-all-done = bf16[16,72,768]{2,1,0:T(8,128)(2,1)S(1)} async-done(((bf16[16,72,768]{2,1,0:T(8,128)(2,1)}), bf16[16,72,768]{2,1,0:T(8,128)(2,1)S(1)}, u32[]{:S(2)}, u32[]{:S(2)}) %all-to-all-start) | async-done | bytes 1769504 | tf_op jit(solution)/shard_map/all_to_all | solution.py:54
  86.4 11.5 %attend.2 = (bf16[1024,192]{1,0:T(8,128)(2,1)S(1)}, f32[8,1024]{1,0:T(8,128)S(1)}) custom-call(f32[3]{0:T(128)S(1)} %and_convert_fusion.live_ref, s32[1024,1]{1,0:T(8,128)S(1)} %copy-done.32, s32[1,1024]{1,0:T(1,128)S(1)} %bitcast.137, bf16[1024,576]{1,0:T(8,128)(2,1)S(1)} %project.4.qkv_ref), custom_call_target="tpu_custom_call" | custom-call | flops 3221225472 | bytes 1572864 | tf_op jit(solution)/shard_map/attend/pallas_call | solution.py:203
  110.2 10.9 %collective-permute-done.15 = bf16[128,1152]{1,0:T(8,128)(2,1)S(1)} collective-permute-done((bf16[128,1152]{1,0:T(8,128)(2,1)S(1)}, bf16[128,1152]{1,0:T(8,128)(2,1)S(1)}, u32[]{:S(2)}, u32[]{:S(2)}) %collective-permute-start.15) | collective-permute-done | bytes 294944 | tf_op jit(solution)/shard_map/ppermute | solution.py:42
  127.9 6.1 %all-gather.3.cloned.1.call-done.w_ref = bf16[1152,5120]{1,0:T(8,128)(2,1)} async-done(((bf16[72,5120]{1,0:T(8,128)(2,1)}), bf16[1152,5120]{1,0:T(8,128)(2,1)}) %all-gather.3.cloned.1.call-update) | async-done | bytes 11796496 | tf_op jit(solution)/shard_map/all_gather | solution.py:446
  134.1 5.5 %multiply_convert_fusion.1 = (bf16[256,2176]{1,0:T(8,128)(2,1)S(1)}, f32[256,2176]{1,0:T(8,128)}) fusion(f32[2176]{0:T(1024)S(1)} %get-tuple-element.193, bf16[1152,5120]{1,0:T(8,128)(2,1)} %all-gather.3.cloned.1.call-done.w_ref, bf16[128,1152]{1,0:T(8,128)(2,1)S(1)} %collective-permute-done.16, bf16[128,1152]{1,0:T(8,128)(2,1)S(1)} %add_convert_fusion.2), kind=kOutput, calls=%fused_computation.59 | convolution fusion | flops 1287979008 | bytes 8954368 | tf_op jit(solution)/shard_map/dot_general | solution.py:99
  150.8 12.3 %collective-permute-done.21 = bf16[128,1152]{1,0:T(8,128)(2,1)S(1)} collective-permute-done((bf16[128,1152]{1,0:T(8,128)(2,1)S(1)}, bf16[128,1152]{1,0:T(8,128)(2,1)S(1)}, u32[]{:S(2)}, u32[]{:S(2)}) %collective-permute-start.21) | collective-permute-done | bytes 294944 | tf_op jit(solution)/shard_map/ppermute | solution.py:42
  171.1 11.5 %attend.3 = (bf16[1024,192]{1,0:T(8,128)(2,1)S(1)}, f32[8,1024]{1,0:T(8,128)S(1)}) custom-call(f32[3]{0:T(128)S(1)} %and_convert_fusion.live_ref, s32[1024,1]{1,0:T(8,128)S(1)} %copy-done.33, s32[1,1024]{1,0:T(1,128)S(1)} %bitcast.138, bf16[1024,576]{1,0:T(8,128)(2,1)S(1)} %project.5.qkv_ref), custom_call_target="tpu_custom_call" | custom-call | flops 3221225472 | bytes 1572864 | tf_op jit(solution)/shard_map/attend/pallas_call | solution.py:203
  196.1 10.5 %collective-permute-done.26 = bf16[128,1152]{1,0:T(8,128)(2,1)S(1)} collective-permute-done((bf16[128,1152]{1,0:T(8,128)(2,1)S(1)}, bf16[128,1152]{1,0:T(8,128)(2,1)S(1)}, u32[]{:S(2)}, u32[]{:S(2)}) %collective-permute-start.26) | collective-permute-done | bytes 294944 | tf_op jit(solution)/shard_map/ppermute | solution.py:42
  222.3 5.9 %hidden_grads.2 = bf16[1152,4352]{1,0:T(8,128)(2,1)} custom-call(bf16[256,1152]{1,0:T(8,128)(2,1)S(1)} %pad_maximum_fusion.4.refs_0_, bf16[256,2176]{1,0:T(8,128)(2,1)S(1)} %get-tuple-element.309.refs_1_, bf16[256,1152]{1,0:T(8,128)(2,1)S(1)} %pad_maximum_fusion.5.refs_2_, bf16[256,2176]{1,0:T(8,128)(2,1)S(1)} %get-tuple-element.306.refs_3_), custom_call_target="tpu_custom_call" | custom-call | flops 2566914048 | bytes 10027008 | tf_op jit(solution)/shard_map/hidden_grads/pallas_call | solution.py:366
  241.3 12.5 %collective-permute-done.33 = bf16[128,1152]{1,0:T(8,128)(2,1)S(1)} collective-permute-done((bf16[128,1152]{1,0:T(8,128)(2,1)S(1)}, bf16[128,1152]{1,0:T(8,128)(2,1)S(1)}, u32[]{:S(2)}, u32[]{:S(2)}) %collective-permute-start.33) | collective-permute-done | bytes 294944 | tf_op jit(solution)/shard_map/ppermute | solution.py:42
  260.4 13.5 %attend_back.2.rows_ref.dqkv_ref = bf16[1024,576]{1,0:T(8,128)(2,1)S(1)} custom-call(f32[3]{0:T(128)S(1)} %and_convert_fusion.live_ref, s32[1024,1]{1,0:T(8,128)S(1)} %copy-done.34, s32[1,1024]{1,0:T(1,128)S(1)} %bitcast.139, f32[8,1024]{1,0:T(8,128)S(1)} %get-tuple-element.78.lse_ref, bf16[1024,192]{1,0:T(8,128)(2,1)S(1)} %project.6.dout_ref, ...), custom_call_target="tpu_custom_call" | custom-call | flops 8053063680 | bytes 2752512 | tf_op jit(solution)/shard_map/attend_back/pallas_call | solution.py:226
  288.1 5.8 %head_grads.2.refs_4_ = bf16[1152,768]{1,0:T(8,128)(2,1)} custom-call(bf16[512,1152]{1,0:T(8,128)(2,1)S(1)} %copy-done.6, bf16[512,1152]{1,0:T(8,128)(2,1)} %collective-permute-done.22.other.x1, bf16[512,1152]{1,0:T(8,128)(2,1)S(1)} %pad_maximum_fusion.1.mine.m0, bf16[512,1152]{1,0:T(8,128)(2,1)S(1)} %collective-permute-done.34.other.m1, ...), custom_call_target="tpu_custom_call" | custom-call | flops 1811939328 | bytes 8388608 | tf_op jit(solution)/shard_map/head_grads/pallas_call | solution.py:326
  293.9 7.2 %collective-permute-done.37 = bf16[128,1152]{1,0:T(8,128)(2,1)S(1)} collective-permute-done((bf16[128,1152]{1,0:T(8,128)(2,1)S(1)}, bf16[128,1152]{1,0:T(8,128)(2,1)S(1)}, u32[]{:S(2)}, u32[]{:S(2)}) %collective-permute-start.37) | collective-permute-done | bytes 294944 | tf_op jit(solution)/shard_map/ppermute | solution.py:42
  311.5 6.1 %hidden_grads.3 = bf16[1152,5120]{1,0:T(8,128)(2,1)} custom-call(bf16[256,1152]{1,0:T(8,128)(2,1)S(1)} %pad_maximum_fusion.3.refs_0_, bf16[256,2176]{1,0:T(8,128)(2,1)S(1)} %get-tuple-element.311.refs_1_, bf16[256,1152]{1,0:T(8,128)(2,1)S(1)} %pad_maximum_fusion.6.refs_2_, bf16[256,2176]{1,0:T(8,128)(2,1)S(1)} %copy-done.23, bf16[1152,768]{1,0:T(8,128)(2,1)S(1)} %copy-done.9), custom_call_target="tpu_custom_call" | custom-call | flops 2566914048 | bytes 11796480 | tf_op jit(solution)/shard_map/hidden_grads/pallas_call | solution.py:366
  329.3 12.8 %collective-permute-done.43 = bf16[128,1152]{1,0:T(8,128)(2,1)S(1)} collective-permute-done((bf16[128,1152]{1,0:T(8,128)(2,1)}, bf16[128,1152]{1,0:T(8,128)(2,1)S(1)}, u32[]{:S(2)}, u32[]{:S(2)}) %collective-permute-start.43) | collective-permute-done | bytes 294944 | tf_op jit(solution)/shard_map/ppermute | solution.py:42
  344.2 4.7 %fusion.8 = f32[256,1152]{1,0:T(8,128)S(1)} fusion(bf16[256,2176]{1,0:T(8,128)(2,1)S(1)} %copy-done.25, bf16[1152,4352]{1,0:T(8,128)(2,1)} %all-gather.5.cloned.1.call-done), kind=kOutput, calls=%fused_computation.9 | convolution fusion | flops 1283457024 | bytes 7307264 | tf_op jit(solution)/shard_map/dot_general | solution.py:99
  363.6 13.5 %attend_back.3.rows_ref.dqkv_ref = bf16[1024,576]{1,0:T(8,128)(2,1)S(1)} custom-call(f32[3]{0:T(128)S(1)} %and_convert_fusion.live_ref, s32[1024,1]{1,0:T(8,128)S(1)} %copy-done.35, s32[1,1024]{1,0:T(1,128)S(1)} %bitcast.140, f32[8,1024]{1,0:T(8,128)S(1)} %get-tuple-element.88.lse_ref, bf16[1024,192]{1,0:T(8,128)(2,1)S(1)} %copy-done.31, ...), custom_call_target="tpu_custom_call" | custom-call | flops 8053063680 | bytes 2752512 | tf_op jit(solution)/shard_map/attend_back/pallas_call | solution.py:226
  391.8 5.8 %head_grads.3 = bf16[1152,768]{1,0:T(8,128)(2,1)} custom-call(bf16[512,1152]{1,0:T(8,128)(2,1)S(1)} %copy-done.11, bf16[512,1152]{1,0:T(8,128)(2,1)} %collective-permute-done.8.other.x1, bf16[512,1152]{1,0:T(8,128)(2,1)S(1)} %copy-done.8, bf16[512,1152]{1,0:T(8,128)(2,1)S(1)} %copy-done.13, bf16[1024,576]{1,0:T(8,128)(2,1)} %copy-done.4, ...), custom_call_target="tpu_custom_call" | custom-call | flops 1811939328 | bytes 8388608 | tf_op jit(solution)/shard_map/head_grads/pallas_call | solution.py:326
  397.6 5.5 %all-to-all-start.1 = ((bf16[16,72,768]{2,1,0:T(8,128)(2,1)}), bf16[16,72,768]{2,1,0:T(8,128)(2,1)S(1)}, u32[]{:S(2)}, u32[]{:S(2)}) async-start(bf16[16,72,768]{2,1,0:T(8,128)(2,1)} %bitcast.142), calls=%async_computation.1 | async-start | bytes 3538944 | tf_op jit(solution)/shard_map/all_to_all | solution.py:59
  421.4 4.7 fusion.47
  426.1 12.1 %collective-permute-done.58 = f32[20,1152]{1,0:T(8,128)S(1)} collective-permute-done((f32[20,1152]{1,0:T(8,128)S(1)}, f32[20,1152]{1,0:T(8,128)S(1)}, u32[]{:S(2)}, u32[]{:S(2)}) %collective-permute-start.58) | collective-permute-done | bytes 92192 | tf_op jit(solution)/shard_map/ppermute | solution.py:50
  (564 shorter events, 242.8 us)
Async XLA Ops:
  7.2 126.8 %all-gather.3.cloned.1.call-start = ((), (), s32[]{:S(2)}) async-start(), calls=%async_computation.4 | async-start | bytes 12533760 | tf_op jit(solution)/shard_map/all_gather | solution.py:446
  45.8 31.7 %all-to-all-start = ((bf16[16,72,768]{2,1,0:T(8,128)(2,1)}), bf16[16,72,768]{2,1,0:T(8,128)(2,1)S(1)}, u32[]{:S(2)}, u32[]{:S(2)}) async-start(bf16[16,72,768]{2,1,0:T(8,128)(2,1)} %broadcast_in_dim.35), calls=%async_computation | async-start | bytes 3538944 | tf_op jit(solution)/shard_map/all_to_all | solution.py:54
  53.9 160.4 %all-gather.5.cloned.1.call-start = ((), (), s32[]{:S(2)}) async-start(), calls=%async_computation.5 | async-start | bytes 10653696 | tf_op jit(solution)/shard_map/all_gather | solution.py:446
  63.2 19.4 %collective-permute-start.8 = (bf16[512,1152]{1,0:T(8,128)(2,1)S(1)}, bf16[512,1152]{1,0:T(8,128)(2,1)}, u32[]{:S(2)}, u32[]{:S(2)}) collective-permute-start(bf16[512,1152]{1,0:T(8,128)(2,1)S(1)} %constant_dynamic-update-slice_fusion.1.mine.x0), channel_id=1, source_target_pairs={{0,1},{1,0},{2,3},{3,2},{4,5},{5,4},{6,7},{7,6},{8,9},{9,8},{10,11... | collective-permute-start | bytes 3538952 | tf_op jit(solution)/shard_map/ppermute | solution.py:38
  77.6 20.3 %collective-permute-start.9 = (bf16[36,2176]{1,0:T(8,128)(2,1)S(1)}, bf16[36,2176]{1,0:T(8,128)(2,1)S(1)}, u32[]{:S(2)}, u32[]{:S(2)}) collective-permute-start(bf16[36,2176]{1,0:T(8,128)(2,1)S(1)} %fusion.101), channel_id=1, source_target_pairs={{0,4},{1,5},{2,6},{3,7},{4,0},{5,1},{6,2},{7,3},{8,12},{9,13},{10,... | collective-permute-start | bytes 470024 | tf_op jit(solution)/shard_map/ppermute | solution.py:42
  78.8 19.4 %collective-permute-start.11 = (bf16[36,2176]{1,0:T(8,128)(2,1)S(1)}, bf16[36,2176]{1,0:T(8,128)(2,1)S(1)}, u32[]{:S(2)}, u32[]{:S(2)}) collective-permute-start(bf16[36,2176]{1,0:T(8,128)(2,1)S(1)} %fusion.101), channel_id=1, source_target_pairs={{0,6},{1,7},{2,4},{3,5},{4,2},{5,3},{6,0},{7,1},{8,14},{9,15},{10,... | collective-permute-start | bytes 470024 | tf_op jit(solution)/shard_map/ppermute | solution.py:42
  81.6 16.6 %collective-permute-start.10 = (bf16[36,2176]{1,0:T(8,128)(2,1)S(1)}, bf16[36,2176]{1,0:T(8,128)(2,1)S(1)}, u32[]{:S(2)}, u32[]{:S(2)}) collective-permute-start(bf16[36,2176]{1,0:T(8,128)(2,1)S(1)} %fusion.101), channel_id=1, source_target_pairs={{0,2},{1,3},{2,0},{3,1},{4,6},{5,7},{6,4},{7,5},{8,10},{9,11},{10,... | collective-permute-start | bytes 470024 | tf_op jit(solution)/shard_map/ppermute | solution.py:42
  99.9 257.2 %reduce-scatter.8.cloned.1.call-start = ((), (), s32[]{:S(2)}) async-start(), calls=%async_computation.6 | async-start | bytes 10653696
  104.5 16.7 %collective-permute-start.15 = (bf16[128,1152]{1,0:T(8,128)(2,1)S(1)}, bf16[128,1152]{1,0:T(8,128)(2,1)S(1)}, u32[]{:S(2)}, u32[]{:S(2)}) collective-permute-start(bf16[128,1152]{1,0:T(8,128)(2,1)S(1)} %get-tuple-element.70), channel_id=1, source_target_pairs={{0,6},{1,7},{2,4},{3,5},{4,2},{5,3},{6,0},{7,1},{8,14},{9,15},{10,... | collective-permute-start | bytes 884744 | tf_op jit(solution)/shard_map/ppermute | solution.py:42
  146.5 16.7 %collective-permute-start.21 = (bf16[128,1152]{1,0:T(8,128)(2,1)S(1)}, bf16[128,1152]{1,0:T(8,128)(2,1)S(1)}, u32[]{:S(2)}, u32[]{:S(2)}) collective-permute-start(bf16[128,1152]{1,0:T(8,128)(2,1)S(1)} %add_convert_fusion.1), channel_id=1, source_target_pairs={{0,6},{1,7},{2,4},{3,5},{4,2},{5,3},{6,0},{7,1},{8,14},{9,15},{10,... | collective-permute-start | bytes 884744 | tf_op jit(solution)/shard_map/ppermute | solution.py:42
  190.0 16.7 %collective-permute-start.26 = (bf16[128,1152]{1,0:T(8,128)(2,1)S(1)}, bf16[128,1152]{1,0:T(8,128)(2,1)S(1)}, u32[]{:S(2)}, u32[]{:S(2)}) collective-permute-start(bf16[128,1152]{1,0:T(8,128)(2,1)S(1)} %get-tuple-element.76), channel_id=1, source_target_pairs={{0,6},{1,7},{2,4},{3,5},{4,2},{5,3},{6,0},{7,1},{8,14},{9,15},{10,... | collective-permute-start | bytes 884744 | tf_op jit(solution)/shard_map/ppermute | solution.py:42
  229.2 209.1 %reduce-scatter.10.cloned.1.call-start = ((), (), s32[]{:S(2)}) async-start(), calls=%async_computation.7 | async-start | bytes 12533760
  237.1 16.7 %collective-permute-start.33 = (bf16[128,1152]{1,0:T(8,128)(2,1)S(1)}, bf16[128,1152]{1,0:T(8,128)(2,1)S(1)}, u32[]{:S(2)}, u32[]{:S(2)}) collective-permute-start(bf16[128,1152]{1,0:T(8,128)(2,1)S(1)} %get-tuple-element.203), channel_id=1, source_target_pairs={{0,6},{1,7},{2,4},{3,5},{4,2},{5,3},{6,0},{7,1},{8,14},{9,15},{10,... | collective-permute-start | bytes 884744 | tf_op jit(solution)/shard_map/ppermute | solution.py:42
  325.2 16.9 %collective-permute-start.43 = (bf16[128,1152]{1,0:T(8,128)(2,1)}, bf16[128,1152]{1,0:T(8,128)(2,1)S(1)}, u32[]{:S(2)}, u32[]{:S(2)}) collective-permute-start(bf16[128,1152]{1,0:T(8,128)(2,1)} %get-tuple-element.209), channel_id=1, source_target_pairs={{0,6},{1,7},{2,4},{3,5},{4,2},{5,3},{6,0},{7,1},{8,14},{9,15},{10,... | collective-permute-start | bytes 884744 | tf_op jit(solution)/shard_map/ppermute | solution.py:42
  326.4 16.5 %collective-permute-start.41 = (bf16[128,1152]{1,0:T(8,128)(2,1)}, bf16[128,1152]{1,0:T(8,128)(2,1)}, u32[]{:S(2)}, u32[]{:S(2)}) collective-permute-start(bf16[128,1152]{1,0:T(8,128)(2,1)} %get-tuple-element.209), channel_id=1, source_target_pairs={{0,4},{1,5},{2,6},{3,7},{4,0},{5,1},{6,2},{7,3},{8,12},{9,13},{10,... | collective-permute-start | bytes 884744 | tf_op jit(solution)/shard_map/ppermute | solution.py:42
  358.7 18.4 %collective-permute-start.47 = (bf16[36,2176]{1,0:T(8,128)(2,1)S(1)}, bf16[36,2176]{1,0:T(8,128)(2,1)S(1)}, u32[]{:S(2)}, u32[]{:S(2)}) collective-permute-start(bf16[36,2176]{1,0:T(8,128)(2,1)S(1)} %pad_maximum_fusion.12), channel_id=1, source_target_pairs={{0,6},{1,7},{2,4},{3,5},{4,2},{5,3},{6,0},{7,1},{8,14},{9,15},{10,... | collective-permute-start | bytes 470024 | tf_op jit(solution)/shard_map/ppermute | solution.py:42
  359.5 17.6 %collective-permute-start.46 = (bf16[36,2176]{1,0:T(8,128)(2,1)S(1)}, bf16[36,2176]{1,0:T(8,128)(2,1)S(1)}, u32[]{:S(2)}, u32[]{:S(2)}) collective-permute-start(bf16[36,2176]{1,0:T(8,128)(2,1)S(1)} %pad_maximum_fusion.11), channel_id=1, source_target_pairs={{0,2},{1,3},{2,0},{3,1},{4,6},{5,7},{6,4},{7,5},{8,10},{9,11},{10,... | collective-permute-start | bytes 470024 | tf_op jit(solution)/shard_map/ppermute | solution.py:42
  360.7 16.4 %collective-permute-start.45 = (bf16[36,2176]{1,0:T(8,128)(2,1)S(1)}, bf16[36,2176]{1,0:T(8,128)(2,1)S(1)}, u32[]{:S(2)}, u32[]{:S(2)}) collective-permute-start(bf16[36,2176]{1,0:T(8,128)(2,1)S(1)} %pad_maximum_fusion.10), channel_id=1, source_target_pairs={{0,4},{1,5},{2,6},{3,7},{4,0},{5,1},{6,2},{7,3},{8,12},{9,13},{10,... | collective-permute-start | bytes 470024 | tf_op jit(solution)/shard_map/ppermute | solution.py:42
  387.6 16.8 %collective-permute-start.51 = (bf16[128,1152]{1,0:T(8,128)(2,1)}, bf16[128,1152]{1,0:T(8,128)(2,1)S(1)}, u32[]{:S(2)}, u32[]{:S(2)}) collective-permute-start(bf16[128,1152]{1,0:T(8,128)(2,1)} %get-tuple-element.94), channel_id=1, source_target_pairs={{0,6},{1,7},{2,4},{3,5},{4,2},{5,3},{6,0},{7,1},{8,14},{9,15},{10,... | collective-permute-start | bytes 884744 | tf_op jit(solution)/shard_map/ppermute | solution.py:42
  388.1 16.3 %collective-permute-start.50 = (bf16[128,1152]{1,0:T(8,128)(2,1)}, bf16[128,1152]{1,0:T(8,128)(2,1)}, u32[]{:S(2)}, u32[]{:S(2)}) collective-permute-start(bf16[128,1152]{1,0:T(8,128)(2,1)} %get-tuple-element.93), channel_id=1, source_target_pairs={{0,2},{1,3},{2,0},{3,1},{4,6},{5,7},{6,4},{7,5},{8,10},{9,11},{10,... | collective-permute-start | bytes 884744 | tf_op jit(solution)/shard_map/ppermute | solution.py:42
  397.6 41.0 %all-to-all-start.1 = ((bf16[16,72,768]{2,1,0:T(8,128)(2,1)}), bf16[16,72,768]{2,1,0:T(8,128)(2,1)S(1)}, u32[]{:S(2)}, u32[]{:S(2)}) async-start(bf16[16,72,768]{2,1,0:T(8,128)(2,1)} %bitcast.142), calls=%async_computation.1 | async-start | bytes 3538944 | tf_op jit(solution)/shard_map/all_to_all | solution.py:59
  416.9 21.2 %collective-permute-start.58 = (f32[20,1152]{1,0:T(8,128)S(1)}, f32[20,1152]{1,0:T(8,128)S(1)}, u32[]{:S(2)}, u32[]{:S(2)}) collective-permute-start(f32[20,1152]{1,0:T(8,128)S(1)} %pad_maximum_fusion.22), channel_id=1, source_target_pairs={{0,16},{8,24},{16,0},{24,8},{32,48},{40,56},{48,32},{56,40},{64,80... | collective-permute-start | bytes 276488 | tf_op jit(solution)/shard_map/ppermute | solution.py:50
  419.9 18.3 %collective-permute-start.59 = (f32[20,1152]{1,0:T(8,128)S(1)}, f32[20,1152]{1,0:T(8,128)S(1)}, u32[]{:S(2)}, u32[]{:S(2)}) collective-permute-start(f32[20,1152]{1,0:T(8,128)S(1)} %pad_maximum_fusion.22), channel_id=1, source_target_pairs={{0,24},{8,16},{16,8},{24,0},{32,56},{40,48},{48,40},{56,32},{64,88... | collective-permute-start | bytes 276488 | tf_op jit(solution)/shard_map/ppermute | solution.py:50
  421.2 17.1 %collective-permute-start.57 = (f32[20,1152]{1,0:T(8,128)S(1)}, f32[20,1152]{1,0:T(8,128)S(1)}, u32[]{:S(2)}, u32[]{:S(2)}) collective-permute-start(f32[20,1152]{1,0:T(8,128)S(1)} %pad_maximum_fusion.22), channel_id=1, source_target_pairs={{0,8},{8,0},{16,24},{24,16},{32,40},{40,32},{48,56},{56,48},{64,72... | collective-permute-start | bytes 276488 | tf_op jit(solution)/shard_map/ppermute | solution.py:50
  (140 other events, 1218.7 us)
Sparse Core Ops, SparseCore 0:
  26.9 107.0 all-gather.2
  136.2 78.0 all-gather.4
  229.3 92.4 reduce-scatter.7
  325.6 110.4 reduce-scatter.9
